TPU v7x, 256 devices: a whole 4x4x8 slice. The times are simulated.
256 devices in a mesh: grp: 8 (over y, core), blk: 32 (over z, x).
Axes of the slice: x: 4, y: 4, z: 8, core: 2. Of those that a mesh axis runs over, the one named last changes fastest.
Arguments:
- rhs: float32 [12288, 1920], P(('grp', 'blk')), may hold values from -6 to 6
- membership: int32 [12288], P(('grp', 'blk')), may hold values from 0 to 7
- pair_ends: int32 [131072, 2], P(('grp', 'blk')), may hold values from 0 to 63, as said below
- pair_dir: int32 [131072], P(('grp', 'blk')), may hold values from 0 to 2
- pair_reach: float32 [131072], P(('grp', 'blk')), may hold values from 0.05 to 0.25
- pair_count: int32 [256], P(('grp', 'blk')), may hold values from 256 to 512, as said below
- send_idx: int32 [256, 14, 4], P(('grp', 'blk')), may hold values from 0 to 7
- rotation: float32 [3, 15, 128, 128], replicated, may hold values from -0.5 to 0.5
- translation: float32 [15, 128, 128], replicated, may hold values from -0.5 to 0.5
- mie: float32 [1920], replicated, may hold values from 0.2 to 1
Outputs:
- basis: float32 [12288, 1920], P(('grp', 'blk'))
- image: float32 [12288, 1920], P(('grp', 'blk'))
Inputs may be any that keep to these rules, and one draw needn't show every extreme that they name: `pair_ends`: column 0 names a cluster of the pair's own device. Column 1 names either another cluster of the same device (below 8, never equal to column 0) or 8 + k * 4 + slot, the cluster sent in that slot by the neighbour at offset k, and only neighbours that lie on the grid are named. Every row of a neighbour on the grid is named by some pair among the first 256 pair slots of its device. `pair_count`: some device has all 512 pair slots live.
All inputs are finite; a program needn't handle non-finite values.
Results may differ from a plain program's by a relative error of at most 0.000053.
Values sent between devices are 32-bit elements; how exact they have to be, the bound alone decides.
No kernel may reach another device: no remote copies, remote signals or barrier semaphores. Data moves between devices by JAX's collectives and lax.ppermute only.
A program may use at most 128 MiB of HBM per device.

v0:
```python
import functools

import jax
import jax.numpy as jnp
from jax import lax
from jax.experimental import pallas as pl
from jax.experimental.pallas import tpu as pltpu
from jax.sharding import Mesh
from jax.sharding import PartitionSpec as P

F32 = jnp.float32
BF16 = jnp.bfloat16
HI = lax.Precision.HIGHEST
ALL = ("y", "c", "z", "x")
ROW = ("z", "x")
COL = ("y", "c")
K = 8
C = 1920
NB = 15
W = 128
NPEER = 14
CAP = 4
EXTRA = 256
VMEM_LIMIT = 24 * 1024 * 1024

NN = (((1,), (0,)), ((), ()))
NT = (((1,), (1,)), ((), ()))
TN = (((0,), (0,)), ((), ()))


def dot(a, b, dims=NN):
    return lax.dot_general(a, b, dims, precision=HI, preferred_element_type=F32)


def halves(x):
    high = x.astype(BF16)
    return high, (x - high.astype(F32)).astype(BF16)


def dot3(a, b, dims=NN):
    rows = a.shape[0]
    a_high32 = a.astype(BF16).astype(F32)
    both = jnp.concatenate([a_high32, a - a_high32], axis=0).astype(BF16)
    b_high, b_low = halves(b)
    first = lax.dot_general(both, b_high, dims, preferred_element_type=F32)
    second = lax.dot_general(a.astype(BF16), b_low, dims, preferred_element_type=F32)
    return first[:rows] + first[rows:] + second


def lanes(shape):
    return lax.broadcasted_iota(jnp.int32, shape, 1)


def sublanes(shape):
    return lax.broadcasted_iota(jnp.int32, shape, 0)


def gather_kernel(count_ref, rhs_ref, member_ref, ends_ref, dir_ref, reach_ref, send_ref, out_ref, square_ref, pad_ref):
    spheres = rhs_ref.shape[0]
    pairs = dir_ref.shape[1]
    rhs = rhs_ref[...]
    member = (sublanes((K, spheres)) == member_ref[...]).astype(F32)
    out_ref[:, :C] = dot(member, rhs)
    squares = jnp.sum(rhs * rhs, axis=0, keepdims=True)
    partial = squares[:, :W]
    for g in range(1, NB):
        partial = partial + squares[:, g * W : (g + 1) * W]
    square_ref[...] = partial
    weight = jnp.where(lanes((1, pairs)) < count_ref[0], reach_ref[...], 0.0)
    own = ends_ref[0:1, :]
    near = ends_ref[1:2, :]
    far = near - K
    place = jnp.where(near < K, near, K + NPEER * (far & (CAP - 1)) + (far >> 2))
    rows = sublanes((W, pairs)) & 63
    near_hot = (rows == place).astype(F32)
    own_weight = jnp.where(sublanes((K, pairs)) == own, weight, 0.0)
    lane = lanes((K, W))
    blocks = [dot(jnp.where(dir_ref[...] == d, own_weight, 0.0), near_hot, NT) for d in range(3)]
    pad_ref[...] = jnp.zeros_like(pad_ref)
    pad_ref[0:CAP, 0:NPEER] = send_ref[...].astype(F32)
    names = jnp.where(lane < 64 + K, (lane - 64).astype(F32), 0.0)
    for slot in range(CAP):
        row = jnp.broadcast_to(pad_ref[slot : slot + 1, :], (K, W))
        names = names + pltpu.roll(row, 64 + K + NPEER * slot, 1)
    out_ref[:, C : C + W] = jnp.where(lane < 64, blocks[0], blocks[1])
    out_ref[:, C + W :] = jnp.where(lane < 64, blocks[2], names)


def pair_matrix(units):
    x = lax.axis_index("x")
    c = lax.axis_index("c")
    core = 1 - 2 * c
    one = 1 - 2 * (x & 1)
    two = jnp.where(x < 2, 2, -2)
    lane = lanes((K, W))
    low = lane < 64
    half = lane & 63
    seen = half - K
    peer = seen - NPEER * (
        (seen >= NPEER).astype(jnp.int32)
        + (seen >= 2 * NPEER).astype(jnp.int32)
        + (seen >= 3 * NPEER).astype(jnp.int32)
    )
    peer = jnp.where(half < K, -1, peer)
    names_of = sublanes((K, W)).astype(F32)
    hot, first, second = [], [], []
    for group, d_row in enumerate((0, core, -core)):
        for place, d_col in enumerate((0, one, -one, two, -two)):
            v0, v1 = units[group * 5 + place]
            names = jnp.where(low, pltpu.roll(v1, 64, 1), v1)
            if group == 0 and place == 0:
                here = peer == -1
                there = here
                own_hot = jnp.where(names == names_of, 1.0, 0.0)
            else:
                f = (1 - d_row) * 5 + 2 - d_col
                b = 14 - f
                here = peer == f - (f > 7).astype(jnp.int32)
                there = peer == b - (b > 7).astype(jnp.int32)
            hot.append(jnp.where((names == names_of) & here, 1.0, 0.0))
            first.append(jnp.where(there, v0, 0.0))
            second.append(jnp.where(there & low, v1, 0.0))
    hot = jnp.concatenate(hot, axis=0)
    first = jnp.concatenate(first, axis=0)
    second = jnp.concatenate(second, axis=0)
    v0, v1 = units[0]

    def two_classes(v):
        return jnp.concatenate([jnp.where(low, v, 0.0), jnp.where(low, 0.0, v)], axis=0)

    return jnp.concatenate(
        [
            dot(two_classes(v0), hot, NT),
            dot(jnp.where(low, v1, 0.0), hot, NT),
            dot(two_classes(own_hot), first, NT),
            dot(jnp.where(low, own_hot, 0.0), second, NT),
        ],
        axis=0,
    )


def field_of(matrix, rows, rotation_ref, translation_ref, y_ref, z_ref):
    ends = dot3(matrix, rows)
    low = lanes((3 * K, W)) < 64
    for g in range(NB):
        at = slice(g * W, (g + 1) * W)
        for d in range(3):
            pair = jnp.concatenate([ends[d * K : d * K + K, at], ends[24 + d * K : 24 + d * K + K, at]], axis=0)
            turned = pltpu.roll(dot3(pair, rotation_ref[d, g]), 64, 1)
            y_ref[d * K : d * K + K, at] = turned[:K]
            y_ref[24 + d * K : 24 + d * K + K, at] = turned[K:]
    for g in range(NB):
        at = slice(g * W, (g + 1) * W)
        b = (g - 1) % NB
        before = slice(b * W, (b + 1) * W)
        front = jnp.where(low, y_ref[:24, before], y_ref[:24, at])
        behind = jnp.where(low, y_ref[24:, before], y_ref[24:, at])
        moved = dot3(front, translation_ref[g]) + dot3(behind, translation_ref[g], NT)
        z_ref[:, at] = pltpu.roll(moved, 64, 1)
    out = []
    for g in range(NB):
        at = slice(g * W, (g + 1) * W)
        a = (g + 1) % NB
        z = jnp.where(low, z_ref[:, at], z_ref[:, a * W : (a + 1) * W])
        out.append(sum(dot3(z[d * K : d * K + K], rotation_ref[d, g], NT) for d in range(3)))
    return out


def first_kernel(
    own_ref, core_ref, side_ref, member_ref, square_ref, rotation_ref, translation_ref, mie_ref,
    matrix_ref, field_ref, next_ref, sums_ref, y_ref, z_ref,
):
    refs = [r.at[i] for r in (own_ref, core_ref, side_ref) for i in range(5)]
    matrix = pair_matrix([(r[:, C : C + W], r[:, C + W : C + 2 * W]) for r in refs])
    matrix_ref[...] = matrix
    rows = jnp.concatenate([r[:, :C] for r in refs], axis=0)
    field = field_of(matrix, rows, rotation_ref, translation_ref, y_ref, z_ref)
    spheres = member_ref.shape[1]
    member = (sublanes((K, spheres)) == member_ref[...]).astype(F32)
    count = jnp.sum(member, axis=1, keepdims=True)
    inner = jnp.zeros((K, W), F32)
    square = jnp.zeros((K, W), F32)
    for g in range(NB):
        at = slice(g * W, (g + 1) * W)
        scaled = field[g] * mie_ref[:, at]
        total = scaled * count
        field_ref[:, at] = scaled
        next_ref[:, at] = total
        inner = inner + scaled * own_ref[0, :, at]
        square = square + scaled * total
    sums_ref[...] = jnp.zeros_like(sums_ref)
    sums_ref[0:1, :] = square_ref[...]
    sums_ref[1:2, :] = jnp.sum(inner, axis=0, keepdims=True)
    sums_ref[2:3, :] = jnp.sum(square, axis=0, keepdims=True)


def second_kernel(
    own_ref, core_ref, side_ref, matrix_ref, rotation_ref, translation_ref, mie_ref, field_ref, y_ref, z_ref
):
    rows = jnp.concatenate([r[i] for r in (own_ref, core_ref, side_ref) for i in range(5)], axis=0)
    field = field_of(matrix_ref[...], rows, rotation_ref, translation_ref, y_ref, z_ref)
    for g in range(NB):
        at = slice(g * W, (g + 1) * W)
        field_ref[:, at] = field[g] * mie_ref[:, at]


def last_kernel(entries, rhs_ref, member_ref, first_ref, second_ref, sums_ref, basis_ref, image_ref):
    sums = jnp.sum(sums_ref[...], axis=1, keepdims=True) / entries
    s, t, u = sums[0:1], sums[1:2], sums[2:3]
    scale2 = s + 1e-06
    rest = (1e-06 + t) / scale2
    norm = jnp.sqrt((rest * rest * s - 2.0 * rest * t + u) / scale2 + 1e-06)
    factor = 1.0 / (norm * jnp.sqrt(scale2))
    spheres = rhs_ref.shape[0]
    member = (sublanes((K, spheres)) == member_ref[...]).astype(F32)
    first = first_ref[...] * factor
    change = rest * first - second_ref[...] * factor
    basis = (rest * factor) * rhs_ref[...] - dot(member, first, TN)
    basis_ref[...] = basis
    image_ref[...] = basis - dot(member, change, TN)


def call(kernel, out_shape, scratch=(), smem=0, inputs=0):
    space = [pl.BlockSpec(memory_space=pltpu.SMEM)] * smem + [pl.BlockSpec(memory_space=pltpu.VMEM)] * (inputs - smem)
    return pl.pallas_call(
        kernel,
        out_shape=out_shape,
        in_specs=space,
        scratch_shapes=list(scratch),
        compiler_params=pltpu.CompilerParams(vmem_limit_bytes=VMEM_LIMIT),
    )


def like(*shape):
    return jax.ShapeDtypeStruct(shape, F32)


def swap(v, axis, mask):
    return lax.ppermute(v, axis, [(i, i ^ mask) for i in range(lax.axis_size(axis))])


def spread(v):
    length = lax.axis_size("z")
    x = lax.axis_index("x")
    near = swap(v, "x", 1)
    pair = jnp.stack([v, near])
    far = swap(pair, "x", 3)
    hops = [(z * 4 + i, (z + 1) * 4 + i) for z in range(length - 1) for i in (0, 1)]
    hops += [(z * 4 + i, (z - 1) * 4 + i) for z in range(1, length) for i in (2, 3)]
    deep = lax.ppermute(far, ROW, hops)
    edge = (x == 0) | (x == 3)
    line = jnp.stack([v, near, jnp.where(edge, deep[0], far[0]), far[1], deep[1]])
    other = swap(line, "c", 1)
    last = lax.axis_size("y") * 2 - 1
    steps = [(i, i + 1) for i in range(1, last, 2)] + [(i + 1, i) for i in range(1, last, 2)]
    side = lax.ppermute(line, COL, steps)
    return line, other, side


def total(v):
    for axis, masks in (("x", (1, 3)), ("c", (1,)), ("y", (1, 3)), ("z", (1, 2, 4))):
        for mask in masks:
            v = v + swap(v, axis, mask)
    return v


def body(rhs, membership, pair_ends, pair_dir, pair_reach, pair_count, send_idx, rotation, translation, mie):
    spheres = rhs.shape[0]
    pairs = pair_dir.shape[0]
    member = membership.reshape(1, spheres)
    mie = mie.reshape(1, C)
    packed, squares = call(
        gather_kernel, (like(K, C + EXTRA), like(1, W)), [pltpu.VMEM((K, W), F32)], smem=1, inputs=7
    )(
        pair_count,
        rhs,
        member,
        pair_ends.T,
        pair_dir.reshape(1, pairs),
        pair_reach.reshape(1, pairs),
        jnp.transpose(send_idx, (0, 2, 1)).reshape(CAP, NPEER),
    )
    work = [pltpu.VMEM((6 * K, C), F32), pltpu.VMEM((3 * K, C), F32)]
    matrix, first, following, sums = call(
        first_kernel, (like(6 * K, 15 * K), like(K, C), like(K, C), like(K, W)), work, inputs=8
    )(*spread(packed), member, squares, rotation, translation, mie)
    second = call(second_kernel, like(K, C), work, inputs=7)(*spread(following), matrix, rotation, translation, mie)
    sums = total(sums)
    entries = float(lax.axis_size(ALL) * spheres * C)
    return tuple(
        call(functools.partial(last_kernel, entries), (like(spheres, C), like(spheres, C)), inputs=5)(
            rhs, member, first, second, sums
        )
    )


def solution(mesh):
    torus = Mesh(mesh.devices.reshape(4, 2, 8, 4), ALL)
    return jax.shard_map(
        body,
        mesh=torus,
        in_specs=(
            P(ALL, None),
            P(ALL),
            P(ALL, None),
            P(ALL),
            P(ALL),
            P(ALL),
            P(ALL, None, None),
            P(),
            P(),
            P(),
        ),
        out_specs=(P(ALL, None), P(ALL, None)),
        check_vma=False,
    )
```

profile of v0, /device:TPU:8, one launch (start us, length us, event | category | flops | bytes accessed | tf_op | source)
XLA Modules:
  0.0 103.2 jit_solution(13802093337751060599)
XLA Ops:
  1.3 0.0 copy-start.4
  1.3 1.0 copy-done.4
  2.3 0.0 copy-start.6
  2.3 0.7 copy-done.6
  2.9 0.0 copy-start.9
  2.9 0.7 copy-done.9
  3.6 0.0 copy-start.10
  3.6 0.7 copy-done.10
  4.3 0.0 copy-start.11
  4.3 0.7 copy-done.11
  5.0 0.0 copy-start.12
  5.0 0.7 copy-done.12
  5.7 0.9 shard_map.113
  6.6 1.5 %collective-permute-start = (f32[8,2176]{1,0:T(8,128)S(1)}, f32[8,2176]{1,0:T(8,128)S(1)}, u32[]{:S(2)}, u32[]{:S(2)}) collective-permute-start(f32[8,2176]{1,0:T(8,128)S(1)} %get-tuple-element.8), channel_id=1, source_target_pairs={{0,1},{1,0},{2,3},{3,2},{4,5},{5,4},{6,7},{7,6},{8,9},{9,8},{10,11... | collective-permute-start | bytes 208904 | tf_op jit(solution)/shard_map/ppermute | solution.py:239
  8.1 2.8 %collective-permute-done = f32[8,2176]{1,0:T(8,128)S(1)} collective-permute-done((f32[8,2176]{1,0:T(8,128)S(1)}, f32[8,2176]{1,0:T(8,128)S(1)}, u32[]{:S(2)}, u32[]{:S(2)}) %collective-permute-start) | collective-permute-done | bytes 69664 | tf_op jit(solution)/shard_map/ppermute | solution.py:239
  10.9 2.8 %collective-permute-start.1 = (f32[2,8,2176]{2,1,0:T(8,128)S(1)}, f32[2,8,2176]{2,1,0:T(8,128)S(1)}, u32[]{:S(2)}, u32[]{:S(2)}) collective-permute-start(f32[2,8,2176]{2,1,0:T(8,128)S(1)} %pad_maximum_fusion), channel_id=1, source_target_pairs={{0,3},{1,2},{2,1},{3,0},{4,7},{5,6},{6,5},{7,4},{8,11},{9,10},{10,... | collective-permute-start | bytes 417800 | tf_op jit(solution)/shard_map/ppermute | solution.py:239
  13.8 3.5 %collective-permute-done.1 = f32[2,8,2176]{2,1,0:T(8,128)S(1)} collective-permute-done((f32[2,8,2176]{2,1,0:T(8,128)S(1)}, f32[2,8,2176]{2,1,0:T(8,128)S(1)}, u32[]{:S(2)}, u32[]{:S(2)}) %collective-permute-start.1) | collective-permute-done | bytes 139296 | tf_op jit(solution)/shard_map/ppermute | solution.py:239
  17.3 3.8 %collective-permute-start.2 = (f32[2,8,2176]{2,1,0:T(8,128)S(1)}, f32[2,8,2176]{2,1,0:T(8,128)S(1)}, u32[]{:S(2)}, u32[]{:S(2)}) collective-permute-start(f32[2,8,2176]{2,1,0:T(8,128)S(1)} %collective-permute-done.1), channel_id=1, source_target_pairs={{0,4},{1,5},{4,8},{5,9},{8,12},{9,13},{12,16},{13,17},{16,20},{17,... | collective-permute-start | bytes 417800 | tf_op jit(solution)/shard_map/ppermute | solution.py:250
  21.1 2.6 %collective-permute-done.2 = f32[2,8,2176]{2,1,0:T(8,128)S(1)} collective-permute-done((f32[2,8,2176]{2,1,0:T(8,128)S(1)}, f32[2,8,2176]{2,1,0:T(8,128)S(1)}, u32[]{:S(2)}, u32[]{:S(2)}) %collective-permute-start.2) | collective-permute-done | bytes 139296 | tf_op jit(solution)/shard_map/ppermute | solution.py:250
  23.7 1.9 %collective-permute-start.4 = (f32[5,8,2176]{2,1,0:T(8,128)S(1)}, f32[5,8,2176]{2,1,0:T(8,128)S(1)}, u32[]{:S(2)}, u32[]{:S(2)}) collective-permute-start(f32[5,8,2176]{2,1,0:T(8,128)S(1)} %slice_dynamic-update-slice_fusion.own_ref), channel_id=1, source_target_pairs={{32,64},{96,128},{160,192},{64,32},{128,96},{192,160},{33,65},{97,... | collective-permute-start | bytes 1044488 | tf_op jit(solution)/shard_map/ppermute | solution.py:256
  25.6 1.8 %collective-permute-start.3 = (f32[5,8,2176]{2,1,0:T(8,128)S(1)}, f32[5,8,2176]{2,1,0:T(8,128)S(1)}, u32[]{:S(2)}, u32[]{:S(2)}) collective-permute-start(f32[5,8,2176]{2,1,0:T(8,128)S(1)} %slice_dynamic-update-slice_fusion.own_ref), channel_id=1, source_target_pairs={{0,32},{32,0},{1,33},{33,1},{2,34},{34,2},{3,35},{35,3},{4,36},{36... | collective-permute-start | bytes 1044488 | tf_op jit(solution)/shard_map/ppermute | solution.py:239
  27.4 0.7 reshape.23.mie_ref
  28.1 4.2 %collective-permute-done.4.side_ref = f32[5,8,2176]{2,1,0:T(8,128)S(1)} collective-permute-done((f32[5,8,2176]{2,1,0:T(8,128)S(1)}, f32[5,8,2176]{2,1,0:T(8,128)S(1)}, u32[]{:S(2)}, u32[]{:S(2)}) %collective-permute-start.4) | collective-permute-done | bytes 348192 | tf_op jit(solution)/shard_map/ppermute | solution.py:256
  32.3 0.0 collective-permute-done.3.core_ref
  32.3 0.0 copy-start
  32.3 1.8 %copy-done = f32[3,15,128,128]{3,2,1,0:T(8,128)S(1)} copy-done((f32[3,15,128,128]{3,2,1,0:T(8,128)S(1)}, f32[3,15,128,128]{3,2,1,0:T(8,128)}, u32[]{:S(2)}) %copy-start) | copy-done | bytes 2949144
  34.2 0.0 copy-start.2
  34.2 1.2 %copy-done.2 = f32[15,128,128]{2,1,0:T(8,128)S(1)} copy-done((f32[15,128,128]{2,1,0:T(8,128)S(1)}, f32[15,128,128]{2,1,0:T(8,128)}, u32[]{:S(2)}) %copy-start.2) | copy-done | bytes 983064
  35.4 0.0 copy-start.7
  35.4 0.7 copy-done.7
  36.0 0.0 copy-start.1
  36.0 4.2 %shard_map.114 = (f32[48,120]{1,0:T(8,128)S(1)}, f32[8,1920]{1,0:T(8,128)S(1)}, f32[8,1920]{1,0:T(8,128)S(1)}, f32[8,128]{1,0:T(8,128)S(1)}) custom-call(f32[5,8,2176]{2,1,0:T(8,128)S(1)} %slice_dynamic-update-slice_fusion.own_ref, f32[5,8,2176]{2,1,0:T(8,128)S(1)} %collective-permute-done.3.core_ref, f32[5,8,2176]{2,1,0:T(8,128)S(1)} %collective-permute-done.4.side_ref, ...), custom_call_target="tpu_custom_call" | custom-call | tf_op jit(solution)/shard_map/pallas_call | solution.py:284
  40.2 0.4 collective-permute-start.5
  40.6 3.9 %collective-permute-done.5 = f32[8,1920]{1,0:T(8,128)S(1)} collective-permute-done((f32[8,1920]{1,0:T(8,128)S(1)}, f32[8,1920]{1,0:T(8,128)S(1)}, u32[]{:S(2)}, u32[]{:S(2)}) %collective-permute-start.5) | collective-permute-done | bytes 61472 | tf_op jit(solution)/shard_map/ppermute | solution.py:239
  44.6 3.4 %collective-permute-start.6 = (f32[2,8,1920]{2,1,0:T(8,128)S(1)}, f32[2,8,1920]{2,1,0:T(8,128)S(1)}, u32[]{:S(2)}, u32[]{:S(2)}) collective-permute-start(f32[2,8,1920]{2,1,0:T(8,128)S(1)} %pad_maximum_fusion.1), channel_id=1, source_target_pairs={{0,3},{1,2},{2,1},{3,0},{4,7},{5,6},{6,5},{7,4},{8,11},{9,10},{10,... | collective-permute-start | bytes 368648 | tf_op jit(solution)/shard_map/ppermute | solution.py:239
  47.9 2.9 %collective-permute-done.6 = f32[2,8,1920]{2,1,0:T(8,128)S(1)} collective-permute-done((f32[2,8,1920]{2,1,0:T(8,128)S(1)}, f32[2,8,1920]{2,1,0:T(8,128)S(1)}, u32[]{:S(2)}, u32[]{:S(2)}) %collective-permute-start.6) | collective-permute-done | bytes 122912 | tf_op jit(solution)/shard_map/ppermute | solution.py:239
  50.8 4.3 %collective-permute-start.7 = (f32[2,8,1920]{2,1,0:T(8,128)S(1)}, f32[2,8,1920]{2,1,0:T(8,128)S(1)}, u32[]{:S(2)}, u32[]{:S(2)}) collective-permute-start(f32[2,8,1920]{2,1,0:T(8,128)S(1)} %collective-permute-done.6), channel_id=1, source_target_pairs={{0,4},{1,5},{4,8},{5,9},{8,12},{9,13},{12,16},{13,17},{16,20},{17,... | collective-permute-start | bytes 368648 | tf_op jit(solution)/shard_map/ppermute | solution.py:250
  55.1 2.4 %collective-permute-done.7 = f32[2,8,1920]{2,1,0:T(8,128)S(1)} collective-permute-done((f32[2,8,1920]{2,1,0:T(8,128)S(1)}, f32[2,8,1920]{2,1,0:T(8,128)S(1)}, u32[]{:S(2)}, u32[]{:S(2)}) %collective-permute-start.7) | collective-permute-done | bytes 122912 | tf_op jit(solution)/shard_map/ppermute | solution.py:250
  57.5 1.9 %collective-permute-start.9 = (f32[5,8,1920]{2,1,0:T(8,128)S(1)}, f32[5,8,1920]{2,1,0:T(8,128)S(1)}, u32[]{:S(2)}, u32[]{:S(2)}) collective-permute-start(f32[5,8,1920]{2,1,0:T(8,128)S(1)} %slice_dynamic-update-slice_fusion.2.own_ref), channel_id=1, source_target_pairs={{32,64},{96,128},{160,192},{64,32},{128,96},{192,160},{33,65},{97,... | collective-permute-start | bytes 921608 | tf_op jit(solution)/shard_map/ppermute | solution.py:256
  59.5 1.8 %collective-permute-start.8 = (f32[5,8,1920]{2,1,0:T(8,128)S(1)}, f32[5,8,1920]{2,1,0:T(8,128)S(1)}, u32[]{:S(2)}, u32[]{:S(2)}) collective-permute-start(f32[5,8,1920]{2,1,0:T(8,128)S(1)} %slice_dynamic-update-slice_fusion.2.own_ref), channel_id=1, source_target_pairs={{0,32},{32,0},{1,33},{33,1},{2,34},{34,2},{3,35},{35,3},{4,36},{36... | collective-permute-start | bytes 921608 | tf_op jit(solution)/shard_map/ppermute | solution.py:239
  61.2 0.0 collective-permute-start.10
  61.2 3.6 %collective-permute-done.10 = f32[8,128]{1,0:T(8,128)S(1)} collective-permute-done((f32[8,128]{1,0:T(8,128)S(1)}, f32[8,128]{1,0:T(8,128)S(1)}, u32[]{:S(2)}, u32[]{:S(2)}) %collective-permute-start.10) | collective-permute-done | bytes 4128 | tf_op jit(solution)/shard_map/ppermute | solution.py:239
  64.9 3.3 %collective-permute-start.11 = (f32[8,128]{1,0:T(8,128)S(1)}, f32[8,128]{1,0:T(8,128)S(1)}, u32[]{:S(2)}, u32[]{:S(2)}) collective-permute-start(f32[8,128]{1,0:T(8,128)S(1)} %add.24), channel_id=1, source_target_pairs={{0,3},{1,2},{2,1},{3,0},{4,7},{5,6},{6,5},{7,4},{8,11},{9,10},{10,... | collective-permute-start | bytes 12296 | tf_op jit(solution)/shard_map/ppermute | solution.py:239
  68.1 1.6 %collective-permute-done.11 = f32[8,128]{1,0:T(8,128)S(1)} collective-permute-done((f32[8,128]{1,0:T(8,128)S(1)}, f32[8,128]{1,0:T(8,128)S(1)}, u32[]{:S(2)}, u32[]{:S(2)}) %collective-permute-start.11) | collective-permute-done | bytes 4128 | tf_op jit(solution)/shard_map/ppermute | solution.py:239
  69.7 0.0 collective-permute-start.12
  69.7 1.2 %collective-permute-done.12 = f32[8,128]{1,0:T(8,128)S(1)} collective-permute-done((f32[8,128]{1,0:T(8,128)S(1)}, f32[8,128]{1,0:T(8,128)S(1)}, u32[]{:S(2)}, u32[]{:S(2)}) %collective-permute-start.12) | collective-permute-done | bytes 4128 | tf_op jit(solution)/shard_map/ppermute | solution.py:239
  70.9 0.4 collective-permute-start.13
  71.3 3.2 %collective-permute-done.13 = f32[8,128]{1,0:T(8,128)S(1)} collective-permute-done((f32[8,128]{1,0:T(8,128)S(1)}, f32[8,128]{1,0:T(8,128)S(1)}, u32[]{:S(2)}, u32[]{:S(2)}) %collective-permute-start.13) | collective-permute-done | bytes 4128 | tf_op jit(solution)/shard_map/ppermute | solution.py:239
  74.5 1.3 %collective-permute-start.14 = (f32[8,128]{1,0:T(8,128)S(1)}, f32[8,128]{1,0:T(8,128)S(1)}, u32[]{:S(2)}, u32[]{:S(2)}) collective-permute-start(f32[8,128]{1,0:T(8,128)S(1)} %add.27), channel_id=1, source_target_pairs={{0,192},{64,128},{128,64},{192,0},{1,193},{65,129},{129,65},{193,1... | collective-permute-start | bytes 12296 | tf_op jit(solution)/shard_map/ppermute | solution.py:239
  75.8 2.3 %collective-permute-done.14 = f32[8,128]{1,0:T(8,128)S(1)} collective-permute-done((f32[8,128]{1,0:T(8,128)S(1)}, f32[8,128]{1,0:T(8,128)S(1)}, u32[]{:S(2)}, u32[]{:S(2)}) %collective-permute-start.14) | collective-permute-done | bytes 4128 | tf_op jit(solution)/shard_map/ppermute | solution.py:239
  78.1 2.4 %collective-permute-start.15 = (f32[8,128]{1,0:T(8,128)S(1)}, f32[8,128]{1,0:T(8,128)S(1)}, u32[]{:S(2)}, u32[]{:S(2)}) collective-permute-start(f32[8,128]{1,0:T(8,128)S(1)} %add.28), channel_id=1, source_target_pairs={{0,4},{4,0},{8,12},{12,8},{16,20},{20,16},{24,28},{28,24},{1,5},{5... | collective-permute-start | bytes 12296 | tf_op jit(solution)/shard_map/ppermute | solution.py:239
  80.5 1.6 %collective-permute-done.15 = f32[8,128]{1,0:T(8,128)S(1)} collective-permute-done((f32[8,128]{1,0:T(8,128)S(1)}, f32[8,128]{1,0:T(8,128)S(1)}, u32[]{:S(2)}, u32[]{:S(2)}) %collective-permute-start.15) | collective-permute-done | bytes 4128 | tf_op jit(solution)/shard_map/ppermute | solution.py:239
  82.1 5.2 %collective-permute-start.16 = (f32[8,128]{1,0:T(8,128)S(1)}, f32[8,128]{1,0:T(8,128)S(1)}, u32[]{:S(2)}, u32[]{:S(2)}) collective-permute-start(f32[8,128]{1,0:T(8,128)S(1)} %add.29), channel_id=1, source_target_pairs={{0,8},{4,12},{8,0},{12,4},{16,24},{20,28},{24,16},{28,20},{1,9},{5... | collective-permute-start | bytes 12296 | tf_op jit(solution)/shard_map/ppermute | solution.py:239
  87.3 1.6 %collective-permute-done.16 = f32[8,128]{1,0:T(8,128)S(1)} collective-permute-done((f32[8,128]{1,0:T(8,128)S(1)}, f32[8,128]{1,0:T(8,128)S(1)}, u32[]{:S(2)}, u32[]{:S(2)}) %collective-permute-start.16) | collective-permute-done | bytes 4128 | tf_op jit(solution)/shard_map/ppermute | solution.py:239
  88.9 7.4 %collective-permute-start.17 = (f32[8,128]{1,0:T(8,128)S(1)}, f32[8,128]{1,0:T(8,128)S(1)}, u32[]{:S(2)}, u32[]{:S(2)}) collective-permute-start(f32[8,128]{1,0:T(8,128)S(1)} %add.30), channel_id=1, source_target_pairs={{0,16},{4,20},{8,24},{12,28},{16,0},{20,4},{24,8},{28,12},{1,17},{... | collective-permute-start | bytes 12296 | tf_op jit(solution)/shard_map/ppermute | solution.py:239
  96.3 1.6 %collective-permute-done.17 = f32[8,128]{1,0:T(8,128)S(1)} collective-permute-done((f32[8,128]{1,0:T(8,128)S(1)}, f32[8,128]{1,0:T(8,128)S(1)}, u32[]{:S(2)}, u32[]{:S(2)}) %collective-permute-start.17) | collective-permute-done | bytes 4128 | tf_op jit(solution)/shard_map/ppermute | solution.py:239
  97.9 0.0 collective-permute-done.9.side_ref
  97.9 0.0 collective-permute-done.8.core_ref
  97.9 0.0 copy-done.1
  97.9 0.0 copy-done.3
  97.9 3.6 %shard_map.115.second_ref = f32[8,1920]{1,0:T(8,128)S(1)} custom-call(f32[5,8,1920]{2,1,0:T(8,128)S(1)} %slice_dynamic-update-slice_fusion.2.own_ref, f32[5,8,1920]{2,1,0:T(8,128)S(1)} %collective-permute-done.8.core_ref, f32[5,8,1920]{2,1,0:T(8,128)S(1)} %collective-permute-done.9.side_ref, f32[48,120]{1,0:T(8,128)S(1)} %get-tuple-element.12.matrix_ref, ...), custom_call_target="tpu_custom_call" | custom-call | tf_op jit(solution)/shard_map/pallas_call | solution.py:287
  101.6 0.0 copy-done.5
  101.6 0.0 copy-done.8
  101.6 1.6 %shard_map.116 = (f32[48,1920]{1,0:T(8,128)}, f32[48,1920]{1,0:T(8,128)}) custom-call(f32[48,1920]{1,0:T(8,128)S(1)} %copy-done.5, s32[1,48]{1,0:T(1,128)S(1)} %bitcast.19, f32[8,1920]{1,0:T(8,128)S(1)} %get-tuple-element.10.first_ref, f32[8,1920]{1,0:T(8,128)S(1)} %shard_map.115.second_ref, f32[8,128]{1,0:T(8,128)S(1)} %add.31.sums_ref), custom_call_target="tpu_custom_call" | custom-call | tf_op jit(solution)/shard_map/pallas_call | solution.py:291
  (23 shorter events, 0.1 us)
Async XLA Ops:
  1.3 1.0 copy-start.4
  2.3 0.7 copy-start.6
  2.9 0.7 copy-start.9
  3.6 0.7 copy-start.10
  4.3 0.7 copy-start.11
  5.0 0.7 copy-start.12
  6.6 4.3 %collective-permute-start = (f32[8,2176]{1,0:T(8,128)S(1)}, f32[8,2176]{1,0:T(8,128)S(1)}, u32[]{:S(2)}, u32[]{:S(2)}) collective-permute-start(f32[8,2176]{1,0:T(8,128)S(1)} %get-tuple-element.8), channel_id=1, source_target_pairs={{0,1},{1,0},{2,3},{3,2},{4,5},{5,4},{6,7},{7,6},{8,9},{9,8},{10,11... | collective-permute-start | bytes 208904 | tf_op jit(solution)/shard_map/ppermute | solution.py:239
  10.9 6.4 %collective-permute-start.1 = (f32[2,8,2176]{2,1,0:T(8,128)S(1)}, f32[2,8,2176]{2,1,0:T(8,128)S(1)}, u32[]{:S(2)}, u32[]{:S(2)}) collective-permute-start(f32[2,8,2176]{2,1,0:T(8,128)S(1)} %pad_maximum_fusion), channel_id=1, source_target_pairs={{0,3},{1,2},{2,1},{3,0},{4,7},{5,6},{6,5},{7,4},{8,11},{9,10},{10,... | collective-permute-start | bytes 417800 | tf_op jit(solution)/shard_map/ppermute | solution.py:239
  17.3 6.4 %collective-permute-start.2 = (f32[2,8,2176]{2,1,0:T(8,128)S(1)}, f32[2,8,2176]{2,1,0:T(8,128)S(1)}, u32[]{:S(2)}, u32[]{:S(2)}) collective-permute-start(f32[2,8,2176]{2,1,0:T(8,128)S(1)} %collective-permute-done.1), channel_id=1, source_target_pairs={{0,4},{1,5},{4,8},{5,9},{8,12},{9,13},{12,16},{13,17},{16,20},{17,... | collective-permute-start | bytes 417800 | tf_op jit(solution)/shard_map/ppermute | solution.py:250
  23.7 8.6 %collective-permute-start.4 = (f32[5,8,2176]{2,1,0:T(8,128)S(1)}, f32[5,8,2176]{2,1,0:T(8,128)S(1)}, u32[]{:S(2)}, u32[]{:S(2)}) collective-permute-start(f32[5,8,2176]{2,1,0:T(8,128)S(1)} %slice_dynamic-update-slice_fusion.own_ref), channel_id=1, source_target_pairs={{32,64},{96,128},{160,192},{64,32},{128,96},{192,160},{33,65},{97,... | collective-permute-start | bytes 1044488 | tf_op jit(solution)/shard_map/ppermute | solution.py:256
  25.6 6.7 %collective-permute-start.3 = (f32[5,8,2176]{2,1,0:T(8,128)S(1)}, f32[5,8,2176]{2,1,0:T(8,128)S(1)}, u32[]{:S(2)}, u32[]{:S(2)}) collective-permute-start(f32[5,8,2176]{2,1,0:T(8,128)S(1)} %slice_dynamic-update-slice_fusion.own_ref), channel_id=1, source_target_pairs={{0,32},{32,0},{1,33},{33,1},{2,34},{34,2},{3,35},{35,3},{4,36},{36... | collective-permute-start | bytes 1044488 | tf_op jit(solution)/shard_map/ppermute | solution.py:239
  32.3 1.8 %copy-start = (f32[3,15,128,128]{3,2,1,0:T(8,128)S(1)}, f32[3,15,128,128]{3,2,1,0:T(8,128)}, u32[]{:S(2)}) copy-start(f32[3,15,128,128]{3,2,1,0:T(8,128)} %rotation_ref.3) | copy-start | bytes 8847364
  34.2 1.2 %copy-start.2 = (f32[15,128,128]{2,1,0:T(8,128)S(1)}, f32[15,128,128]{2,1,0:T(8,128)}, u32[]{:S(2)}) copy-start(f32[15,128,128]{2,1,0:T(8,128)} %translation_ref.3) | copy-start | bytes 2949124
  35.4 0.7 copy-start.7
  36.0 61.9 %copy-start.1 = (f32[3,15,128,128]{3,2,1,0:T(8,128)S(1)}, f32[3,15,128,128]{3,2,1,0:T(8,128)}, u32[]{:S(2)}) copy-start(f32[3,15,128,128]{3,2,1,0:T(8,128)} %rotation_ref.3) | copy-start | bytes 8847364
  36.0 61.9 %copy-start.3 = (f32[15,128,128]{2,1,0:T(8,128)S(1)}, f32[15,128,128]{2,1,0:T(8,128)}, u32[]{:S(2)}) copy-start(f32[15,128,128]{2,1,0:T(8,128)} %translation_ref.3) | copy-start | bytes 2949124
  40.2 4.3 %collective-permute-start.5 = (f32[8,1920]{1,0:T(8,128)S(1)}, f32[8,1920]{1,0:T(8,128)S(1)}, u32[]{:S(2)}, u32[]{:S(2)}) collective-permute-start(f32[8,1920]{1,0:T(8,128)S(1)} %get-tuple-element.11), channel_id=1, source_target_pairs={{0,1},{1,0},{2,3},{3,2},{4,5},{5,4},{6,7},{7,6},{8,9},{9,8},{10,11... | collective-permute-start | bytes 184328 | tf_op jit(solution)/shard_map/ppermute | solution.py:239
  44.5 57.0 %copy-start.5 = (f32[48,1920]{1,0:T(8,128)S(1)}, f32[48,1920]{1,0:T(8,128)}, u32[]{:S(2)}) copy-start(f32[48,1920]{1,0:T(8,128)} %rhs_ref.3) | copy-start | bytes 1105924
  44.5 57.0 %copy-start.8 = (s32[48]{0:T(128)S(1)}, s32[48]{0:T(128)}, u32[]{:S(2)}) copy-start(s32[48]{0:T(128)} %param.11) | copy-start | bytes 580
  44.6 6.2 %collective-permute-start.6 = (f32[2,8,1920]{2,1,0:T(8,128)S(1)}, f32[2,8,1920]{2,1,0:T(8,128)S(1)}, u32[]{:S(2)}, u32[]{:S(2)}) collective-permute-start(f32[2,8,1920]{2,1,0:T(8,128)S(1)} %pad_maximum_fusion.1), channel_id=1, source_target_pairs={{0,3},{1,2},{2,1},{3,0},{4,7},{5,6},{6,5},{7,4},{8,11},{9,10},{10,... | collective-permute-start | bytes 368648 | tf_op jit(solution)/shard_map/ppermute | solution.py:239
  50.8 6.7 %collective-permute-start.7 = (f32[2,8,1920]{2,1,0:T(8,128)S(1)}, f32[2,8,1920]{2,1,0:T(8,128)S(1)}, u32[]{:S(2)}, u32[]{:S(2)}) collective-permute-start(f32[2,8,1920]{2,1,0:T(8,128)S(1)} %collective-permute-done.6), channel_id=1, source_target_pairs={{0,4},{1,5},{4,8},{5,9},{8,12},{9,13},{12,16},{13,17},{16,20},{17,... | collective-permute-start | bytes 368648 | tf_op jit(solution)/shard_map/ppermute | solution.py:250
  57.5 40.4 %collective-permute-start.9 = (f32[5,8,1920]{2,1,0:T(8,128)S(1)}, f32[5,8,1920]{2,1,0:T(8,128)S(1)}, u32[]{:S(2)}, u32[]{:S(2)}) collective-permute-start(f32[5,8,1920]{2,1,0:T(8,128)S(1)} %slice_dynamic-update-slice_fusion.2.own_ref), channel_id=1, source_target_pairs={{32,64},{96,128},{160,192},{64,32},{128,96},{192,160},{33,65},{97,... | collective-permute-start | bytes 921608 | tf_op jit(solution)/shard_map/ppermute | solution.py:256
  59.5 38.4 %collective-permute-start.8 = (f32[5,8,1920]{2,1,0:T(8,128)S(1)}, f32[5,8,1920]{2,1,0:T(8,128)S(1)}, u32[]{:S(2)}, u32[]{:S(2)}) collective-permute-start(f32[5,8,1920]{2,1,0:T(8,128)S(1)} %slice_dynamic-update-slice_fusion.2.own_ref), channel_id=1, source_target_pairs={{0,32},{32,0},{1,33},{33,1},{2,34},{34,2},{3,35},{35,3},{4,36},{36... | collective-permute-start | bytes 921608 | tf_op jit(solution)/shard_map/ppermute | solution.py:239
  61.2 3.6 %collective-permute-start.10 = (f32[8,128]{1,0:T(8,128)S(1)}, f32[8,128]{1,0:T(8,128)S(1)}, u32[]{:S(2)}, u32[]{:S(2)}) collective-permute-start(f32[8,128]{1,0:T(8,128)S(1)} %get-tuple-element.13), channel_id=1, source_target_pairs={{0,1},{1,0},{2,3},{3,2},{4,5},{5,4},{6,7},{7,6},{8,9},{9,8},{10,11... | collective-permute-start | bytes 12296 | tf_op jit(solution)/shard_map/ppermute | solution.py:239
  64.9 4.9 %collective-permute-start.11 = (f32[8,128]{1,0:T(8,128)S(1)}, f32[8,128]{1,0:T(8,128)S(1)}, u32[]{:S(2)}, u32[]{:S(2)}) collective-permute-start(f32[8,128]{1,0:T(8,128)S(1)} %add.24), channel_id=1, source_target_pairs={{0,3},{1,2},{2,1},{3,0},{4,7},{5,6},{6,5},{7,4},{8,11},{9,10},{10,... | collective-permute-start | bytes 12296 | tf_op jit(solution)/shard_map/ppermute | solution.py:239
  69.7 1.2 %collective-permute-start.12 = (f32[8,128]{1,0:T(8,128)S(1)}, f32[8,128]{1,0:T(8,128)S(1)}, u32[]{:S(2)}, u32[]{:S(2)}) collective-permute-start(f32[8,128]{1,0:T(8,128)S(1)} %add.25), channel_id=1, source_target_pairs={{0,32},{32,0},{1,33},{33,1},{2,34},{34,2},{3,35},{35,3},{4,36},{36... | collective-permute-start | bytes 12296 | tf_op jit(solution)/shard_map/ppermute | solution.py:239
  70.9 3.6 %collective-permute-start.13 = (f32[8,128]{1,0:T(8,128)S(1)}, f32[8,128]{1,0:T(8,128)S(1)}, u32[]{:S(2)}, u32[]{:S(2)}) collective-permute-start(f32[8,128]{1,0:T(8,128)S(1)} %add.26), channel_id=1, source_target_pairs={{0,64},{64,0},{128,192},{192,128},{1,65},{65,1},{129,193},{193,129... | collective-permute-start | bytes 12296 | tf_op jit(solution)/shard_map/ppermute | solution.py:239
  74.5 3.6 %collective-permute-start.14 = (f32[8,128]{1,0:T(8,128)S(1)}, f32[8,128]{1,0:T(8,128)S(1)}, u32[]{:S(2)}, u32[]{:S(2)}) collective-permute-start(f32[8,128]{1,0:T(8,128)S(1)} %add.27), channel_id=1, source_target_pairs={{0,192},{64,128},{128,64},{192,0},{1,193},{65,129},{129,65},{193,1... | collective-permute-start | bytes 12296 | tf_op jit(solution)/shard_map/ppermute | solution.py:239
  78.1 4.0 %collective-permute-start.15 = (f32[8,128]{1,0:T(8,128)S(1)}, f32[8,128]{1,0:T(8,128)S(1)}, u32[]{:S(2)}, u32[]{:S(2)}) collective-permute-start(f32[8,128]{1,0:T(8,128)S(1)} %add.28), channel_id=1, source_target_pairs={{0,4},{4,0},{8,12},{12,8},{16,20},{20,16},{24,28},{28,24},{1,5},{5... | collective-permute-start | bytes 12296 | tf_op jit(solution)/shard_map/ppermute | solution.py:239
  82.1 6.8 %collective-permute-start.16 = (f32[8,128]{1,0:T(8,128)S(1)}, f32[8,128]{1,0:T(8,128)S(1)}, u32[]{:S(2)}, u32[]{:S(2)}) collective-permute-start(f32[8,128]{1,0:T(8,128)S(1)} %add.29), channel_id=1, source_target_pairs={{0,8},{4,12},{8,0},{12,4},{16,24},{20,28},{24,16},{28,20},{1,9},{5... | collective-permute-start | bytes 12296 | tf_op jit(solution)/shard_map/ppermute | solution.py:239
  88.9 9.0 %collective-permute-start.17 = (f32[8,128]{1,0:T(8,128)S(1)}, f32[8,128]{1,0:T(8,128)S(1)}, u32[]{:S(2)}, u32[]{:S(2)}) collective-permute-start(f32[8,128]{1,0:T(8,128)S(1)} %add.30), channel_id=1, source_target_pairs={{0,16},{4,20},{8,24},{12,28},{16,0},{20,4},{24,8},{28,12},{1,17},{... | collective-permute-start | bytes 12296 | tf_op jit(solution)/shard_map/ppermute | solution.py:239
where the time goes:
time: 104 us; the launch traced here: 103 us
  starting transfers between devices  43.6 us (42%)
  waiting for transfers between devices  38.9 us (37%)
  Pallas kernels  10.4 us (10%)
  local copies, waits for them, and re-layouts  8.84 us (8%)
  between operations  1.44 us (1%)
    ppermute x14, starting transfers between devices, swap(): lax.ppermute(v, axis, [(i, i ^ mask) for i in range(lax.axis_size(axis))])  31.7 us
    ppermute x14, waiting for transfers between devices, swap(): lax.ppermute(v, axis, [(i, i ^ mask) for i in range(lax.axis_size(axis))])  29.7 us
    unnamed x32, local copies, waits for them, and re-layouts  8.12 us
    ppermute x2, starting transfers between devices, spread(): deep = lax.ppermute(far, ROW, hops)  8.11 us
    ppermute x2, waiting for transfers between devices, spread(): deep = lax.ppermute(far, ROW, hops)  4.96 us
    ppermute x2, waiting for transfers between devices, spread(): side = lax.ppermute(line, COL, steps)  4.22 us
    pallas_call x1, Pallas kernels, body(): call(first_kernel, (like(6 * K, 15 * K), like(K, C), like(K, C), like(K,...  4.19 us
    ppermute x2, starting transfers between devices, spread(): side = lax.ppermute(line, COL, steps)  3.84 us
  transfers between devices with their start and end apart: 18, of which 15 were waited for; matrix products, arithmetic and copies ran while one was open for 1% of the time, Pallas kernels for 0%

commit v1 on v0

--- a/solution.py
+++ b/solution.py
@@ -55,7 +55,18 @@
     return lax.broadcasted_iota(jnp.int32, shape, 0)
 
 
-def gather_kernel(count_ref, rhs_ref, member_ref, ends_ref, dir_ref, reach_ref, send_ref, out_ref, square_ref, pad_ref):
+def gather_kernel(count_ref, *refs):
+    sources, (out_ref, square_ref, rhs_ref), (pad_ref, member_ref, ends_ref, dir_ref, reach_ref, send_ref, sem) = (
+        refs[:6],
+        refs[6:9],
+        refs[9:],
+    )
+    targets = (rhs_ref, member_ref, ends_ref, dir_ref, reach_ref, send_ref)
+    copies = [pltpu.make_async_copy(a, b, sem.at[i]) for i, (a, b) in enumerate(zip(sources, targets))]
+    for copy in copies:
+        copy.start()
+    for copy in copies:
+        copy.wait()
     spheres = rhs_ref.shape[0]
     pairs = dir_ref.shape[1]
     rhs = rhs_ref[...]
@@ -139,42 +150,77 @@
     )
 
 
-def field_of(matrix, rows, rotation_ref, translation_ref, y_ref, z_ref):
+def stacked(x):
+    high = x.astype(BF16).astype(F32)
+    return jnp.concatenate([high, x - high], axis=0).astype(BF16)
+
+
+def times(x, parts):
+    rows, columns = x.shape[0], parts.shape[1] // 2
+    out = lax.dot_general(stacked(x), parts, NN, preferred_element_type=F32)
+    return out[:rows, :columns] + (out[:rows, columns:] + out[rows:, :columns]) + out[rows:, columns:]
+
+
+def split_kernel(rotation_any, translation_any, turn_ref, move_ref, back_ref, rotation_ref, translation_ref, sem):
+    copies = start_all((rotation_any, translation_any), (rotation_ref, translation_ref), sem)
+
+    def put(ref, g, row, w):
+        ref[g, row : row + W, :] = jnp.concatenate(halves(w), axis=1)
+
+    copies[0].wait()
+    for g in range(NB):
+        for d in range(3):
+            w = rotation_ref[d, g]
+            put(turn_ref, g, d * W, w)
+            put(back_ref, g, d * W, w.T)
+    copies[1].wait()
+    for g in range(NB):
+        w = translation_ref[g]
+        put(move_ref, g, 0, w)
+        put(move_ref, g, W, w.T)
+
+
+def field_of(matrix, rows, turn_ref, move_ref, back_ref):
     ends = dot3(matrix, rows)
     low = lanes((3 * K, W)) < 64
+    turned = []
     for g in range(NB):
         at = slice(g * W, (g + 1) * W)
+        parts = []
         for d in range(3):
             pair = jnp.concatenate([ends[d * K : d * K + K, at], ends[24 + d * K : 24 + d * K + K, at]], axis=0)
-            turned = pltpu.roll(dot3(pair, rotation_ref[d, g]), 64, 1)
-            y_ref[d * K : d * K + K, at] = turned[:K]
-            y_ref[24 + d * K : 24 + d * K + K, at] = turned[K:]
-    for g in range(NB):
-        at = slice(g * W, (g + 1) * W)
-        b = (g - 1) % NB
-        before = slice(b * W, (b + 1) * W)
-        front = jnp.where(low, y_ref[:24, before], y_ref[:24, at])
-        behind = jnp.where(low, y_ref[24:, before], y_ref[24:, at])
-        moved = dot3(front, translation_ref[g]) + dot3(behind, translation_ref[g], NT)
-        z_ref[:, at] = pltpu.roll(moved, 64, 1)
+            parts.append(pltpu.roll(times(pair, turn_ref[g, d * W : (d + 1) * W, :]), 64, 1))
+        front = jnp.concatenate([p[:K] for p in parts], axis=0)
+        behind = jnp.concatenate([p[K:] for p in parts], axis=0)
+        turned.append((front, behind))
+    moved = []
+    for g in range(NB):
+        both = [jnp.where(low, before, here) for before, here in zip(turned[g - 1], turned[g])]
+        moved.append(pltpu.roll(times(jnp.concatenate(both, axis=1), move_ref[g]), 64, 1))
     out = []
     for g in range(NB):
-        at = slice(g * W, (g + 1) * W)
-        a = (g + 1) % NB
-        z = jnp.where(low, z_ref[:, at], z_ref[:, a * W : (a + 1) * W])
-        out.append(sum(dot3(z[d * K : d * K + K], rotation_ref[d, g], NT) for d in range(3)))
+        z = jnp.where(low, moved[g], moved[(g + 1) % NB])
+        flat = jnp.concatenate([z[d * K : d * K + K] for d in range(3)], axis=1)
+        out.append(times(flat, back_ref[g]))
     return out
 
 
+def start_all(sources, targets, sem):
+    copies = [pltpu.make_async_copy(a, b, sem.at[i]) for i, (a, b) in enumerate(zip(sources, targets))]
+    for copy in copies:
+        copy.start()
+    return copies
+
+
 def first_kernel(
-    own_ref, core_ref, side_ref, member_ref, square_ref, rotation_ref, translation_ref, mie_ref,
-    matrix_ref, field_ref, next_ref, sums_ref, y_ref, z_ref,
+    own_ref, core_ref, side_ref, square_ref, turn_ref, move_ref, back_ref, mie_ref, member_ref,
+    matrix_ref, field_ref, next_ref,
 ):
     refs = [r.at[i] for r in (own_ref, core_ref, side_ref) for i in range(5)]
     matrix = pair_matrix([(r[:, C : C + W], r[:, C + W : C + 2 * W]) for r in refs])
     matrix_ref[...] = matrix
     rows = jnp.concatenate([r[:, :C] for r in refs], axis=0)
-    field = field_of(matrix, rows, rotation_ref, translation_ref, y_ref, z_ref)
+    field = field_of(matrix, rows, turn_ref, move_ref, back_ref)
     spheres = member_ref.shape[1]
     member = (sublanes((K, spheres)) == member_ref[...]).astype(F32)
     count = jnp.sum(member, axis=1, keepdims=True)
@@ -182,26 +228,24 @@
     square = jnp.zeros((K, W), F32)
     for g in range(NB):
         at = slice(g * W, (g + 1) * W)
-        scaled = field[g] * mie_ref[:, at]
+        scaled = field[g] * mie_ref[g : g + 1, :]
         total = scaled * count
         field_ref[:, at] = scaled
         next_ref[:, at] = total
         inner = inner + scaled * own_ref[0, :, at]
         square = square + scaled * total
-    sums_ref[...] = jnp.zeros_like(sums_ref)
-    sums_ref[0:1, :] = square_ref[...]
-    sums_ref[1:2, :] = jnp.sum(inner, axis=0, keepdims=True)
-    sums_ref[2:3, :] = jnp.sum(square, axis=0, keepdims=True)
-
-
-def second_kernel(
-    own_ref, core_ref, side_ref, matrix_ref, rotation_ref, translation_ref, mie_ref, field_ref, y_ref, z_ref
-):
+    row = sublanes((K, W))
+    inner = jnp.sum(inner, axis=0, keepdims=True)
+    square = jnp.sum(square, axis=0, keepdims=True)
+    next_ref[:, C:] = jnp.where(row == 0, square_ref[...], jnp.where(row == 1, inner, jnp.where(row == 2, square, 0.0)))
+
+
+def second_kernel(own_ref, core_ref, side_ref, matrix_ref, turn_ref, move_ref, back_ref, mie_ref, field_ref):
     rows = jnp.concatenate([r[i] for r in (own_ref, core_ref, side_ref) for i in range(5)], axis=0)
-    field = field_of(matrix_ref[...], rows, rotation_ref, translation_ref, y_ref, z_ref)
+    field = field_of(matrix_ref[...], rows, turn_ref, move_ref, back_ref)
     for g in range(NB):
         at = slice(g * W, (g + 1) * W)
-        field_ref[:, at] = field[g] * mie_ref[:, at]
+        field_ref[:, at] = field[g] * mie_ref[g : g + 1, :]
 
 
 def last_kernel(entries, rhs_ref, member_ref, first_ref, second_ref, sums_ref, basis_ref, image_ref):
@@ -220,15 +264,23 @@
     image_ref[...] = basis - dot(member, change, TN)
 
 
-def call(kernel, out_shape, scratch=(), smem=0, inputs=0):
-    space = [pl.BlockSpec(memory_space=pltpu.SMEM)] * smem + [pl.BlockSpec(memory_space=pltpu.VMEM)] * (inputs - smem)
-    return pl.pallas_call(
+def call(kernel, out_shape, vmem, anywhere=0, scratch=(), smem=0, work=0):
+    space = [pl.BlockSpec(memory_space=pltpu.SMEM)] * smem + [pl.BlockSpec(memory_space=pltpu.VMEM)] * vmem
+    space += [pl.BlockSpec(memory_space=pltpu.HBM)] * anywhere
+    run = pl.pallas_call(
         kernel,
         out_shape=out_shape,
         in_specs=space,
         scratch_shapes=list(scratch),
         compiler_params=pltpu.CompilerParams(vmem_limit_bytes=VMEM_LIMIT),
-    )
+        cost_estimate=pl.CostEstimate(flops=work, bytes_accessed=0, transcendentals=0) if work else None,
+    )
+
+    def placed(*operands):
+        held = [pltpu.with_memory_space_constraint(v, pltpu.HBM) for v in operands[smem + vmem :]]
+        return run(*operands[: smem + vmem], *held)
+
+    return placed
 
 
 def like(*shape):
@@ -239,38 +291,51 @@
     return lax.ppermute(v, axis, [(i, i ^ mask) for i in range(lax.axis_size(axis))])
 
 
-def spread(v):
+def beside(v):
     length = lax.axis_size("z")
-    x = lax.axis_index("x")
-    near = swap(v, "x", 1)
-    pair = jnp.stack([v, near])
-    far = swap(pair, "x", 3)
-    hops = [(z * 4 + i, (z + 1) * 4 + i) for z in range(length - 1) for i in (0, 1)]
-    hops += [(z * 4 + i, (z - 1) * 4 + i) for z in range(1, length) for i in (2, 3)]
-    deep = lax.ppermute(far, ROW, hops)
-    edge = (x == 0) | (x == 3)
-    line = jnp.stack([v, near, jnp.where(edge, deep[0], far[0]), far[1], deep[1]])
-    other = swap(line, "c", 1)
-    last = lax.axis_size("y") * 2 - 1
-    steps = [(i, i + 1) for i in range(1, last, 2)] + [(i + 1, i) for i in range(1, last, 2)]
-    side = lax.ppermute(line, COL, steps)
-    return line, other, side
-
-
-def total(v):
-    for axis, masks in (("x", (1, 3)), ("c", (1,)), ("y", (1, 3)), ("z", (1, 2, 4))):
-        for mask in masks:
-            v = v + swap(v, axis, mask)
-    return v
+    inside = [(4 * z + 1, 4 * z + 2) for z in range(length)]
+    devices = 4 * length
+    odd = inside + [(4 * z + 3, (4 * z + 4) % devices) for z in range(length)]
+    wide = [(4 * z + i, (4 * z + i + 2) % devices) for z in range(length) for i in (2, 3)]
+    return (
+        swap(v, "x", 1),
+        lax.ppermute(v, ROW, odd + [(b, a) for a, b in odd]),
+        swap(v, "x", 2),
+        lax.ppermute(v, ROW, wide + [(b, a) for a, b in wide]),
+    )
+
+
+def across(line):
+    devices = lax.axis_size(COL)
+    steps = [(i, (i + 1) % devices) for i in range(1, devices, 2)]
+    side = lax.ppermute(line, COL, steps + [(b, a) for a, b in steps])
+    return line, swap(line, "c", 1), side
+
+
+def plus(v, axis, masks):
+    return functools.reduce(jnp.add, [v] + [swap(v, axis, mask) for mask in masks])
 
 
 def body(rhs, membership, pair_ends, pair_dir, pair_reach, pair_count, send_idx, rotation, translation, mie):
     spheres = rhs.shape[0]
     pairs = pair_dir.shape[0]
     member = membership.reshape(1, spheres)
-    mie = mie.reshape(1, C)
-    packed, squares = call(
-        gather_kernel, (like(K, C + EXTRA), like(1, W)), [pltpu.VMEM((K, W), F32)], smem=1, inputs=7
+    mie = mie.reshape(NB, W)
+    whole = [
+        pltpu.VMEM((1, spheres), jnp.int32),
+        pltpu.VMEM((2, pairs), jnp.int32),
+        pltpu.VMEM((1, pairs), jnp.int32),
+        pltpu.VMEM((1, pairs), F32),
+        pltpu.VMEM((CAP, NPEER), jnp.int32),
+        pltpu.SemaphoreType.DMA((6,)),
+    ]
+    packed, squares, kept = call(
+        gather_kernel,
+        (like(K, C + EXTRA), like(1, W), like(spheres, C)),
+        0,
+        6,
+        [pltpu.VMEM((K, W), F32)] + whole,
+        1,
     )(
         pair_count,
         rhs,
@@ -280,16 +345,31 @@
         pair_reach.reshape(1, pairs),
         jnp.transpose(send_idx, (0, 2, 1)).reshape(CAP, NPEER),
     )
-    work = [pltpu.VMEM((6 * K, C), F32), pltpu.VMEM((3 * K, C), F32)]
-    matrix, first, following, sums = call(
-        first_kernel, (like(6 * K, 15 * K), like(K, C), like(K, C), like(K, W)), work, inputs=8
-    )(*spread(packed), member, squares, rotation, translation, mie)
-    second = call(second_kernel, like(K, C), work, inputs=7)(*spread(following), matrix, rotation, translation, mie)
-    sums = total(sums)
+    weights = call(
+        split_kernel,
+        tuple(jax.ShapeDtypeStruct((NB, rows * W, 2 * W), BF16) for rows in (3, 2, 3)),
+        0,
+        2,
+        [pltpu.VMEM(rotation.shape, F32), pltpu.VMEM(translation.shape, F32), pltpu.SemaphoreType.DMA((2,))],
+        work=3 * 10**9,
+    )(rotation, translation)
+    line = jnp.stack((packed,) + beside(packed))
+    matrix, first, following = call(first_kernel, (like(6 * K, 15 * K), like(K, C), like(K, C + W)), 9)(
+        *across(line), squares, *weights, mie, member
+    )
+    near = beside(following)
+    line = jnp.stack([v[:, :C] for v in (following,) + near])
+    own = following[:, C:]
+    sums = own + near[0][:, C:] + near[2][:, C:] + swap(own, "x", 3)
+    around = across(line)
+    sums = plus(sums, "z", (4, 2, 6))
+    second = call(second_kernel, like(K, C), 8, work=5 * 10**9)(*around, matrix, *weights, mie)
+    sums = plus(sums, "y", (2, 1, 3))
+    sums = plus(plus(sums, "c", (1,)), "z", (1,))
     entries = float(lax.axis_size(ALL) * spheres * C)
     return tuple(
-        call(functools.partial(last_kernel, entries), (like(spheres, C), like(spheres, C)), inputs=5)(
-            rhs, member, first, second, sums
+        call(functools.partial(last_kernel, entries), (like(spheres, C), like(spheres, C)), 5)(
+            kept, member, first, second, sums
         )
     )
 

time: 104 us -> 67 us (0.64)
  waiting for transfers between devices: 38.9 us -> 20.8 us
  starting transfers between devices: 43.6 us -> 34.1 us
  local copies, waits for them, and re-layouts: 8.84 us -> 0.08 us
    ppermute x14 -> x15, starting transfers between devices: 31.7 us -> 18.5 us  [swap(): lax.ppermute(v, axis, [(i, i ^ mask) for i in range(lax.axis_size(axis))])]
    ppermute x14 -> x15, waiting for transfers between devices: 29.7 us -> 18.9 us  [swap(): lax.ppermute(v, axis, [(i, i ^ mask) for i in range(lax.axis_size(axis))])]
    unnamed x32 -> x12, local copies, waits for them, and re-layouts: 8.12 us -> 0.06 us
    ppermute x4 -> x6, waiting for transfers between devices: 9.18 us -> 1.99 us  [the longest x2 1.98 us: across(): side = lax.ppermute(line, COL, steps + [(b, a) for a, b in steps])]
    ppermute x4 -> x6, starting transfers between devices: 11.9 us -> 15.7 us  [the longest x2 9.68 us: beside(): lax.ppermute(v, ROW, wide + [(b, a) for a, b in wide])]
    pallas_call x4 -> x5, Pallas kernels: 10.4 us -> 10.4 us  [placed(): return run(*operands[:smem + vmem], *held)]
  transfers between devices with their start and end apart: 18 -> 21, of which waited for: 15 -> 8; matrix products, arithmetic and copies ran while one was open for 1% -> 0% of each run, Pallas kernels for 0% -> 5%
where the time goes in v1:
time: 67 us; the launch traced here: 66.9 us
  starting transfers between devices  34.1 us (51%)
  waiting for transfers between devices  20.8 us (31%)
  Pallas kernels  10.4 us (16%)
  between operations  1.45 us (2%)
    ppermute x15, waiting for transfers between devices, swap(): lax.ppermute(v, axis, [(i, i ^ mask) for i in range(lax.axis_size(axis))])  18.9 us
    ppermute x15, starting transfers between devices, swap(): lax.ppermute(v, axis, [(i, i ^ mask) for i in range(lax.axis_size(axis))])  18.5 us
    pallas_call x5, Pallas kernels, placed(): return run(*operands[:smem + vmem], *held)  10.4 us
    ppermute x2, starting transfers between devices, beside(): lax.ppermute(v, ROW, wide + [(b, a) for a, b in wide])  9.68 us
    ppermute x2, starting transfers between devices, beside(): lax.ppermute(v, ROW, odd + [(b, a) for a, b in odd])  5.79 us
    ppermute x2, waiting for transfers between devices, across(): side = lax.ppermute(line, COL, steps + [(b, a) for a, b in steps])  1.98 us
  transfers between devices with their start and end apart: 21, of which 8 were waited for; matrix products, arithmetic and copies ran while one was open for 0% of the time, Pallas kernels for 5%

profile of v1, /device:TPU:8, one launch (start us, length us, event | category | flops | bytes accessed | tf_op | source)
XLA Modules:
  0.0 66.9 jit_solution(8885162220560620092)
XLA Ops:
  1.3 2.0 %shard_map.113 = (f32[8,2176]{1,0:T(8,128)S(1)}, f32[1,128]{1,0:T(1,128)S(1)}, f32[48,1920]{1,0:T(8,128)S(1)}) custom-call(s32[1]{0:T(128)S(6)} %copy.20.count_ref, f32[48,1920]{1,0:T(8,128)} %refs_0_.1, s32[1,48]{1,0:T(1,128)} %bitcast.38, s32[2,512]{1,0:T(2,128)} %bitcast.41, s32[1,512]{1,0:T(1,128)} %bitcast.42, f32[1,512]{1,0:T(1,128)} %bitcast.43, ...), custom_call_target="tpu_custom_call" | custom-call | tf_op jit(solution)/shard_map/pallas_call | solution.py:281
  3.3 8.4 %collective-permute-start.3 = (f32[8,2176]{1,0:T(8,128)S(1)}, f32[8,2176]{1,0:T(8,128)S(1)}, u32[]{:S(2)}, u32[]{:S(2)}) collective-permute-start(f32[8,2176]{1,0:T(8,128)S(1)} %get-tuple-element.12), channel_id=1, source_target_pairs={{2,4},{3,5},{6,8},{7,9},{10,12},{11,13},{14,16},{15,17},{18,20},{1... | collective-permute-start | bytes 208904 | tf_op jit(solution)/shard_map/ppermute | solution.py:304
  11.7 0.0 collective-permute-start.2
  11.7 3.7 %collective-permute-start.1 = (f32[8,2176]{1,0:T(8,128)S(1)}, f32[8,2176]{1,0:T(8,128)S(1)}, u32[]{:S(2)}, u32[]{:S(2)}) collective-permute-start(f32[8,2176]{1,0:T(8,128)S(1)} %get-tuple-element.12), channel_id=1, source_target_pairs={{1,2},{5,6},{9,10},{13,14},{17,18},{21,22},{25,26},{29,30},{3,4},{... | collective-permute-start | bytes 208904 | tf_op jit(solution)/shard_map/ppermute | solution.py:302
  15.4 0.0 collective-permute-start
  15.4 4.3 %collective-permute-done = f32[8,2176]{1,0:T(8,128)S(1)} collective-permute-done((f32[8,2176]{1,0:T(8,128)S(1)}, f32[8,2176]{1,0:T(8,128)S(1)}, u32[]{:S(2)}, u32[]{:S(2)}) %collective-permute-start) | collective-permute-done | bytes 69664 | tf_op jit(solution)/shard_map/ppermute | solution.py:291
  19.7 0.0 collective-permute-done.1
  19.7 0.0 collective-permute-done.2
  19.8 0.0 collective-permute-done.3
  19.8 0.0 copy-start
  19.8 0.0 copy-start.1
  19.8 0.1 collective-permute-start.5
  19.9 1.7 %collective-permute-start.4 = (f32[5,8,2176]{2,1,0:T(8,128)S(1)}, f32[5,8,2176]{2,1,0:T(8,128)S(1)}, u32[]{:S(2)}, u32[]{:S(2)}) collective-permute-start(f32[5,8,2176]{2,1,0:T(8,128)S(1)} %bitcast_dynamic-update-slice_fusion.own_ref), channel_id=1, source_target_pairs={{0,32},{32,0},{1,33},{33,1},{2,34},{34,2},{3,35},{35,3},{4,36},{36... | collective-permute-start | bytes 1044488 | tf_op jit(solution)/shard_map/ppermute | solution.py:291
  21.6 3.0 %shard_map.114 = (bf16[15,384,256]{2,1,0:T(8,128)(2,1)S(1)}, bf16[15,256,256]{2,1,0:T(8,128)(2,1)S(1)}, bf16[15,384,256]{2,1,0:T(8,128)(2,1)S(1)}) custom-call(f32[3,15,128,128]{3,2,1,0:T(8,128)} %rotation_any.1, f32[15,128,128]{2,1,0:T(8,128)} %translation_any.1), custom_call_target="tpu_custom_call" | custom-call | flops 3000000000 | tf_op jit(solution)/shard_map/pallas_call | solution.py:281
  24.6 2.0 %collective-permute-done.5.side_ref = f32[5,8,2176]{2,1,0:T(8,128)S(1)} collective-permute-done((f32[5,8,2176]{2,1,0:T(8,128)S(1)}, f32[5,8,2176]{2,1,0:T(8,128)S(1)}, u32[]{:S(2)}, u32[]{:S(2)}) %collective-permute-start.5) | collective-permute-done | bytes 348192 | tf_op jit(solution)/shard_map/ppermute | solution.py:311
  26.6 0.0 collective-permute-done.4.core_ref
  26.6 0.0 copy-done
  26.6 0.0 copy-done.1
  26.6 2.1 %shard_map.115 = (f32[48,120]{1,0:T(8,128)S(1)}, f32[8,1920]{1,0:T(8,128)S(1)}, f32[8,2048]{1,0:T(8,128)S(1)}) custom-call(f32[5,8,2176]{2,1,0:T(8,128)S(1)} %bitcast_dynamic-update-slice_fusion.own_ref, f32[5,8,2176]{2,1,0:T(8,128)S(1)} %collective-permute-done.4.core_ref, f32[5,8,2176]{2,1,0:T(8,128)S(1)} %collective-permute-done.5.side_ref, ...), custom_call_target="tpu_custom_call" | custom-call | tf_op jit(solution)/shard_map/pallas_call | solution.py:281
  28.8 1.3 %collective-permute-start.9 = (f32[8,2048]{1,0:T(8,128)S(1)}, f32[8,2048]{1,0:T(8,128)S(1)}, u32[]{:S(2)}, u32[]{:S(2)}) collective-permute-start(f32[8,2048]{1,0:T(8,128)S(1)} %get-tuple-element.18), channel_id=1, source_target_pairs={{2,4},{3,5},{6,8},{7,9},{10,12},{11,13},{14,16},{15,17},{18,20},{1... | collective-permute-start | bytes 196616 | tf_op jit(solution)/shard_map/ppermute | solution.py:304
  30.1 2.8 %collective-permute-start.8 = (f32[8,2048]{1,0:T(8,128)S(1)}, f32[8,2048]{1,0:T(8,128)S(1)}, u32[]{:S(2)}, u32[]{:S(2)}) collective-permute-start(f32[8,2048]{1,0:T(8,128)S(1)} %get-tuple-element.18), channel_id=1, source_target_pairs={{0,2},{1,3},{2,0},{3,1},{4,6},{5,7},{6,4},{7,5},{8,10},{9,11},{10,... | collective-permute-start | bytes 196616 | tf_op jit(solution)/shard_map/ppermute | solution.py:291
  32.8 2.1 %collective-permute-start.7 = (f32[8,2048]{1,0:T(8,128)S(1)}, f32[8,2048]{1,0:T(8,128)S(1)}, u32[]{:S(2)}, u32[]{:S(2)}) collective-permute-start(f32[8,2048]{1,0:T(8,128)S(1)} %get-tuple-element.18), channel_id=1, source_target_pairs={{1,2},{5,6},{9,10},{13,14},{17,18},{21,22},{25,26},{29,30},{3,4},{... | collective-permute-start | bytes 196616 | tf_op jit(solution)/shard_map/ppermute | solution.py:302
  34.9 0.0 collective-permute-start.6
  34.9 0.8 %collective-permute-start.12 = (f32[8,128]{1,0:T(8,128)S(1)}, f32[8,128]{1,0:T(8,128)S(1)}, u32[]{:S(2)}, u32[]{:S(2)}) collective-permute-start(f32[8,128]{1,0:T(8,128)S(1)} %slice.29), channel_id=1, source_target_pairs={{0,3},{1,2},{2,1},{3,0},{4,7},{5,6},{6,5},{7,4},{8,11},{9,10},{10,... | collective-permute-start | bytes 12296 | tf_op jit(solution)/shard_map/ppermute | solution.py:291
  35.7 4.1 %collective-permute-done.12 = f32[8,128]{1,0:T(8,128)S(1)} collective-permute-done((f32[8,128]{1,0:T(8,128)S(1)}, f32[8,128]{1,0:T(8,128)S(1)}, u32[]{:S(2)}, u32[]{:S(2)}) %collective-permute-start.12) | collective-permute-done | bytes 4128 | tf_op jit(solution)/shard_map/ppermute | solution.py:291
  39.8 0.0 collective-permute-done.8
  39.8 0.0 collective-permute-done.6
  39.8 1.1 %collective-permute-start.15 = (f32[8,128]{1,0:T(8,128)S(1)}, f32[8,128]{1,0:T(8,128)S(1)}, u32[]{:S(2)}, u32[]{:S(2)}) collective-permute-start(f32[8,128]{1,0:T(8,128)S(1)} %fusion.4), channel_id=1, source_target_pairs={{0,24},{4,28},{8,16},{12,20},{16,8},{20,12},{24,0},{28,4},{1,25},{... | collective-permute-start | bytes 12296 | tf_op jit(solution)/shard_map/ppermute | solution.py:291
  40.9 1.9 %collective-permute-start.14 = (f32[8,128]{1,0:T(8,128)S(1)}, f32[8,128]{1,0:T(8,128)S(1)}, u32[]{:S(2)}, u32[]{:S(2)}) collective-permute-start(f32[8,128]{1,0:T(8,128)S(1)} %fusion.4), channel_id=1, source_target_pairs={{0,8},{4,12},{8,0},{12,4},{16,24},{20,28},{24,16},{28,20},{1,9},{5... | collective-permute-start | bytes 12296 | tf_op jit(solution)/shard_map/ppermute | solution.py:291
  42.8 3.5 %collective-permute-start.13 = (f32[8,128]{1,0:T(8,128)S(1)}, f32[8,128]{1,0:T(8,128)S(1)}, u32[]{:S(2)}, u32[]{:S(2)}) collective-permute-start(f32[8,128]{1,0:T(8,128)S(1)} %fusion.4), channel_id=1, source_target_pairs={{0,16},{4,20},{8,24},{12,28},{16,0},{20,4},{24,8},{28,12},{1,17},{... | collective-permute-start | bytes 12296 | tf_op jit(solution)/shard_map/ppermute | solution.py:291
  46.4 0.0 collective-permute-done.7
  46.4 0.0 collective-permute-done.9
  46.4 0.1 collective-permute-start.11
  46.5 1.7 %collective-permute-start.10 = (f32[5,8,1920]{2,1,0:T(8,128)S(1)}, f32[5,8,1920]{2,1,0:T(8,128)S(1)}, u32[]{:S(2)}, u32[]{:S(2)}) collective-permute-start(f32[5,8,1920]{2,1,0:T(8,128)S(1)} %fusion.own_ref), channel_id=1, source_target_pairs={{0,32},{32,0},{1,33},{33,1},{2,34},{34,2},{3,35},{35,3},{4,36},{36... | collective-permute-start | bytes 921608 | tf_op jit(solution)/shard_map/ppermute | solution.py:291
  48.2 0.0 collective-permute-done.15
  48.2 0.0 collective-permute-done.14
  48.2 2.1 %collective-permute-done.13 = f32[8,128]{1,0:T(8,128)S(1)} collective-permute-done((f32[8,128]{1,0:T(8,128)S(1)}, f32[8,128]{1,0:T(8,128)S(1)}, u32[]{:S(2)}, u32[]{:S(2)}) %collective-permute-start.13) | collective-permute-done | bytes 4128 | tf_op jit(solution)/shard_map/ppermute | solution.py:291
  50.3 1.6 %collective-permute-start.18 = (f32[8,128]{1,0:T(8,128)S(1)}, f32[8,128]{1,0:T(8,128)S(1)}, u32[]{:S(2)}, u32[]{:S(2)}) collective-permute-start(f32[8,128]{1,0:T(8,128)S(1)} %add_add_fusion.1), channel_id=1, source_target_pairs={{0,192},{64,128},{128,64},{192,0},{1,193},{65,129},{129,65},{193,1... | collective-permute-start | bytes 12296 | tf_op jit(solution)/shard_map/ppermute | solution.py:291
  51.9 1.9 %collective-permute-start.17 = (f32[8,128]{1,0:T(8,128)S(1)}, f32[8,128]{1,0:T(8,128)S(1)}, u32[]{:S(2)}, u32[]{:S(2)}) collective-permute-start(f32[8,128]{1,0:T(8,128)S(1)} %add_add_fusion.1), channel_id=1, source_target_pairs={{0,64},{64,0},{128,192},{192,128},{1,65},{65,1},{129,193},{193,129... | collective-permute-start | bytes 12296 | tf_op jit(solution)/shard_map/ppermute | solution.py:291
  53.8 0.3 collective-permute-start.16
  54.1 0.0 collective-permute-done.18
  54.1 1.4 %collective-permute-done.17 = f32[8,128]{1,0:T(8,128)S(1)} collective-permute-done((f32[8,128]{1,0:T(8,128)S(1)}, f32[8,128]{1,0:T(8,128)S(1)}, u32[]{:S(2)}, u32[]{:S(2)}) %collective-permute-start.17) | collective-permute-done | bytes 4128 | tf_op jit(solution)/shard_map/ppermute | solution.py:291
  55.5 3.4 %collective-permute-done.16 = f32[8,128]{1,0:T(8,128)S(1)} collective-permute-done((f32[8,128]{1,0:T(8,128)S(1)}, f32[8,128]{1,0:T(8,128)S(1)}, u32[]{:S(2)}, u32[]{:S(2)}) %collective-permute-start.16) | collective-permute-done | bytes 4128 | tf_op jit(solution)/shard_map/ppermute | solution.py:291
  58.9 0.0 collective-permute-start.19
  58.9 1.2 %collective-permute-done.19 = f32[8,128]{1,0:T(8,128)S(1)} collective-permute-done((f32[8,128]{1,0:T(8,128)S(1)}, f32[8,128]{1,0:T(8,128)S(1)}, u32[]{:S(2)}, u32[]{:S(2)}) %collective-permute-start.19) | collective-permute-done | bytes 4128 | tf_op jit(solution)/shard_map/ppermute | solution.py:291
  60.1 1.3 %collective-permute-start.20 = (f32[8,128]{1,0:T(8,128)S(1)}, f32[8,128]{1,0:T(8,128)S(1)}, u32[]{:S(2)}, u32[]{:S(2)}) collective-permute-start(f32[8,128]{1,0:T(8,128)S(1)} %add.42), channel_id=1, source_target_pairs={{0,4},{4,0},{8,12},{12,8},{16,20},{20,16},{24,28},{28,24},{1,5},{5... | collective-permute-start | bytes 12296 | tf_op jit(solution)/shard_map/ppermute | solution.py:291
  61.4 2.3 %collective-permute-done.20 = f32[8,128]{1,0:T(8,128)S(1)} collective-permute-done((f32[8,128]{1,0:T(8,128)S(1)}, f32[8,128]{1,0:T(8,128)S(1)}, u32[]{:S(2)}, u32[]{:S(2)}) %collective-permute-start.20) | collective-permute-done | bytes 4128 | tf_op jit(solution)/shard_map/ppermute | solution.py:291
  63.7 0.0 collective-permute-done.11.side_ref
  63.7 0.0 collective-permute-done.10.core_ref
  63.7 1.6 %shard_map.116.second_ref = f32[8,1920]{1,0:T(8,128)S(1)} custom-call(f32[5,8,1920]{2,1,0:T(8,128)S(1)} %fusion.own_ref, f32[5,8,1920]{2,1,0:T(8,128)S(1)} %collective-permute-done.10.core_ref, f32[5,8,1920]{2,1,0:T(8,128)S(1)} %collective-permute-done.11.side_ref, f32[48,120]{1,0:T(8,128)S(1)} %get-tuple-element.19.matrix_ref, ...), custom_call_target="tpu_custom_call" | custom-call | flops 5000000000 | tf_op jit(solution)/shard_map/pallas_call | solution.py:281
  65.3 1.6 %shard_map.117 = (f32[48,1920]{1,0:T(8,128)}, f32[48,1920]{1,0:T(8,128)}) custom-call(f32[48,1920]{1,0:T(8,128)S(1)} %get-tuple-element.11.rhs_ref, s32[1,48]{1,0:T(1,128)S(1)} %bitcast.40, f32[8,1920]{1,0:T(8,128)S(1)} %get-tuple-element.17.first_ref, f32[8,1920]{1,0:T(8,128)S(1)} %shard_map.116.second_ref, f32[8,128]{1,0:T(8,128)S(1)} %add.43.sums_ref), custom_call_target="tpu_custom_call" | custom-call | tf_op jit(solution)/shard_map/pallas_call | solution.py:281
  (16 shorter events, 0.1 us)
Async XLA Ops:
  3.3 16.5 %collective-permute-start.3 = (f32[8,2176]{1,0:T(8,128)S(1)}, f32[8,2176]{1,0:T(8,128)S(1)}, u32[]{:S(2)}, u32[]{:S(2)}) collective-permute-start(f32[8,2176]{1,0:T(8,128)S(1)} %get-tuple-element.12), channel_id=1, source_target_pairs={{2,4},{3,5},{6,8},{7,9},{10,12},{11,13},{14,16},{15,17},{18,20},{1... | collective-permute-start | bytes 208904 | tf_op jit(solution)/shard_map/ppermute | solution.py:304
  11.7 8.1 %collective-permute-start.2 = (f32[8,2176]{1,0:T(8,128)S(1)}, f32[8,2176]{1,0:T(8,128)S(1)}, u32[]{:S(2)}, u32[]{:S(2)}) collective-permute-start(f32[8,2176]{1,0:T(8,128)S(1)} %get-tuple-element.12), channel_id=1, source_target_pairs={{0,2},{1,3},{2,0},{3,1},{4,6},{5,7},{6,4},{7,5},{8,10},{9,11},{10,... | collective-permute-start | bytes 208904 | tf_op jit(solution)/shard_map/ppermute | solution.py:291
  11.7 8.0 %collective-permute-start.1 = (f32[8,2176]{1,0:T(8,128)S(1)}, f32[8,2176]{1,0:T(8,128)S(1)}, u32[]{:S(2)}, u32[]{:S(2)}) collective-permute-start(f32[8,2176]{1,0:T(8,128)S(1)} %get-tuple-element.12), channel_id=1, source_target_pairs={{1,2},{5,6},{9,10},{13,14},{17,18},{21,22},{25,26},{29,30},{3,4},{... | collective-permute-start | bytes 208904 | tf_op jit(solution)/shard_map/ppermute | solution.py:302
  15.4 4.3 %collective-permute-start = (f32[8,2176]{1,0:T(8,128)S(1)}, f32[8,2176]{1,0:T(8,128)S(1)}, u32[]{:S(2)}, u32[]{:S(2)}) collective-permute-start(f32[8,2176]{1,0:T(8,128)S(1)} %get-tuple-element.12), channel_id=1, source_target_pairs={{0,1},{1,0},{2,3},{3,2},{4,5},{5,4},{6,7},{7,6},{8,9},{9,8},{10,11... | collective-permute-start | bytes 208904 | tf_op jit(solution)/shard_map/ppermute | solution.py:291
  19.8 6.8 %copy-start = (f32[1920]{0:T(1024)S(1)}, f32[1920]{0:T(1024)}, u32[]{:S(2)}) copy-start(f32[1920]{0:T(1024)} %param.19) | copy-start | bytes 23044
  19.8 6.8 %copy-start.1 = (s32[48]{0:T(128)S(1)}, s32[48]{0:T(128)}, u32[]{:S(2)}) copy-start(s32[48]{0:T(128)} %param.11) | copy-start | bytes 580
  19.8 6.8 %collective-permute-start.5 = (f32[5,8,2176]{2,1,0:T(8,128)S(1)}, f32[5,8,2176]{2,1,0:T(8,128)S(1)}, u32[]{:S(2)}, u32[]{:S(2)}) collective-permute-start(f32[5,8,2176]{2,1,0:T(8,128)S(1)} %bitcast_dynamic-update-slice_fusion.own_ref), channel_id=1, source_target_pairs={{32,64},{96,128},{160,192},{224,0},{64,32},{128,96},{192,160},{0,2... | collective-permute-start | bytes 1044488 | tf_op jit(solution)/shard_map/ppermute | solution.py:311
  19.9 6.7 %collective-permute-start.4 = (f32[5,8,2176]{2,1,0:T(8,128)S(1)}, f32[5,8,2176]{2,1,0:T(8,128)S(1)}, u32[]{:S(2)}, u32[]{:S(2)}) collective-permute-start(f32[5,8,2176]{2,1,0:T(8,128)S(1)} %bitcast_dynamic-update-slice_fusion.own_ref), channel_id=1, source_target_pairs={{0,32},{32,0},{1,33},{33,1},{2,34},{34,2},{3,35},{35,3},{4,36},{36... | collective-permute-start | bytes 1044488 | tf_op jit(solution)/shard_map/ppermute | solution.py:291
  28.8 17.6 %collective-permute-start.9 = (f32[8,2048]{1,0:T(8,128)S(1)}, f32[8,2048]{1,0:T(8,128)S(1)}, u32[]{:S(2)}, u32[]{:S(2)}) collective-permute-start(f32[8,2048]{1,0:T(8,128)S(1)} %get-tuple-element.18), channel_id=1, source_target_pairs={{2,4},{3,5},{6,8},{7,9},{10,12},{11,13},{14,16},{15,17},{18,20},{1... | collective-permute-start | bytes 196616 | tf_op jit(solution)/shard_map/ppermute | solution.py:304
  30.1 9.7 %collective-permute-start.8 = (f32[8,2048]{1,0:T(8,128)S(1)}, f32[8,2048]{1,0:T(8,128)S(1)}, u32[]{:S(2)}, u32[]{:S(2)}) collective-permute-start(f32[8,2048]{1,0:T(8,128)S(1)} %get-tuple-element.18), channel_id=1, source_target_pairs={{0,2},{1,3},{2,0},{3,1},{4,6},{5,7},{6,4},{7,5},{8,10},{9,11},{10,... | collective-permute-start | bytes 196616 | tf_op jit(solution)/shard_map/ppermute | solution.py:291
  32.8 13.5 %collective-permute-start.7 = (f32[8,2048]{1,0:T(8,128)S(1)}, f32[8,2048]{1,0:T(8,128)S(1)}, u32[]{:S(2)}, u32[]{:S(2)}) collective-permute-start(f32[8,2048]{1,0:T(8,128)S(1)} %get-tuple-element.18), channel_id=1, source_target_pairs={{1,2},{5,6},{9,10},{13,14},{17,18},{21,22},{25,26},{29,30},{3,4},{... | collective-permute-start | bytes 196616 | tf_op jit(solution)/shard_map/ppermute | solution.py:302
  34.9 4.8 %collective-permute-start.6 = (f32[8,2048]{1,0:T(8,128)S(1)}, f32[8,2048]{1,0:T(8,128)S(1)}, u32[]{:S(2)}, u32[]{:S(2)}) collective-permute-start(f32[8,2048]{1,0:T(8,128)S(1)} %get-tuple-element.18), channel_id=1, source_target_pairs={{0,1},{1,0},{2,3},{3,2},{4,5},{5,4},{6,7},{7,6},{8,9},{9,8},{10,11... | collective-permute-start | bytes 196616 | tf_op jit(solution)/shard_map/ppermute | solution.py:291
  34.9 4.8 %collective-permute-start.12 = (f32[8,128]{1,0:T(8,128)S(1)}, f32[8,128]{1,0:T(8,128)S(1)}, u32[]{:S(2)}, u32[]{:S(2)}) collective-permute-start(f32[8,128]{1,0:T(8,128)S(1)} %slice.29), channel_id=1, source_target_pairs={{0,3},{1,2},{2,1},{3,0},{4,7},{5,6},{6,5},{7,4},{8,11},{9,10},{10,... | collective-permute-start | bytes 12296 | tf_op jit(solution)/shard_map/ppermute | solution.py:291
  39.8 8.4 %collective-permute-start.15 = (f32[8,128]{1,0:T(8,128)S(1)}, f32[8,128]{1,0:T(8,128)S(1)}, u32[]{:S(2)}, u32[]{:S(2)}) collective-permute-start(f32[8,128]{1,0:T(8,128)S(1)} %fusion.4), channel_id=1, source_target_pairs={{0,24},{4,28},{8,16},{12,20},{16,8},{20,12},{24,0},{28,4},{1,25},{... | collective-permute-start | bytes 12296 | tf_op jit(solution)/shard_map/ppermute | solution.py:291
  40.9 7.3 %collective-permute-start.14 = (f32[8,128]{1,0:T(8,128)S(1)}, f32[8,128]{1,0:T(8,128)S(1)}, u32[]{:S(2)}, u32[]{:S(2)}) collective-permute-start(f32[8,128]{1,0:T(8,128)S(1)} %fusion.4), channel_id=1, source_target_pairs={{0,8},{4,12},{8,0},{12,4},{16,24},{20,28},{24,16},{28,20},{1,9},{5... | collective-permute-start | bytes 12296 | tf_op jit(solution)/shard_map/ppermute | solution.py:291
  42.8 7.5 %collective-permute-start.13 = (f32[8,128]{1,0:T(8,128)S(1)}, f32[8,128]{1,0:T(8,128)S(1)}, u32[]{:S(2)}, u32[]{:S(2)}) collective-permute-start(f32[8,128]{1,0:T(8,128)S(1)} %fusion.4), channel_id=1, source_target_pairs={{0,16},{4,20},{8,24},{12,28},{16,0},{20,4},{24,8},{28,12},{1,17},{... | collective-permute-start | bytes 12296 | tf_op jit(solution)/shard_map/ppermute | solution.py:291
  46.4 17.3 %collective-permute-start.11 = (f32[5,8,1920]{2,1,0:T(8,128)S(1)}, f32[5,8,1920]{2,1,0:T(8,128)S(1)}, u32[]{:S(2)}, u32[]{:S(2)}) collective-permute-start(f32[5,8,1920]{2,1,0:T(8,128)S(1)} %fusion.own_ref), channel_id=1, source_target_pairs={{32,64},{96,128},{160,192},{224,0},{64,32},{128,96},{192,160},{0,2... | collective-permute-start | bytes 921608 | tf_op jit(solution)/shard_map/ppermute | solution.py:311
  46.5 17.2 %collective-permute-start.10 = (f32[5,8,1920]{2,1,0:T(8,128)S(1)}, f32[5,8,1920]{2,1,0:T(8,128)S(1)}, u32[]{:S(2)}, u32[]{:S(2)}) collective-permute-start(f32[5,8,1920]{2,1,0:T(8,128)S(1)} %fusion.own_ref), channel_id=1, source_target_pairs={{0,32},{32,0},{1,33},{33,1},{2,34},{34,2},{3,35},{35,3},{4,36},{36... | collective-permute-start | bytes 921608 | tf_op jit(solution)/shard_map/ppermute | solution.py:291
  50.3 3.7 %collective-permute-start.18 = (f32[8,128]{1,0:T(8,128)S(1)}, f32[8,128]{1,0:T(8,128)S(1)}, u32[]{:S(2)}, u32[]{:S(2)}) collective-permute-start(f32[8,128]{1,0:T(8,128)S(1)} %add_add_fusion.1), channel_id=1, source_target_pairs={{0,192},{64,128},{128,64},{192,0},{1,193},{65,129},{129,65},{193,1... | collective-permute-start | bytes 12296 | tf_op jit(solution)/shard_map/ppermute | solution.py:291
  51.9 3.6 %collective-permute-start.17 = (f32[8,128]{1,0:T(8,128)S(1)}, f32[8,128]{1,0:T(8,128)S(1)}, u32[]{:S(2)}, u32[]{:S(2)}) collective-permute-start(f32[8,128]{1,0:T(8,128)S(1)} %add_add_fusion.1), channel_id=1, source_target_pairs={{0,64},{64,0},{128,192},{192,128},{1,65},{65,1},{129,193},{193,129... | collective-permute-start | bytes 12296 | tf_op jit(solution)/shard_map/ppermute | solution.py:291
  53.8 5.1 %collective-permute-start.16 = (f32[8,128]{1,0:T(8,128)S(1)}, f32[8,128]{1,0:T(8,128)S(1)}, u32[]{:S(2)}, u32[]{:S(2)}) collective-permute-start(f32[8,128]{1,0:T(8,128)S(1)} %add_add_fusion.1), channel_id=1, source_target_pairs={{0,128},{64,192},{128,0},{192,64},{1,129},{65,193},{129,1},{193,65... | collective-permute-start | bytes 12296 | tf_op jit(solution)/shard_map/ppermute | solution.py:291
  58.9 1.2 %collective-permute-start.19 = (f32[8,128]{1,0:T(8,128)S(1)}, f32[8,128]{1,0:T(8,128)S(1)}, u32[]{:S(2)}, u32[]{:S(2)}) collective-permute-start(f32[8,128]{1,0:T(8,128)S(1)} %add_add_fusion), channel_id=1, source_target_pairs={{0,32},{32,0},{1,33},{33,1},{2,34},{34,2},{3,35},{35,3},{4,36},{36... | collective-permute-start | bytes 12296 | tf_op jit(solution)/shard_map/ppermute | solution.py:291
  60.1 3.6 %collective-permute-start.20 = (f32[8,128]{1,0:T(8,128)S(1)}, f32[8,128]{1,0:T(8,128)S(1)}, u32[]{:S(2)}, u32[]{:S(2)}) collective-permute-start(f32[8,128]{1,0:T(8,128)S(1)} %add.42), channel_id=1, source_target_pairs={{0,4},{4,0},{8,12},{12,8},{16,20},{20,16},{24,28},{28,24},{1,5},{5... | collective-permute-start | bytes 12296 | tf_op jit(solution)/shard_map/ppermute | solution.py:291

commit v2 on v1

--- a/solution.py
+++ b/solution.py
@@ -10,7 +10,6 @@
 
 F32 = jnp.float32
 BF16 = jnp.bfloat16
-HI = lax.Precision.HIGHEST
 ALL = ("y", "c", "z", "x")
 ROW = ("z", "x")
 COL = ("y", "c")
@@ -28,10 +27,6 @@
 TN = (((0,), (0,)), ((), ()))
 
 
-def dot(a, b, dims=NN):
-    return lax.dot_general(a, b, dims, precision=HI, preferred_element_type=F32)
-
-
 def halves(x):
     high = x.astype(BF16)
     return high, (x - high.astype(F32)).astype(BF16)
@@ -45,6 +40,35 @@
     first = lax.dot_general(both, b_high, dims, preferred_element_type=F32)
     second = lax.dot_general(a.astype(BF16), b_low, dims, preferred_element_type=F32)
     return first[:rows] + first[rows:] + second
+
+
+def thirds(x):
+    high = x.astype(BF16).astype(F32)
+    rest = x - high
+    middle = rest.astype(BF16).astype(F32)
+    return high, middle, rest - middle
+
+
+def weighted_hot(x, hot):
+    rows = x.shape[0]
+    out = lax.dot_general(
+        jnp.concatenate(thirds(x), axis=0).astype(BF16), hot.astype(BF16), NT, preferred_element_type=F32
+    )
+    return out[:rows] + out[rows : 2 * rows] + out[2 * rows :]
+
+
+def hot_times(hot, x, dims=NN):
+    hot = hot.astype(BF16)
+    return sum(lax.dot_general(hot, part.astype(BF16), dims, preferred_element_type=F32) for part in thirds(x))
+
+
+def rows_of(member, x):
+    return lax.dot_general(
+        jnp.concatenate([member] * 3, axis=0).astype(BF16),
+        jnp.concatenate(thirds(x), axis=0).astype(BF16),
+        TN,
+        preferred_element_type=F32,
+    )
 
 
 def lanes(shape):
@@ -71,7 +95,7 @@
     pairs = dir_ref.shape[1]
     rhs = rhs_ref[...]
     member = (sublanes((K, spheres)) == member_ref[...]).astype(F32)
-    out_ref[:, :C] = dot(member, rhs)
+    out_ref[:, :C] = hot_times(member, rhs)
     squares = jnp.sum(rhs * rhs, axis=0, keepdims=True)
     partial = squares[:, :W]
     for g in range(1, NB):
@@ -86,7 +110,9 @@
     near_hot = (rows == place).astype(F32)
     own_weight = jnp.where(sublanes((K, pairs)) == own, weight, 0.0)
     lane = lanes((K, W))
-    blocks = [dot(jnp.where(dir_ref[...] == d, own_weight, 0.0), near_hot, NT) for d in range(3)]
+    classes = jnp.concatenate([jnp.where(dir_ref[...] == d, own_weight, 0.0) for d in range(3)], axis=0)
+    table = weighted_hot(classes, near_hot)
+    blocks = [table[d * K : d * K + K] for d in range(3)]
     pad_ref[...] = jnp.zeros_like(pad_ref)
     pad_ref[0:CAP, 0:NPEER] = send_ref[...].astype(F32)
     names = jnp.where(lane < 64 + K, (lane - 64).astype(F32), 0.0)
@@ -139,12 +165,12 @@
     def two_classes(v):
         return jnp.concatenate([jnp.where(low, v, 0.0), jnp.where(low, 0.0, v)], axis=0)
 
+    ends = jnp.concatenate([two_classes(v0), jnp.where(low, v1, 0.0)], axis=0)
     return jnp.concatenate(
         [
-            dot(two_classes(v0), hot, NT),
-            dot(jnp.where(low, v1, 0.0), hot, NT),
-            dot(two_classes(own_hot), first, NT),
-            dot(jnp.where(low, own_hot, 0.0), second, NT),
+            weighted_hot(ends, hot),
+            hot_times(two_classes(own_hot), first, NT),
+            hot_times(jnp.where(low, own_hot, 0.0), second, NT),
         ],
         axis=0,
     )
@@ -240,28 +266,32 @@
     next_ref[:, C:] = jnp.where(row == 0, square_ref[...], jnp.where(row == 1, inner, jnp.where(row == 2, square, 0.0)))
 
 
-def second_kernel(own_ref, core_ref, side_ref, matrix_ref, turn_ref, move_ref, back_ref, mie_ref, field_ref):
-    rows = jnp.concatenate([r[i] for r in (own_ref, core_ref, side_ref) for i in range(5)], axis=0)
+def second_kernel(
+    own_ref, core_ref, side_ref, matrix_ref, turn_ref, move_ref, back_ref, mie_ref, member_ref, first_ref,
+    near_ref, next_ref,
+):
+    core = [core_ref[i * K : i * K + K, :] for i in range(5)]
+    rows = jnp.concatenate([own_ref[i] for i in range(5)] + core + [side_ref[i] for i in range(5)], axis=0)
     field = field_of(matrix_ref[...], rows, turn_ref, move_ref, back_ref)
+    spheres = member_ref.shape[1]
+    member = (sublanes((K, spheres)) == member_ref[...]).astype(F32)
     for g in range(NB):
         at = slice(g * W, (g + 1) * W)
-        field_ref[:, at] = field[g] * mie_ref[g : g + 1, :]
-
-
-def last_kernel(entries, rhs_ref, member_ref, first_ref, second_ref, sums_ref, basis_ref, image_ref):
+        near_ref[:, at] = rows_of(member, first_ref[:, at])
+        next_ref[:, at] = rows_of(member, field[g] * mie_ref[g : g + 1, :])
+
+
+def last_kernel(entries, rhs_ref, first_ref, second_ref, sums_ref, basis_ref, image_ref):
     sums = jnp.sum(sums_ref[...], axis=1, keepdims=True) / entries
     s, t, u = sums[0:1], sums[1:2], sums[2:3]
     scale2 = s + 1e-06
     rest = (1e-06 + t) / scale2
     norm = jnp.sqrt((rest * rest * s - 2.0 * rest * t + u) / scale2 + 1e-06)
     factor = 1.0 / (norm * jnp.sqrt(scale2))
-    spheres = rhs_ref.shape[0]
-    member = (sublanes((K, spheres)) == member_ref[...]).astype(F32)
     first = first_ref[...] * factor
-    change = rest * first - second_ref[...] * factor
-    basis = (rest * factor) * rhs_ref[...] - dot(member, first, TN)
+    basis = (rest * factor) * rhs_ref[...] - first
     basis_ref[...] = basis
-    image_ref[...] = basis - dot(member, change, TN)
+    image_ref[...] = basis - (rest * first - second_ref[...] * factor)
 
 
 def call(kernel, out_shape, vmem, anywhere=0, scratch=(), smem=0, work=0):
@@ -305,11 +335,14 @@
     )
 
 
-def across(line):
+def over_side(line):
     devices = lax.axis_size(COL)
     steps = [(i, (i + 1) % devices) for i in range(1, devices, 2)]
-    side = lax.ppermute(line, COL, steps + [(b, a) for a, b in steps])
-    return line, swap(line, "c", 1), side
+    return lax.ppermute(line, COL, steps + [(b, a) for a, b in steps])
+
+
+def after(v, other):
+    return lax.optimization_barrier((v, other))[0]
 
 
 def plus(v, axis, masks):
@@ -355,21 +388,25 @@
     )(rotation, translation)
     line = jnp.stack((packed,) + beside(packed))
     matrix, first, following = call(first_kernel, (like(6 * K, 15 * K), like(K, C), like(K, C + W)), 9)(
-        *across(line), squares, *weights, mie, member
+        line, swap(line, "c", 1), over_side(line), squares, *weights, mie, member
     )
     near = beside(following)
     line = jnp.stack([v[:, :C] for v in (following,) + near])
-    own = following[:, C:]
-    sums = own + near[0][:, C:] + near[2][:, C:] + swap(own, "x", 3)
-    around = across(line)
-    sums = plus(sums, "z", (4, 2, 6))
-    second = call(second_kernel, like(K, C), 8, work=5 * 10**9)(*around, matrix, *weights, mie)
+    sums = after(sum(v[:, C:] for v in near[:3]) + following[:, C:], near[3])
+    carried = jnp.concatenate([line.reshape(5 * K, C), jnp.pad(sums, ((0, 0), (0, C - W)))], axis=0)
+    core = swap(carried, "c", 1)
+    side = over_side(line)
+    sums = sums + core[5 * K :, :W]
+    near, second = call(second_kernel, (like(spheres, C), like(spheres, C)), 10, work=5 * 10**9)(
+        line, core, side, matrix, *weights, mie, member, first
+    )
+    sums = plus(sums, "z", (2, 6, 4))
     sums = plus(sums, "y", (2, 1, 3))
-    sums = plus(plus(sums, "c", (1,)), "z", (1,))
+    sums = plus(after(sums, second), "z", (1,))
     entries = float(lax.axis_size(ALL) * spheres * C)
     return tuple(
-        call(functools.partial(last_kernel, entries), (like(spheres, C), like(spheres, C)), 5)(
-            kept, member, first, second, sums
+        call(functools.partial(last_kernel, entries), (like(spheres, C), like(spheres, C)), 4)(
+            kept, near, second, sums
         )
     )
 

time: 67 us -> 63.2 us (0.943)
  waiting for transfers between devices: 20.8 us -> 18.8 us
  Pallas kernels: 10.4 us -> 9.27 us
  starting transfers between devices: 34.1 us -> 33.4 us
    ppermute x15 -> x13, waiting for transfers between devices: 18.9 us -> 13.6 us  [swap(): lax.ppermute(v, axis, [(i, i ^ mask) for i in range(lax.axis_size(axis))])]
    ppermute x2, waiting for transfers between devices: 0.01 us -> 3.2 us  [beside(): lax.ppermute(v, ROW, odd + [(b, a) for a, b in odd])]
    ppermute x15 -> x13, starting transfers between devices: 18.5 us -> 16.1 us  [swap(): lax.ppermute(v, axis, [(i, i ^ mask) for i in range(lax.axis_size(axis))])]
    ppermute x2, starting transfers between devices: 0.19 us -> 1.85 us  [over_side(): return lax.ppermute(line, COL, steps + [(b, a) for a, b in steps])]
    pallas_call x5, Pallas kernels: 10.4 us -> 9.27 us  [placed(): return run(*operands[:smem + vmem], *held)]
  transfers between devices with their start and end apart: 21 -> 19, of which waited for: 8 -> 8; matrix products, arithmetic and copies ran while one was open for 0% -> 0% of each run, Pallas kernels for 5% -> 8%
where the time goes in v2:
time: 63.2 us; the launch traced here: 63.1 us
  starting transfers between devices  33.4 us (53%)
  waiting for transfers between devices  18.8 us (30%)
  Pallas kernels  9.27 us (15%)
  between operations  1.48 us (2%)
    ppermute x13, starting transfers between devices, swap(): lax.ppermute(v, axis, [(i, i ^ mask) for i in range(lax.axis_size(axis))])  16.1 us
    ppermute x13, waiting for transfers between devices, swap(): lax.ppermute(v, axis, [(i, i ^ mask) for i in range(lax.axis_size(axis))])  13.6 us
    ppermute x2, starting transfers between devices, beside(): lax.ppermute(v, ROW, wide + [(b, a) for a, b in wide])  9.69 us
    pallas_call x5, Pallas kernels, placed(): return run(*operands[:smem + vmem], *held)  9.27 us
    ppermute x2, starting transfers between devices, beside(): lax.ppermute(v, ROW, odd + [(b, a) for a, b in odd])  5.78 us
    ppermute x2, waiting for transfers between devices, beside(): lax.ppermute(v, ROW, odd + [(b, a) for a, b in odd])  3.2 us
    ppermute x2, waiting for transfers between devices, over_side(): return lax.ppermute(line, COL, steps + [(b, a) for a, b in steps])  1.98 us
    ppermute x2, starting transfers between devices, over_side(): return lax.ppermute(line, COL, steps + [(b, a) for a, b in steps])  1.85 us
  transfers between devices with their start and end apart: 19, of which 8 were waited for; matrix products, arithmetic and copies ran while one was open for 0% of the time, Pallas kernels for 8%

profile of v2, /device:TPU:8, one launch (start us, length us, event | category | flops | bytes accessed | tf_op | source)
XLA Modules:
  0.0 63.1 jit_solution(10821626799794281330)
XLA Ops:
  1.3 1.4 %shard_map.113 = (f32[8,2176]{1,0:T(8,128)S(1)}, f32[1,128]{1,0:T(1,128)S(1)}, f32[48,1920]{1,0:T(8,128)S(1)}) custom-call(s32[1]{0:T(128)S(6)} %copy.20.count_ref, f32[48,1920]{1,0:T(8,128)} %refs_0_.1, s32[1,48]{1,0:T(1,128)} %bitcast.40, s32[2,512]{1,0:T(2,128)} %bitcast.43, s32[1,512]{1,0:T(1,128)} %bitcast.44, f32[1,512]{1,0:T(1,128)} %bitcast.45, ...), custom_call_target="tpu_custom_call" | custom-call | tf_op jit(solution)/shard_map/pallas_call | solution.py:311
  2.7 8.4 %collective-permute-start.3 = (f32[8,2176]{1,0:T(8,128)S(1)}, f32[8,2176]{1,0:T(8,128)S(1)}, u32[]{:S(2)}, u32[]{:S(2)}) collective-permute-start(f32[8,2176]{1,0:T(8,128)S(1)} %get-tuple-element.16), channel_id=1, source_target_pairs={{2,4},{3,5},{6,8},{7,9},{10,12},{11,13},{14,16},{15,17},{18,20},{1... | collective-permute-start | bytes 208904 | tf_op jit(solution)/shard_map/ppermute | solution.py:334
  11.1 0.0 collective-permute-start.2
  11.1 3.7 %collective-permute-start.1 = (f32[8,2176]{1,0:T(8,128)S(1)}, f32[8,2176]{1,0:T(8,128)S(1)}, u32[]{:S(2)}, u32[]{:S(2)}) collective-permute-start(f32[8,2176]{1,0:T(8,128)S(1)} %get-tuple-element.16), channel_id=1, source_target_pairs={{1,2},{5,6},{9,10},{13,14},{17,18},{21,22},{25,26},{29,30},{3,4},{... | collective-permute-start | bytes 208904 | tf_op jit(solution)/shard_map/ppermute | solution.py:332
  14.8 0.0 collective-permute-start
  14.8 4.3 %collective-permute-done = f32[8,2176]{1,0:T(8,128)S(1)} collective-permute-done((f32[8,2176]{1,0:T(8,128)S(1)}, f32[8,2176]{1,0:T(8,128)S(1)}, u32[]{:S(2)}, u32[]{:S(2)}) %collective-permute-start) | collective-permute-done | bytes 69664 | tf_op jit(solution)/shard_map/ppermute | solution.py:321
  19.1 0.0 collective-permute-done.1
  19.1 0.0 collective-permute-done.2
  19.1 0.0 collective-permute-done.3
  19.2 0.0 copy-start
  19.2 0.0 copy-start.1
  19.2 0.1 collective-permute-start.5
  19.3 1.7 %collective-permute-start.4 = (f32[5,8,2176]{2,1,0:T(8,128)S(1)}, f32[5,8,2176]{2,1,0:T(8,128)S(1)}, u32[]{:S(2)}, u32[]{:S(2)}) collective-permute-start(f32[5,8,2176]{2,1,0:T(8,128)S(1)} %bitcast_dynamic-update-slice_fusion.own_ref), channel_id=1, source_target_pairs={{0,32},{32,0},{1,33},{33,1},{2,34},{34,2},{3,35},{35,3},{4,36},{36... | collective-permute-start | bytes 1044488 | tf_op jit(solution)/shard_map/ppermute | solution.py:321
  21.0 3.0 %shard_map.114 = (bf16[15,384,256]{2,1,0:T(8,128)(2,1)S(1)}, bf16[15,256,256]{2,1,0:T(8,128)(2,1)S(1)}, bf16[15,384,256]{2,1,0:T(8,128)(2,1)S(1)}) custom-call(f32[3,15,128,128]{3,2,1,0:T(8,128)} %rotation_any.1, f32[15,128,128]{2,1,0:T(8,128)} %translation_any.1), custom_call_target="tpu_custom_call" | custom-call | flops 3000000000 | tf_op jit(solution)/shard_map/pallas_call | solution.py:311
  24.0 2.0 %collective-permute-done.5.side_ref = f32[5,8,2176]{2,1,0:T(8,128)S(1)} collective-permute-done((f32[5,8,2176]{2,1,0:T(8,128)S(1)}, f32[5,8,2176]{2,1,0:T(8,128)S(1)}, u32[]{:S(2)}, u32[]{:S(2)}) %collective-permute-start.5) | collective-permute-done | bytes 348192 | tf_op jit(solution)/shard_map/ppermute | solution.py:341
  26.0 0.0 collective-permute-done.4.core_ref
  26.0 0.0 copy-done
  26.0 0.0 copy-done.1
  26.0 1.9 %shard_map.115 = (f32[48,120]{1,0:T(8,128)S(1)}, f32[8,1920]{1,0:T(8,128)S(1)}, f32[8,2048]{1,0:T(8,128)S(1)}) custom-call(f32[5,8,2176]{2,1,0:T(8,128)S(1)} %bitcast_dynamic-update-slice_fusion.own_ref, f32[5,8,2176]{2,1,0:T(8,128)S(1)} %collective-permute-done.4.core_ref, f32[5,8,2176]{2,1,0:T(8,128)S(1)} %collective-permute-done.5.side_ref, ...), custom_call_target="tpu_custom_call" | custom-call | tf_op jit(solution)/shard_map/pallas_call | solution.py:311
  27.9 1.3 %collective-permute-start.9 = (f32[8,2048]{1,0:T(8,128)S(1)}, f32[8,2048]{1,0:T(8,128)S(1)}, u32[]{:S(2)}, u32[]{:S(2)}) collective-permute-start(f32[8,2048]{1,0:T(8,128)S(1)} %get-tuple-element.21), channel_id=1, source_target_pairs={{2,4},{3,5},{6,8},{7,9},{10,12},{11,13},{14,16},{15,17},{18,20},{1... | collective-permute-start | bytes 196616 | tf_op jit(solution)/shard_map/ppermute | solution.py:334
  29.2 2.8 %collective-permute-start.8 = (f32[8,2048]{1,0:T(8,128)S(1)}, f32[8,2048]{1,0:T(8,128)S(1)}, u32[]{:S(2)}, u32[]{:S(2)}) collective-permute-start(f32[8,2048]{1,0:T(8,128)S(1)} %get-tuple-element.21), channel_id=1, source_target_pairs={{0,2},{1,3},{2,0},{3,1},{4,6},{5,7},{6,4},{7,5},{8,10},{9,11},{10,... | collective-permute-start | bytes 196616 | tf_op jit(solution)/shard_map/ppermute | solution.py:321
  32.0 2.1 %collective-permute-start.7 = (f32[8,2048]{1,0:T(8,128)S(1)}, f32[8,2048]{1,0:T(8,128)S(1)}, u32[]{:S(2)}, u32[]{:S(2)}) collective-permute-start(f32[8,2048]{1,0:T(8,128)S(1)} %get-tuple-element.21), channel_id=1, source_target_pairs={{1,2},{5,6},{9,10},{13,14},{17,18},{21,22},{25,26},{29,30},{3,4},{... | collective-permute-start | bytes 196616 | tf_op jit(solution)/shard_map/ppermute | solution.py:332
  34.1 0.0 collective-permute-start.6
  34.1 2.3 %collective-permute-done.8 = f32[8,2048]{1,0:T(8,128)S(1)} collective-permute-done((f32[8,2048]{1,0:T(8,128)S(1)}, f32[8,2048]{1,0:T(8,128)S(1)}, u32[]{:S(2)}, u32[]{:S(2)}) %collective-permute-start.8) | collective-permute-done | bytes 65568 | tf_op jit(solution)/shard_map/ppermute | solution.py:321
  36.4 3.2 %collective-permute-done.7 = f32[8,2048]{1,0:T(8,128)S(1)} collective-permute-done((f32[8,2048]{1,0:T(8,128)S(1)}, f32[8,2048]{1,0:T(8,128)S(1)}, u32[]{:S(2)}, u32[]{:S(2)}) %collective-permute-start.7) | collective-permute-done | bytes 65568 | tf_op jit(solution)/shard_map/ppermute | solution.py:332
  39.6 0.0 collective-permute-done.6
  39.6 0.0 collective-permute-done.9
  39.7 0.1 collective-permute-start.10
  39.8 1.8 %collective-permute-start.11 = (f32[5,8,1920]{2,1,0:T(8,128)S(1)}, f32[5,8,1920]{2,1,0:T(8,128)S(1)}, u32[]{:S(2)}, u32[]{:S(2)}) collective-permute-start(f32[5,8,1920]{2,1,0:T(8,128)S(1)} %fusion.own_ref), channel_id=1, source_target_pairs={{32,64},{96,128},{160,192},{224,0},{64,32},{128,96},{192,160},{0,2... | collective-permute-start | bytes 921608 | tf_op jit(solution)/shard_map/ppermute | solution.py:341
  41.5 0.0 collective-permute-done.10.core_ref
  41.6 1.4 %collective-permute-start.14 = (f32[8,128]{1,0:T(8,128)S(1)}, f32[8,128]{1,0:T(8,128)S(1)}, u32[]{:S(2)}, u32[]{:S(2)}) collective-permute-start(f32[8,128]{1,0:T(8,128)S(1)} %slice_add_fusion), channel_id=1, source_target_pairs={{0,16},{4,20},{8,24},{12,28},{16,0},{20,4},{24,8},{28,12},{1,17},{... | collective-permute-start | bytes 12296 | tf_op jit(solution)/shard_map/ppermute | solution.py:321
  43.0 2.3 %collective-permute-start.13 = (f32[8,128]{1,0:T(8,128)S(1)}, f32[8,128]{1,0:T(8,128)S(1)}, u32[]{:S(2)}, u32[]{:S(2)}) collective-permute-start(f32[8,128]{1,0:T(8,128)S(1)} %slice_add_fusion), channel_id=1, source_target_pairs={{0,24},{4,28},{8,16},{12,20},{16,8},{20,12},{24,0},{28,4},{1,25},{... | collective-permute-start | bytes 12296 | tf_op jit(solution)/shard_map/ppermute | solution.py:321
  45.3 2.7 %collective-permute-start.12 = (f32[8,128]{1,0:T(8,128)S(1)}, f32[8,128]{1,0:T(8,128)S(1)}, u32[]{:S(2)}, u32[]{:S(2)}) collective-permute-start(f32[8,128]{1,0:T(8,128)S(1)} %slice_add_fusion), channel_id=1, source_target_pairs={{0,8},{4,12},{8,0},{12,4},{16,24},{20,28},{24,16},{28,20},{1,9},{5... | collective-permute-start | bytes 12296 | tf_op jit(solution)/shard_map/ppermute | solution.py:321
  48.0 1.0 %collective-permute-done.14 = f32[8,128]{1,0:T(8,128)S(1)} collective-permute-done((f32[8,128]{1,0:T(8,128)S(1)}, f32[8,128]{1,0:T(8,128)S(1)}, u32[]{:S(2)}, u32[]{:S(2)}) %collective-permute-start.14) | collective-permute-done | bytes 4128 | tf_op jit(solution)/shard_map/ppermute | solution.py:321
  49.1 0.0 collective-permute-done.13
  49.1 0.8 %collective-permute-done.12 = f32[8,128]{1,0:T(8,128)S(1)} collective-permute-done((f32[8,128]{1,0:T(8,128)S(1)}, f32[8,128]{1,0:T(8,128)S(1)}, u32[]{:S(2)}, u32[]{:S(2)}) %collective-permute-start.12) | collective-permute-done | bytes 4128 | tf_op jit(solution)/shard_map/ppermute | solution.py:321
  49.9 1.5 %collective-permute-start.17 = (f32[8,128]{1,0:T(8,128)S(1)}, f32[8,128]{1,0:T(8,128)S(1)}, u32[]{:S(2)}, u32[]{:S(2)}) collective-permute-start(f32[8,128]{1,0:T(8,128)S(1)} %add_add_fusion.1), channel_id=1, source_target_pairs={{0,192},{64,128},{128,64},{192,0},{1,193},{65,129},{129,65},{193,1... | collective-permute-start | bytes 12296 | tf_op jit(solution)/shard_map/ppermute | solution.py:321
  51.3 1.9 %collective-permute-start.16 = (f32[8,128]{1,0:T(8,128)S(1)}, f32[8,128]{1,0:T(8,128)S(1)}, u32[]{:S(2)}, u32[]{:S(2)}) collective-permute-start(f32[8,128]{1,0:T(8,128)S(1)} %add_add_fusion.1), channel_id=1, source_target_pairs={{0,64},{64,0},{128,192},{192,128},{1,65},{65,1},{129,193},{193,129... | collective-permute-start | bytes 12296 | tf_op jit(solution)/shard_map/ppermute | solution.py:321
  53.2 0.5 collective-permute-start.15
  53.7 0.0 collective-permute-done.11.side_ref
  53.7 1.9 %shard_map.116 = (f32[48,1920]{1,0:T(8,128)S(1)}, f32[48,1920]{1,0:T(8,128)S(1)}) custom-call(f32[5,8,1920]{2,1,0:T(8,128)S(1)} %fusion.own_ref, f32[48,1920]{1,0:T(8,128)S(1)} %collective-permute-done.10.core_ref, f32[5,8,1920]{2,1,0:T(8,128)S(1)} %collective-permute-done.11.side_ref, f32[48,120]{1,0:T(8,128)S(1)} %get-tuple-element.23.matrix_ref, ...), custom_call_target="tpu_custom_call" | custom-call | flops 5000000000 | tf_op jit(solution)/shard_map/pallas_call | solution.py:311
  55.6 0.0 collective-permute-done.17
  55.6 0.0 collective-permute-done.16
  55.6 2.7 %collective-permute-done.15 = f32[8,128]{1,0:T(8,128)S(1)} collective-permute-done((f32[8,128]{1,0:T(8,128)S(1)}, f32[8,128]{1,0:T(8,128)S(1)}, u32[]{:S(2)}, u32[]{:S(2)}) %collective-permute-start.15) | collective-permute-done | bytes 4128 | tf_op jit(solution)/shard_map/ppermute | solution.py:321
  58.3 1.1 %collective-permute-start.18 = (f32[8,128]{1,0:T(8,128)S(1)}, f32[8,128]{1,0:T(8,128)S(1)}, u32[]{:S(2)}, u32[]{:S(2)}) collective-permute-start(f32[8,128]{1,0:T(8,128)S(1)} %add_add_fusion), channel_id=1, source_target_pairs={{0,4},{4,0},{8,12},{12,8},{16,20},{20,16},{24,28},{28,24},{1,5},{5... | collective-permute-start | bytes 12296 | tf_op jit(solution)/shard_map/ppermute | solution.py:321
  59.5 2.5 %collective-permute-done.18 = f32[8,128]{1,0:T(8,128)S(1)} collective-permute-done((f32[8,128]{1,0:T(8,128)S(1)}, f32[8,128]{1,0:T(8,128)S(1)}, u32[]{:S(2)}, u32[]{:S(2)}) %collective-permute-start.18) | collective-permute-done | bytes 4128 | tf_op jit(solution)/shard_map/ppermute | solution.py:321
  62.0 1.1 %shard_map.117 = (f32[48,1920]{1,0:T(8,128)}, f32[48,1920]{1,0:T(8,128)}) custom-call(f32[48,1920]{1,0:T(8,128)S(1)} %get-tuple-element.15.rhs_ref, f32[48,1920]{1,0:T(8,128)S(1)} %get-tuple-element.25.first_ref, f32[48,1920]{1,0:T(8,128)S(1)} %get-tuple-element.26.second_ref, f32[8,128]{1,0:T(8,128)S(1)} %add.45.sums_ref), custom_call_target="tpu_custom_call" | custom-call | tf_op jit(solution)/shard_map/pallas_call | solution.py:311
  (16 shorter events, 0.1 us)
Async XLA Ops:
  2.7 16.5 %collective-permute-start.3 = (f32[8,2176]{1,0:T(8,128)S(1)}, f32[8,2176]{1,0:T(8,128)S(1)}, u32[]{:S(2)}, u32[]{:S(2)}) collective-permute-start(f32[8,2176]{1,0:T(8,128)S(1)} %get-tuple-element.16), channel_id=1, source_target_pairs={{2,4},{3,5},{6,8},{7,9},{10,12},{11,13},{14,16},{15,17},{18,20},{1... | collective-permute-start | bytes 208904 | tf_op jit(solution)/shard_map/ppermute | solution.py:334
  11.1 8.1 %collective-permute-start.2 = (f32[8,2176]{1,0:T(8,128)S(1)}, f32[8,2176]{1,0:T(8,128)S(1)}, u32[]{:S(2)}, u32[]{:S(2)}) collective-permute-start(f32[8,2176]{1,0:T(8,128)S(1)} %get-tuple-element.16), channel_id=1, source_target_pairs={{0,2},{1,3},{2,0},{3,1},{4,6},{5,7},{6,4},{7,5},{8,10},{9,11},{10,... | collective-permute-start | bytes 208904 | tf_op jit(solution)/shard_map/ppermute | solution.py:321
  11.1 8.0 %collective-permute-start.1 = (f32[8,2176]{1,0:T(8,128)S(1)}, f32[8,2176]{1,0:T(8,128)S(1)}, u32[]{:S(2)}, u32[]{:S(2)}) collective-permute-start(f32[8,2176]{1,0:T(8,128)S(1)} %get-tuple-element.16), channel_id=1, source_target_pairs={{1,2},{5,6},{9,10},{13,14},{17,18},{21,22},{25,26},{29,30},{3,4},{... | collective-permute-start | bytes 208904 | tf_op jit(solution)/shard_map/ppermute | solution.py:332
  14.8 4.3 %collective-permute-start = (f32[8,2176]{1,0:T(8,128)S(1)}, f32[8,2176]{1,0:T(8,128)S(1)}, u32[]{:S(2)}, u32[]{:S(2)}) collective-permute-start(f32[8,2176]{1,0:T(8,128)S(1)} %get-tuple-element.16), channel_id=1, source_target_pairs={{0,1},{1,0},{2,3},{3,2},{4,5},{5,4},{6,7},{7,6},{8,9},{9,8},{10,11... | collective-permute-start | bytes 208904 | tf_op jit(solution)/shard_map/ppermute | solution.py:321
  19.2 6.8 %copy-start = (f32[1920]{0:T(1024)S(1)}, f32[1920]{0:T(1024)}, u32[]{:S(2)}) copy-start(f32[1920]{0:T(1024)} %param.19) | copy-start | bytes 23044
  19.2 6.8 %copy-start.1 = (s32[48]{0:T(128)S(1)}, s32[48]{0:T(128)}, u32[]{:S(2)}) copy-start(s32[48]{0:T(128)} %param.11) | copy-start | bytes 580
  19.2 6.8 %collective-permute-start.5 = (f32[5,8,2176]{2,1,0:T(8,128)S(1)}, f32[5,8,2176]{2,1,0:T(8,128)S(1)}, u32[]{:S(2)}, u32[]{:S(2)}) collective-permute-start(f32[5,8,2176]{2,1,0:T(8,128)S(1)} %bitcast_dynamic-update-slice_fusion.own_ref), channel_id=1, source_target_pairs={{32,64},{96,128},{160,192},{224,0},{64,32},{128,96},{192,160},{0,2... | collective-permute-start | bytes 1044488 | tf_op jit(solution)/shard_map/ppermute | solution.py:341
  19.3 6.7 %collective-permute-start.4 = (f32[5,8,2176]{2,1,0:T(8,128)S(1)}, f32[5,8,2176]{2,1,0:T(8,128)S(1)}, u32[]{:S(2)}, u32[]{:S(2)}) collective-permute-start(f32[5,8,2176]{2,1,0:T(8,128)S(1)} %bitcast_dynamic-update-slice_fusion.own_ref), channel_id=1, source_target_pairs={{0,32},{32,0},{1,33},{33,1},{2,34},{34,2},{3,35},{35,3},{4,36},{36... | collective-permute-start | bytes 1044488 | tf_op jit(solution)/shard_map/ppermute | solution.py:321
  27.9 11.7 %collective-permute-start.9 = (f32[8,2048]{1,0:T(8,128)S(1)}, f32[8,2048]{1,0:T(8,128)S(1)}, u32[]{:S(2)}, u32[]{:S(2)}) collective-permute-start(f32[8,2048]{1,0:T(8,128)S(1)} %get-tuple-element.21), channel_id=1, source_target_pairs={{2,4},{3,5},{6,8},{7,9},{10,12},{11,13},{14,16},{15,17},{18,20},{1... | collective-permute-start | bytes 196616 | tf_op jit(solution)/shard_map/ppermute | solution.py:334
  29.2 7.2 %collective-permute-start.8 = (f32[8,2048]{1,0:T(8,128)S(1)}, f32[8,2048]{1,0:T(8,128)S(1)}, u32[]{:S(2)}, u32[]{:S(2)}) collective-permute-start(f32[8,2048]{1,0:T(8,128)S(1)} %get-tuple-element.21), channel_id=1, source_target_pairs={{0,2},{1,3},{2,0},{3,1},{4,6},{5,7},{6,4},{7,5},{8,10},{9,11},{10,... | collective-permute-start | bytes 196616 | tf_op jit(solution)/shard_map/ppermute | solution.py:321
  32.0 7.6 %collective-permute-start.7 = (f32[8,2048]{1,0:T(8,128)S(1)}, f32[8,2048]{1,0:T(8,128)S(1)}, u32[]{:S(2)}, u32[]{:S(2)}) collective-permute-start(f32[8,2048]{1,0:T(8,128)S(1)} %get-tuple-element.21), channel_id=1, source_target_pairs={{1,2},{5,6},{9,10},{13,14},{17,18},{21,22},{25,26},{29,30},{3,4},{... | collective-permute-start | bytes 196616 | tf_op jit(solution)/shard_map/ppermute | solution.py:332
  34.1 5.5 %collective-permute-start.6 = (f32[8,2048]{1,0:T(8,128)S(1)}, f32[8,2048]{1,0:T(8,128)S(1)}, u32[]{:S(2)}, u32[]{:S(2)}) collective-permute-start(f32[8,2048]{1,0:T(8,128)S(1)} %get-tuple-element.21), channel_id=1, source_target_pairs={{0,1},{1,0},{2,3},{3,2},{4,5},{5,4},{6,7},{7,6},{8,9},{9,8},{10,11... | collective-permute-start | bytes 196616 | tf_op jit(solution)/shard_map/ppermute | solution.py:321
  39.7 1.9 %collective-permute-start.10 = (f32[48,1920]{1,0:T(8,128)S(1)}, f32[48,1920]{1,0:T(8,128)S(1)}, u32[]{:S(2)}, u32[]{:S(2)}) collective-permute-start(f32[48,1920]{1,0:T(8,128)S(1)} %select_maximum_fusion), channel_id=1, source_target_pairs={{0,32},{32,0},{1,33},{33,1},{2,34},{34,2},{3,35},{35,3},{4,36},{36... | collective-permute-start | bytes 1105928 | tf_op jit(solution)/shard_map/ppermute | solution.py:321
  39.8 13.9 %collective-permute-start.11 = (f32[5,8,1920]{2,1,0:T(8,128)S(1)}, f32[5,8,1920]{2,1,0:T(8,128)S(1)}, u32[]{:S(2)}, u32[]{:S(2)}) collective-permute-start(f32[5,8,1920]{2,1,0:T(8,128)S(1)} %fusion.own_ref), channel_id=1, source_target_pairs={{32,64},{96,128},{160,192},{224,0},{64,32},{128,96},{192,160},{0,2... | collective-permute-start | bytes 921608 | tf_op jit(solution)/shard_map/ppermute | solution.py:341
  41.6 7.5 %collective-permute-start.14 = (f32[8,128]{1,0:T(8,128)S(1)}, f32[8,128]{1,0:T(8,128)S(1)}, u32[]{:S(2)}, u32[]{:S(2)}) collective-permute-start(f32[8,128]{1,0:T(8,128)S(1)} %slice_add_fusion), channel_id=1, source_target_pairs={{0,16},{4,20},{8,24},{12,28},{16,0},{20,4},{24,8},{28,12},{1,17},{... | collective-permute-start | bytes 12296 | tf_op jit(solution)/shard_map/ppermute | solution.py:321
  43.0 6.1 %collective-permute-start.13 = (f32[8,128]{1,0:T(8,128)S(1)}, f32[8,128]{1,0:T(8,128)S(1)}, u32[]{:S(2)}, u32[]{:S(2)}) collective-permute-start(f32[8,128]{1,0:T(8,128)S(1)} %slice_add_fusion), channel_id=1, source_target_pairs={{0,24},{4,28},{8,16},{12,20},{16,8},{20,12},{24,0},{28,4},{1,25},{... | collective-permute-start | bytes 12296 | tf_op jit(solution)/shard_map/ppermute | solution.py:321
  45.3 4.5 %collective-permute-start.12 = (f32[8,128]{1,0:T(8,128)S(1)}, f32[8,128]{1,0:T(8,128)S(1)}, u32[]{:S(2)}, u32[]{:S(2)}) collective-permute-start(f32[8,128]{1,0:T(8,128)S(1)} %slice_add_fusion), channel_id=1, source_target_pairs={{0,8},{4,12},{8,0},{12,4},{16,24},{20,28},{24,16},{28,20},{1,9},{5... | collective-permute-start | bytes 12296 | tf_op jit(solution)/shard_map/ppermute | solution.py:321
  49.9 5.8 %collective-permute-start.17 = (f32[8,128]{1,0:T(8,128)S(1)}, f32[8,128]{1,0:T(8,128)S(1)}, u32[]{:S(2)}, u32[]{:S(2)}) collective-permute-start(f32[8,128]{1,0:T(8,128)S(1)} %add_add_fusion.1), channel_id=1, source_target_pairs={{0,192},{64,128},{128,64},{192,0},{1,193},{65,129},{129,65},{193,1... | collective-permute-start | bytes 12296 | tf_op jit(solution)/shard_map/ppermute | solution.py:321
  51.3 4.3 %collective-permute-start.16 = (f32[8,128]{1,0:T(8,128)S(1)}, f32[8,128]{1,0:T(8,128)S(1)}, u32[]{:S(2)}, u32[]{:S(2)}) collective-permute-start(f32[8,128]{1,0:T(8,128)S(1)} %add_add_fusion.1), channel_id=1, source_target_pairs={{0,64},{64,0},{128,192},{192,128},{1,65},{65,1},{129,193},{193,129... | collective-permute-start | bytes 12296 | tf_op jit(solution)/shard_map/ppermute | solution.py:321
  53.2 5.1 %collective-permute-start.15 = (f32[8,128]{1,0:T(8,128)S(1)}, f32[8,128]{1,0:T(8,128)S(1)}, u32[]{:S(2)}, u32[]{:S(2)}) collective-permute-start(f32[8,128]{1,0:T(8,128)S(1)} %add_add_fusion.1), channel_id=1, source_target_pairs={{0,128},{64,192},{128,0},{192,64},{1,129},{65,193},{129,1},{193,65... | collective-permute-start | bytes 12296 | tf_op jit(solution)/shard_map/ppermute | solution.py:321
  58.3 3.6 %collective-permute-start.18 = (f32[8,128]{1,0:T(8,128)S(1)}, f32[8,128]{1,0:T(8,128)S(1)}, u32[]{:S(2)}, u32[]{:S(2)}) collective-permute-start(f32[8,128]{1,0:T(8,128)S(1)} %add_add_fusion), channel_id=1, source_target_pairs={{0,4},{4,0},{8,12},{12,8},{16,20},{20,16},{24,28},{28,24},{1,5},{5... | collective-permute-start | bytes 12296 | tf_op jit(solution)/shard_map/ppermute | solution.py:321

commit v3 on v2

--- a/solution.py
+++ b/solution.py
@@ -240,7 +240,7 @@
 
 def first_kernel(
     own_ref, core_ref, side_ref, square_ref, turn_ref, move_ref, back_ref, mie_ref, member_ref,
-    matrix_ref, field_ref, next_ref,
+    matrix_ref, field_ref, next_ref, sums_ref,
 ):
     refs = [r.at[i] for r in (own_ref, core_ref, side_ref) for i in range(5)]
     matrix = pair_matrix([(r[:, C : C + W], r[:, C + W : C + 2 * W]) for r in refs])
@@ -263,7 +263,7 @@
     row = sublanes((K, W))
     inner = jnp.sum(inner, axis=0, keepdims=True)
     square = jnp.sum(square, axis=0, keepdims=True)
-    next_ref[:, C:] = jnp.where(row == 0, square_ref[...], jnp.where(row == 1, inner, jnp.where(row == 2, square, 0.0)))
+    sums_ref[...] = jnp.where(row == 0, square_ref[...], jnp.where(row == 1, inner, jnp.where(row == 2, square, 0.0)))
 
 
 def second_kernel(
@@ -321,18 +321,18 @@
     return lax.ppermute(v, axis, [(i, i ^ mask) for i in range(lax.axis_size(axis))])
 
 
-def beside(v):
+def row_pairs():
     length = lax.axis_size("z")
+    devices = 4 * length
     inside = [(4 * z + 1, 4 * z + 2) for z in range(length)]
-    devices = 4 * length
     odd = inside + [(4 * z + 3, (4 * z + 4) % devices) for z in range(length)]
     wide = [(4 * z + i, (4 * z + i + 2) % devices) for z in range(length) for i in (2, 3)]
-    return (
-        swap(v, "x", 1),
-        lax.ppermute(v, ROW, odd + [(b, a) for a, b in odd]),
-        swap(v, "x", 2),
-        lax.ppermute(v, ROW, wide + [(b, a) for a, b in wide]),
-    )
+    return [odd + [(b, a) for a, b in odd], wide + [(b, a) for a, b in wide]]
+
+
+def beside(v):
+    odd, wide = row_pairs()
+    return swap(v, "x", 1), lax.ppermute(v, ROW, odd), swap(v, "x", 2), lax.ppermute(v, ROW, wide)
 
 
 def over_side(line):
@@ -387,10 +387,15 @@
         work=3 * 10**9,
     )(rotation, translation)
     line = jnp.stack((packed,) + beside(packed))
-    matrix, first, following = call(first_kernel, (like(6 * K, 15 * K), like(K, C), like(K, C + W)), 9)(
+    matrix, first, following, sums = call(
+        first_kernel, (like(6 * K, 15 * K), like(K, C), like(K, C), like(K, W)), 9
+    )(
         line, swap(line, "c", 1), over_side(line), squares, *weights, mie, member
     )
-    near = beside(following)
+    odd, wide = row_pairs()
+    far = lax.ppermute(following, ROW, wide)
+    following = jnp.concatenate([following, plus(sums, "z", (1,))], axis=1)
+    near = (swap(following, "x", 1), lax.ppermute(following, ROW, odd), swap(following, "x", 2), far)
     line = jnp.stack([v[:, :C] for v in (following,) + near])
     sums = after(sum(v[:, C:] for v in near[:3]) + following[:, C:], near[3])
     carried = jnp.concatenate([line.reshape(5 * K, C), jnp.pad(sums, ((0, 0), (0, C - W)))], axis=0)
@@ -402,7 +407,6 @@
     )
     sums = plus(sums, "z", (2, 6, 4))
     sums = plus(sums, "y", (2, 1, 3))
-    sums = plus(after(sums, second), "z", (1,))
     entries = float(lax.axis_size(ALL) * spheres * C)
     return tuple(
         call(functools.partial(last_kernel, entries), (like(spheres, C), like(spheres, C)), 4)(

time: 63.2 us -> 60.6 us (0.959)
  waiting for transfers between devices: 18.8 us -> 16.5 us
    ppermute x13, waiting for transfers between devices: 13.6 us -> 12.1 us  [swap(): lax.ppermute(v, axis, [(i, i ^ mask) for i in range(lax.axis_size(axis))])]
    ppermute x13, starting transfers between devices: 16.1 us -> 14.8 us  [swap(): lax.ppermute(v, axis, [(i, i ^ mask) for i in range(lax.axis_size(axis))])]
    ppermute x4, starting transfers between devices: 15.5 us -> 16.4 us  [the longest x1 8.4 us: beside(): lax.ppermute(v, ROW, wide)]
    ppermute x4, waiting for transfers between devices: 3.21 us -> 2.43 us  [the longest x1 2.43 us: body(): lax.ppermute(following, ROW, odd)]
where the time goes in v3:
time: 60.6 us; the launch traced here: 60.5 us
  starting transfers between devices  33.1 us (55%)
  waiting for transfers between devices  16.5 us (27%)
  Pallas kernels  9.26 us (15%)
  between operations  1.47 us (2%)
    ppermute x13, starting transfers between devices, swap(): lax.ppermute(v, axis, [(i, i ^ mask) for i in range(lax.axis_size(axis))])  14.8 us
    ppermute x13, waiting for transfers between devices, swap(): lax.ppermute(v, axis, [(i, i ^ mask) for i in range(lax.axis_size(axis))])  12.1 us
    pallas_call x5, Pallas kernels, placed(): return run(*operands[:smem + vmem], *held)  9.26 us
    ppermute x1, starting transfers between devices, beside(): lax.ppermute(v, ROW, wide)  8.4 us
    ppermute x1, starting transfers between devices, beside(): lax.ppermute(v, ROW, odd)  3.71 us
    ppermute x1, starting transfers between devices, body(): lax.ppermute(following, ROW, odd)  3.29 us
    ppermute x1, waiting for transfers between devices, body(): lax.ppermute(following, ROW, odd)  2.43 us
    ppermute x2, waiting for transfers between devices, over_side(): return lax.ppermute(line, COL, steps + [(b, a) for a, b in steps])  1.98 us
  transfers between devices with their start and end apart: 19, of which 8 were waited for; matrix products, arithmetic and copies ran while one was open for 0% of the time, Pallas kernels for 8%

profile of v3, /device:TPU:8, one launch (start us, length us, event | category | flops | bytes accessed | tf_op | source)
XLA Modules:
  0.0 60.5 jit_solution(12012046661449503911)
XLA Ops:
  1.3 1.4 %shard_map.113 = (f32[8,2176]{1,0:T(8,128)S(1)}, f32[1,128]{1,0:T(1,128)S(1)}, f32[48,1920]{1,0:T(8,128)S(1)}) custom-call(s32[1]{0:T(128)S(6)} %copy.20.count_ref, f32[48,1920]{1,0:T(8,128)} %refs_0_.1, s32[1,48]{1,0:T(1,128)} %bitcast.38, s32[2,512]{1,0:T(2,128)} %bitcast.41, s32[1,512]{1,0:T(1,128)} %bitcast.42, f32[1,512]{1,0:T(1,128)} %bitcast.43, ...), custom_call_target="tpu_custom_call" | custom-call | tf_op jit(solution)/shard_map/pallas_call | solution.py:311
  2.7 8.4 %collective-permute-start.3 = (f32[8,2176]{1,0:T(8,128)S(1)}, f32[8,2176]{1,0:T(8,128)S(1)}, u32[]{:S(2)}, u32[]{:S(2)}) collective-permute-start(f32[8,2176]{1,0:T(8,128)S(1)} %get-tuple-element.16), channel_id=1, source_target_pairs={{2,4},{3,5},{6,8},{7,9},{10,12},{11,13},{14,16},{15,17},{18,20},{1... | collective-permute-start | bytes 208904 | tf_op jit(solution)/shard_map/ppermute | solution.py:335
  11.1 0.0 collective-permute-start.2
  11.1 3.7 %collective-permute-start.1 = (f32[8,2176]{1,0:T(8,128)S(1)}, f32[8,2176]{1,0:T(8,128)S(1)}, u32[]{:S(2)}, u32[]{:S(2)}) collective-permute-start(f32[8,2176]{1,0:T(8,128)S(1)} %get-tuple-element.16), channel_id=1, source_target_pairs={{1,2},{5,6},{9,10},{13,14},{17,18},{21,22},{25,26},{29,30},{3,4},{... | collective-permute-start | bytes 208904 | tf_op jit(solution)/shard_map/ppermute | solution.py:335
  14.8 0.0 collective-permute-start
  14.8 4.3 %collective-permute-done = f32[8,2176]{1,0:T(8,128)S(1)} collective-permute-done((f32[8,2176]{1,0:T(8,128)S(1)}, f32[8,2176]{1,0:T(8,128)S(1)}, u32[]{:S(2)}, u32[]{:S(2)}) %collective-permute-start) | collective-permute-done | bytes 69664 | tf_op jit(solution)/shard_map/ppermute | solution.py:321
  19.1 0.0 collective-permute-done.1
  19.1 0.0 collective-permute-done.2
  19.1 0.0 collective-permute-done.3
  19.2 0.0 copy-start
  19.2 0.0 copy-start.1
  19.2 0.1 collective-permute-start.5
  19.3 1.7 %collective-permute-start.4 = (f32[5,8,2176]{2,1,0:T(8,128)S(1)}, f32[5,8,2176]{2,1,0:T(8,128)S(1)}, u32[]{:S(2)}, u32[]{:S(2)}) collective-permute-start(f32[5,8,2176]{2,1,0:T(8,128)S(1)} %bitcast_dynamic-update-slice_fusion.own_ref), channel_id=1, source_target_pairs={{0,32},{32,0},{1,33},{33,1},{2,34},{34,2},{3,35},{35,3},{4,36},{36... | collective-permute-start | bytes 1044488 | tf_op jit(solution)/shard_map/ppermute | solution.py:321
  21.0 3.0 %shard_map.114 = (bf16[15,384,256]{2,1,0:T(8,128)(2,1)S(1)}, bf16[15,256,256]{2,1,0:T(8,128)(2,1)S(1)}, bf16[15,384,256]{2,1,0:T(8,128)(2,1)S(1)}) custom-call(f32[3,15,128,128]{3,2,1,0:T(8,128)} %rotation_any.1, f32[15,128,128]{2,1,0:T(8,128)} %translation_any.1), custom_call_target="tpu_custom_call" | custom-call | flops 3000000000 | tf_op jit(solution)/shard_map/pallas_call | solution.py:311
  24.0 2.0 %collective-permute-done.5.side_ref = f32[5,8,2176]{2,1,0:T(8,128)S(1)} collective-permute-done((f32[5,8,2176]{2,1,0:T(8,128)S(1)}, f32[5,8,2176]{2,1,0:T(8,128)S(1)}, u32[]{:S(2)}, u32[]{:S(2)}) %collective-permute-start.5) | collective-permute-done | bytes 348192 | tf_op jit(solution)/shard_map/ppermute | solution.py:341
  26.0 0.0 collective-permute-done.4.core_ref
  26.0 0.0 copy-done
  26.0 0.0 copy-done.1
  26.0 1.9 %shard_map.115 = (f32[48,120]{1,0:T(8,128)S(1)}, f32[8,1920]{1,0:T(8,128)S(1)}, f32[8,1920]{1,0:T(8,128)S(1)}, f32[8,128]{1,0:T(8,128)S(1)}) custom-call(f32[5,8,2176]{2,1,0:T(8,128)S(1)} %bitcast_dynamic-update-slice_fusion.own_ref, f32[5,8,2176]{2,1,0:T(8,128)S(1)} %collective-permute-done.4.core_ref, f32[5,8,2176]{2,1,0:T(8,128)S(1)} %collective-permute-done.5.side_ref, ...), custom_call_target="tpu_custom_call" | custom-call | tf_op jit(solution)/shard_map/pallas_call | solution.py:311
  27.9 1.1 %collective-permute-start.6 = (f32[8,128]{1,0:T(8,128)S(1)}, f32[8,128]{1,0:T(8,128)S(1)}, u32[]{:S(2)}, u32[]{:S(2)}) collective-permute-start(f32[8,128]{1,0:T(8,128)S(1)} %get-tuple-element.22), channel_id=1, source_target_pairs={{0,4},{4,0},{8,12},{12,8},{16,20},{20,16},{24,28},{28,24},{1,5},{5... | collective-permute-start | bytes 12296 | tf_op jit(solution)/shard_map/ppermute | solution.py:321
  29.0 1.0 %collective-permute-start.10 = (f32[8,1920]{1,0:T(8,128)S(1)}, f32[8,1920]{1,0:T(8,128)S(1)}, u32[]{:S(2)}, u32[]{:S(2)}) collective-permute-start(f32[8,1920]{1,0:T(8,128)S(1)} %get-tuple-element.21), channel_id=1, source_target_pairs={{2,4},{3,5},{6,8},{7,9},{10,12},{11,13},{14,16},{15,17},{18,20},{1... | collective-permute-start | bytes 184328 | tf_op jit(solution)/shard_map/ppermute | solution.py:396
  30.1 1.6 %collective-permute-done.6 = f32[8,128]{1,0:T(8,128)S(1)} collective-permute-done((f32[8,128]{1,0:T(8,128)S(1)}, f32[8,128]{1,0:T(8,128)S(1)}, u32[]{:S(2)}, u32[]{:S(2)}) %collective-permute-start.6) | collective-permute-done | bytes 4128 | tf_op jit(solution)/shard_map/ppermute | solution.py:321
  31.6 1.5 %collective-permute-start.9 = (f32[8,2048]{1,0:T(8,128)S(1)}, f32[8,2048]{1,0:T(8,128)S(1)}, u32[]{:S(2)}, u32[]{:S(2)}) collective-permute-start(f32[8,2048]{1,0:T(8,128)S(1)} %pad_maximum_fusion), channel_id=1, source_target_pairs={{0,2},{1,3},{2,0},{3,1},{4,6},{5,7},{6,4},{7,5},{8,10},{9,11},{10,... | collective-permute-start | bytes 196616 | tf_op jit(solution)/shard_map/ppermute | solution.py:321
  33.1 3.3 %collective-permute-start.8 = (f32[8,2048]{1,0:T(8,128)S(1)}, f32[8,2048]{1,0:T(8,128)S(1)}, u32[]{:S(2)}, u32[]{:S(2)}) collective-permute-start(f32[8,2048]{1,0:T(8,128)S(1)} %pad_maximum_fusion), channel_id=1, source_target_pairs={{1,2},{5,6},{9,10},{13,14},{17,18},{21,22},{25,26},{29,30},{3,4},{... | collective-permute-start | bytes 196616 | tf_op jit(solution)/shard_map/ppermute | solution.py:398
  36.4 0.0 collective-permute-start.7
  36.4 1.9 %collective-permute-done.9 = f32[8,2048]{1,0:T(8,128)S(1)} collective-permute-done((f32[8,2048]{1,0:T(8,128)S(1)}, f32[8,2048]{1,0:T(8,128)S(1)}, u32[]{:S(2)}, u32[]{:S(2)}) %collective-permute-start.9) | collective-permute-done | bytes 65568 | tf_op jit(solution)/shard_map/ppermute | solution.py:321
  38.3 2.4 %collective-permute-done.8 = f32[8,2048]{1,0:T(8,128)S(1)} collective-permute-done((f32[8,2048]{1,0:T(8,128)S(1)}, f32[8,2048]{1,0:T(8,128)S(1)}, u32[]{:S(2)}, u32[]{:S(2)}) %collective-permute-start.8) | collective-permute-done | bytes 65568 | tf_op jit(solution)/shard_map/ppermute | solution.py:398
  40.7 0.0 collective-permute-done.7
  40.7 0.0 collective-permute-done.10
  40.8 0.1 collective-permute-start.11
  40.9 1.8 %collective-permute-start.12 = (f32[5,8,1920]{2,1,0:T(8,128)S(1)}, f32[5,8,1920]{2,1,0:T(8,128)S(1)}, u32[]{:S(2)}, u32[]{:S(2)}) collective-permute-start(f32[5,8,1920]{2,1,0:T(8,128)S(1)} %bitcast_dynamic-update-slice_fusion.5.own_ref), channel_id=1, source_target_pairs={{32,64},{96,128},{160,192},{224,0},{64,32},{128,96},{192,160},{0,2... | collective-permute-start | bytes 921608 | tf_op jit(solution)/shard_map/ppermute | solution.py:341
  42.7 0.0 collective-permute-done.11.core_ref
  42.7 2.4 %collective-permute-start.15 = (f32[8,128]{1,0:T(8,128)S(1)}, f32[8,128]{1,0:T(8,128)S(1)}, u32[]{:S(2)}, u32[]{:S(2)}) collective-permute-start(f32[8,128]{1,0:T(8,128)S(1)} %slice_add_fusion), channel_id=1, source_target_pairs={{0,16},{4,20},{8,24},{12,28},{16,0},{20,4},{24,8},{28,12},{1,17},{... | collective-permute-start | bytes 12296 | tf_op jit(solution)/shard_map/ppermute | solution.py:321
  45.1 1.0 %collective-permute-start.14 = (f32[8,128]{1,0:T(8,128)S(1)}, f32[8,128]{1,0:T(8,128)S(1)}, u32[]{:S(2)}, u32[]{:S(2)}) collective-permute-start(f32[8,128]{1,0:T(8,128)S(1)} %slice_add_fusion), channel_id=1, source_target_pairs={{0,24},{4,28},{8,16},{12,20},{16,8},{20,12},{24,0},{28,4},{1,25},{... | collective-permute-start | bytes 12296 | tf_op jit(solution)/shard_map/ppermute | solution.py:321
  46.1 3.1 %collective-permute-start.13 = (f32[8,128]{1,0:T(8,128)S(1)}, f32[8,128]{1,0:T(8,128)S(1)}, u32[]{:S(2)}, u32[]{:S(2)}) collective-permute-start(f32[8,128]{1,0:T(8,128)S(1)} %slice_add_fusion), channel_id=1, source_target_pairs={{0,8},{4,12},{8,0},{12,4},{16,24},{20,28},{24,16},{28,20},{1,9},{5... | collective-permute-start | bytes 12296 | tf_op jit(solution)/shard_map/ppermute | solution.py:321
  49.2 1.0 %collective-permute-done.15 = f32[8,128]{1,0:T(8,128)S(1)} collective-permute-done((f32[8,128]{1,0:T(8,128)S(1)}, f32[8,128]{1,0:T(8,128)S(1)}, u32[]{:S(2)}, u32[]{:S(2)}) %collective-permute-start.15) | collective-permute-done | bytes 4128 | tf_op jit(solution)/shard_map/ppermute | solution.py:321
  50.2 0.6 %collective-permute-done.14 = f32[8,128]{1,0:T(8,128)S(1)} collective-permute-done((f32[8,128]{1,0:T(8,128)S(1)}, f32[8,128]{1,0:T(8,128)S(1)}, u32[]{:S(2)}, u32[]{:S(2)}) %collective-permute-start.14) | collective-permute-done | bytes 4128 | tf_op jit(solution)/shard_map/ppermute | solution.py:321
  50.8 0.0 collective-permute-done.13
  50.8 1.6 %collective-permute-start.18 = (f32[8,128]{1,0:T(8,128)S(1)}, f32[8,128]{1,0:T(8,128)S(1)}, u32[]{:S(2)}, u32[]{:S(2)}) collective-permute-start(f32[8,128]{1,0:T(8,128)S(1)} %add_add_fusion.1), channel_id=1, source_target_pairs={{0,192},{64,128},{128,64},{192,0},{1,193},{65,129},{129,65},{193,1... | collective-permute-start | bytes 12296 | tf_op jit(solution)/shard_map/ppermute | solution.py:321
  52.4 1.9 %collective-permute-start.17 = (f32[8,128]{1,0:T(8,128)S(1)}, f32[8,128]{1,0:T(8,128)S(1)}, u32[]{:S(2)}, u32[]{:S(2)}) collective-permute-start(f32[8,128]{1,0:T(8,128)S(1)} %add_add_fusion.1), channel_id=1, source_target_pairs={{0,64},{64,0},{128,192},{192,128},{1,65},{65,1},{129,193},{193,129... | collective-permute-start | bytes 12296 | tf_op jit(solution)/shard_map/ppermute | solution.py:321
  54.3 0.5 collective-permute-start.16
  54.8 0.0 collective-permute-done.12.side_ref
  54.8 1.9 %shard_map.116 = (f32[48,1920]{1,0:T(8,128)S(1)}, f32[48,1920]{1,0:T(8,128)S(1)}) custom-call(f32[5,8,1920]{2,1,0:T(8,128)S(1)} %bitcast_dynamic-update-slice_fusion.5.own_ref, f32[48,1920]{1,0:T(8,128)S(1)} %collective-permute-done.11.core_ref, f32[5,8,1920]{2,1,0:T(8,128)S(1)} %collective-permute-done.12.side_ref, ...), custom_call_target="tpu_custom_call" | custom-call | flops 5000000000 | tf_op jit(solution)/shard_map/pallas_call | solution.py:311
  56.7 0.0 collective-permute-done.18
  56.7 0.0 collective-permute-done.17
  56.7 2.7 %collective-permute-done.16 = f32[8,128]{1,0:T(8,128)S(1)} collective-permute-done((f32[8,128]{1,0:T(8,128)S(1)}, f32[8,128]{1,0:T(8,128)S(1)}, u32[]{:S(2)}, u32[]{:S(2)}) %collective-permute-start.16) | collective-permute-done | bytes 4128 | tf_op jit(solution)/shard_map/ppermute | solution.py:321
  59.4 1.1 %shard_map.117 = (f32[48,1920]{1,0:T(8,128)}, f32[48,1920]{1,0:T(8,128)}) custom-call(f32[48,1920]{1,0:T(8,128)S(1)} %get-tuple-element.15.rhs_ref, f32[48,1920]{1,0:T(8,128)S(1)} %get-tuple-element.26.first_ref, f32[48,1920]{1,0:T(8,128)S(1)} %get-tuple-element.27.second_ref, f32[8,128]{1,0:T(8,128)S(1)} %add_add_fusion.sums_ref), custom_call_target="tpu_custom_call" | custom-call | tf_op jit(solution)/shard_map/pallas_call | solution.py:311
  (17 shorter events, 0.1 us)
Async XLA Ops:
  2.7 16.5 %collective-permute-start.3 = (f32[8,2176]{1,0:T(8,128)S(1)}, f32[8,2176]{1,0:T(8,128)S(1)}, u32[]{:S(2)}, u32[]{:S(2)}) collective-permute-start(f32[8,2176]{1,0:T(8,128)S(1)} %get-tuple-element.16), channel_id=1, source_target_pairs={{2,4},{3,5},{6,8},{7,9},{10,12},{11,13},{14,16},{15,17},{18,20},{1... | collective-permute-start | bytes 208904 | tf_op jit(solution)/shard_map/ppermute | solution.py:335
  11.1 8.1 %collective-permute-start.2 = (f32[8,2176]{1,0:T(8,128)S(1)}, f32[8,2176]{1,0:T(8,128)S(1)}, u32[]{:S(2)}, u32[]{:S(2)}) collective-permute-start(f32[8,2176]{1,0:T(8,128)S(1)} %get-tuple-element.16), channel_id=1, source_target_pairs={{0,2},{1,3},{2,0},{3,1},{4,6},{5,7},{6,4},{7,5},{8,10},{9,11},{10,... | collective-permute-start | bytes 208904 | tf_op jit(solution)/shard_map/ppermute | solution.py:321
  11.1 8.0 %collective-permute-start.1 = (f32[8,2176]{1,0:T(8,128)S(1)}, f32[8,2176]{1,0:T(8,128)S(1)}, u32[]{:S(2)}, u32[]{:S(2)}) collective-permute-start(f32[8,2176]{1,0:T(8,128)S(1)} %get-tuple-element.16), channel_id=1, source_target_pairs={{1,2},{5,6},{9,10},{13,14},{17,18},{21,22},{25,26},{29,30},{3,4},{... | collective-permute-start | bytes 208904 | tf_op jit(solution)/shard_map/ppermute | solution.py:335
  14.8 4.3 %collective-permute-start = (f32[8,2176]{1,0:T(8,128)S(1)}, f32[8,2176]{1,0:T(8,128)S(1)}, u32[]{:S(2)}, u32[]{:S(2)}) collective-permute-start(f32[8,2176]{1,0:T(8,128)S(1)} %get-tuple-element.16), channel_id=1, source_target_pairs={{0,1},{1,0},{2,3},{3,2},{4,5},{5,4},{6,7},{7,6},{8,9},{9,8},{10,11... | collective-permute-start | bytes 208904 | tf_op jit(solution)/shard_map/ppermute | solution.py:321
  19.2 6.8 %copy-start = (f32[1920]{0:T(1024)S(1)}, f32[1920]{0:T(1024)}, u32[]{:S(2)}) copy-start(f32[1920]{0:T(1024)} %param.19) | copy-start | bytes 23044
  19.2 6.8 %copy-start.1 = (s32[48]{0:T(128)S(1)}, s32[48]{0:T(128)}, u32[]{:S(2)}) copy-start(s32[48]{0:T(128)} %param.11) | copy-start | bytes 580
  19.2 6.8 %collective-permute-start.5 = (f32[5,8,2176]{2,1,0:T(8,128)S(1)}, f32[5,8,2176]{2,1,0:T(8,128)S(1)}, u32[]{:S(2)}, u32[]{:S(2)}) collective-permute-start(f32[5,8,2176]{2,1,0:T(8,128)S(1)} %bitcast_dynamic-update-slice_fusion.own_ref), channel_id=1, source_target_pairs={{32,64},{96,128},{160,192},{224,0},{64,32},{128,96},{192,160},{0,2... | collective-permute-start | bytes 1044488 | tf_op jit(solution)/shard_map/ppermute | solution.py:341
  19.3 6.7 %collective-permute-start.4 = (f32[5,8,2176]{2,1,0:T(8,128)S(1)}, f32[5,8,2176]{2,1,0:T(8,128)S(1)}, u32[]{:S(2)}, u32[]{:S(2)}) collective-permute-start(f32[5,8,2176]{2,1,0:T(8,128)S(1)} %bitcast_dynamic-update-slice_fusion.own_ref), channel_id=1, source_target_pairs={{0,32},{32,0},{1,33},{33,1},{2,34},{34,2},{3,35},{35,3},{4,36},{36... | collective-permute-start | bytes 1044488 | tf_op jit(solution)/shard_map/ppermute | solution.py:321
  27.9 3.7 %collective-permute-start.6 = (f32[8,128]{1,0:T(8,128)S(1)}, f32[8,128]{1,0:T(8,128)S(1)}, u32[]{:S(2)}, u32[]{:S(2)}) collective-permute-start(f32[8,128]{1,0:T(8,128)S(1)} %get-tuple-element.22), channel_id=1, source_target_pairs={{0,4},{4,0},{8,12},{12,8},{16,20},{20,16},{24,28},{28,24},{1,5},{5... | collective-permute-start | bytes 12296 | tf_op jit(solution)/shard_map/ppermute | solution.py:321
  29.0 11.7 %collective-permute-start.10 = (f32[8,1920]{1,0:T(8,128)S(1)}, f32[8,1920]{1,0:T(8,128)S(1)}, u32[]{:S(2)}, u32[]{:S(2)}) collective-permute-start(f32[8,1920]{1,0:T(8,128)S(1)} %get-tuple-element.21), channel_id=1, source_target_pairs={{2,4},{3,5},{6,8},{7,9},{10,12},{11,13},{14,16},{15,17},{18,20},{1... | collective-permute-start | bytes 184328 | tf_op jit(solution)/shard_map/ppermute | solution.py:396
  31.6 6.6 %collective-permute-start.9 = (f32[8,2048]{1,0:T(8,128)S(1)}, f32[8,2048]{1,0:T(8,128)S(1)}, u32[]{:S(2)}, u32[]{:S(2)}) collective-permute-start(f32[8,2048]{1,0:T(8,128)S(1)} %pad_maximum_fusion), channel_id=1, source_target_pairs={{0,2},{1,3},{2,0},{3,1},{4,6},{5,7},{6,4},{7,5},{8,10},{9,11},{10,... | collective-permute-start | bytes 196616 | tf_op jit(solution)/shard_map/ppermute | solution.py:321
  33.1 7.6 %collective-permute-start.8 = (f32[8,2048]{1,0:T(8,128)S(1)}, f32[8,2048]{1,0:T(8,128)S(1)}, u32[]{:S(2)}, u32[]{:S(2)}) collective-permute-start(f32[8,2048]{1,0:T(8,128)S(1)} %pad_maximum_fusion), channel_id=1, source_target_pairs={{1,2},{5,6},{9,10},{13,14},{17,18},{21,22},{25,26},{29,30},{3,4},{... | collective-permute-start | bytes 196616 | tf_op jit(solution)/shard_map/ppermute | solution.py:398
  36.4 4.3 %collective-permute-start.7 = (f32[8,2048]{1,0:T(8,128)S(1)}, f32[8,2048]{1,0:T(8,128)S(1)}, u32[]{:S(2)}, u32[]{:S(2)}) collective-permute-start(f32[8,2048]{1,0:T(8,128)S(1)} %pad_maximum_fusion), channel_id=1, source_target_pairs={{0,1},{1,0},{2,3},{3,2},{4,5},{5,4},{6,7},{7,6},{8,9},{9,8},{10,11... | collective-permute-start | bytes 196616 | tf_op jit(solution)/shard_map/ppermute | solution.py:321
  40.8 1.9 %collective-permute-start.11 = (f32[48,1920]{1,0:T(8,128)S(1)}, f32[48,1920]{1,0:T(8,128)S(1)}, u32[]{:S(2)}, u32[]{:S(2)}) collective-permute-start(f32[48,1920]{1,0:T(8,128)S(1)} %select_maximum_fusion), channel_id=1, source_target_pairs={{0,32},{32,0},{1,33},{33,1},{2,34},{34,2},{3,35},{35,3},{4,36},{36... | collective-permute-start | bytes 1105928 | tf_op jit(solution)/shard_map/ppermute | solution.py:321
  40.9 13.9 %collective-permute-start.12 = (f32[5,8,1920]{2,1,0:T(8,128)S(1)}, f32[5,8,1920]{2,1,0:T(8,128)S(1)}, u32[]{:S(2)}, u32[]{:S(2)}) collective-permute-start(f32[5,8,1920]{2,1,0:T(8,128)S(1)} %bitcast_dynamic-update-slice_fusion.5.own_ref), channel_id=1, source_target_pairs={{32,64},{96,128},{160,192},{224,0},{64,32},{128,96},{192,160},{0,2... | collective-permute-start | bytes 921608 | tf_op jit(solution)/shard_map/ppermute | solution.py:341
  42.7 7.5 %collective-permute-start.15 = (f32[8,128]{1,0:T(8,128)S(1)}, f32[8,128]{1,0:T(8,128)S(1)}, u32[]{:S(2)}, u32[]{:S(2)}) collective-permute-start(f32[8,128]{1,0:T(8,128)S(1)} %slice_add_fusion), channel_id=1, source_target_pairs={{0,16},{4,20},{8,24},{12,28},{16,0},{20,4},{24,8},{28,12},{1,17},{... | collective-permute-start | bytes 12296 | tf_op jit(solution)/shard_map/ppermute | solution.py:321
  45.1 5.7 %collective-permute-start.14 = (f32[8,128]{1,0:T(8,128)S(1)}, f32[8,128]{1,0:T(8,128)S(1)}, u32[]{:S(2)}, u32[]{:S(2)}) collective-permute-start(f32[8,128]{1,0:T(8,128)S(1)} %slice_add_fusion), channel_id=1, source_target_pairs={{0,24},{4,28},{8,16},{12,20},{16,8},{20,12},{24,0},{28,4},{1,25},{... | collective-permute-start | bytes 12296 | tf_op jit(solution)/shard_map/ppermute | solution.py:321
  46.1 4.7 %collective-permute-start.13 = (f32[8,128]{1,0:T(8,128)S(1)}, f32[8,128]{1,0:T(8,128)S(1)}, u32[]{:S(2)}, u32[]{:S(2)}) collective-permute-start(f32[8,128]{1,0:T(8,128)S(1)} %slice_add_fusion), channel_id=1, source_target_pairs={{0,8},{4,12},{8,0},{12,4},{16,24},{20,28},{24,16},{28,20},{1,9},{5... | collective-permute-start | bytes 12296 | tf_op jit(solution)/shard_map/ppermute | solution.py:321
  50.8 5.8 %collective-permute-start.18 = (f32[8,128]{1,0:T(8,128)S(1)}, f32[8,128]{1,0:T(8,128)S(1)}, u32[]{:S(2)}, u32[]{:S(2)}) collective-permute-start(f32[8,128]{1,0:T(8,128)S(1)} %add_add_fusion.1), channel_id=1, source_target_pairs={{0,192},{64,128},{128,64},{192,0},{1,193},{65,129},{129,65},{193,1... | collective-permute-start | bytes 12296 | tf_op jit(solution)/shard_map/ppermute | solution.py:321
  52.4 4.3 %collective-permute-start.17 = (f32[8,128]{1,0:T(8,128)S(1)}, f32[8,128]{1,0:T(8,128)S(1)}, u32[]{:S(2)}, u32[]{:S(2)}) collective-permute-start(f32[8,128]{1,0:T(8,128)S(1)} %add_add_fusion.1), channel_id=1, source_target_pairs={{0,64},{64,0},{128,192},{192,128},{1,65},{65,1},{129,193},{193,129... | collective-permute-start | bytes 12296 | tf_op jit(solution)/shard_map/ppermute | solution.py:321
  54.3 5.1 %collective-permute-start.16 = (f32[8,128]{1,0:T(8,128)S(1)}, f32[8,128]{1,0:T(8,128)S(1)}, u32[]{:S(2)}, u32[]{:S(2)}) collective-permute-start(f32[8,128]{1,0:T(8,128)S(1)} %add_add_fusion.1), channel_id=1, source_target_pairs={{0,128},{64,192},{128,0},{192,64},{1,129},{65,193},{129,1},{193,65... | collective-permute-start | bytes 12296 | tf_op jit(solution)/shard_map/ppermute | solution.py:321

commit v4 on v3

--- a/solution.py
+++ b/solution.py
@@ -239,10 +239,11 @@
 
 
 def first_kernel(
-    own_ref, core_ref, side_ref, square_ref, turn_ref, move_ref, back_ref, mie_ref, member_ref,
+    own_ref, core_ref, wide_ref, close_ref, square_ref, turn_ref, move_ref, back_ref, mie_ref, member_ref,
     matrix_ref, field_ref, next_ref, sums_ref,
 ):
-    refs = [r.at[i] for r in (own_ref, core_ref, side_ref) for i in range(5)]
+    refs = [r.at[i] for r in (own_ref, core_ref) for i in range(5)]
+    refs += [wide_ref.at[0], close_ref.at[0], close_ref.at[1], wide_ref.at[1], wide_ref.at[2]]
     matrix = pair_matrix([(r[:, C : C + W], r[:, C + W : C + 2 * W]) for r in refs])
     matrix_ref[...] = matrix
     rows = jnp.concatenate([r[:, :C] for r in refs], axis=0)
@@ -386,11 +387,14 @@
         [pltpu.VMEM(rotation.shape, F32), pltpu.VMEM(translation.shape, F32), pltpu.SemaphoreType.DMA((2,))],
         work=3 * 10**9,
     )(rotation, translation)
-    line = jnp.stack((packed,) + beside(packed))
+    one, back_one, two, back_two = beside(packed)
+    wide_side = over_side(jnp.stack([packed, two, back_two]))
+    close_side = over_side(after(jnp.stack([one, back_one]), weights[1]))
+    line = jnp.stack([packed, one, back_one, two, back_two])
     matrix, first, following, sums = call(
-        first_kernel, (like(6 * K, 15 * K), like(K, C), like(K, C), like(K, W)), 9
+        first_kernel, (like(6 * K, 15 * K), like(K, C), like(K, C), like(K, W)), 10
     )(
-        line, swap(line, "c", 1), over_side(line), squares, *weights, mie, member
+        line, swap(line, "c", 1), wide_side, close_side, squares, *weights, mie, member
     )
     odd, wide = row_pairs()
     far = lax.ppermute(following, ROW, wide)

time: 60.6 us -> 61.1 us (level)
  starting transfers between devices: 33.1 us -> 34.2 us
    ppermute x13, waiting for transfers between devices: 12.1 us -> 9.21 us  [swap(): lax.ppermute(v, axis, [(i, i ^ mask) for i in range(lax.axis_size(axis))])]
    ppermute x2 -> x3, waiting for transfers between devices: 1.98 us -> 4.29 us  [over_side(): return lax.ppermute(line, COL, steps + [(b, a) for a, b in steps])]
    ppermute x1, starting transfers between devices: 1.03 us -> 2.17 us  [body(): far = lax.ppermute(following, ROW, wide)]
    ppermute x13, starting transfers between devices: 14.8 us -> 13.7 us  [swap(): lax.ppermute(v, axis, [(i, i ^ mask) for i in range(lax.axis_size(axis))])]
    ppermute x2 -> x3, starting transfers between devices: 1.85 us -> 2.43 us  [over_side(): return lax.ppermute(line, COL, steps + [(b, a) for a, b in steps])]
  transfers between devices with their start and end apart: 19 -> 20, of which waited for: 8 -> 10; matrix products, arithmetic and copies ran while one was open for 0% -> 0% of each run, Pallas kernels for 8% -> 8%
where the time goes in v4:
time: 61.1 us; the launch traced here: 61 us
  starting transfers between devices  34.2 us (56%)
  waiting for transfers between devices  15.9 us (26%)
  Pallas kernels  9.29 us (15%)
  between operations  1.48 us (2%)
    ppermute x13, starting transfers between devices, swap(): lax.ppermute(v, axis, [(i, i ^ mask) for i in range(lax.axis_size(axis))])  13.7 us
    pallas_call x5, Pallas kernels, placed(): return run(*operands[:smem + vmem], *held)  9.29 us
    ppermute x13, waiting for transfers between devices, swap(): lax.ppermute(v, axis, [(i, i ^ mask) for i in range(lax.axis_size(axis))])  9.21 us
    ppermute x1, starting transfers between devices, beside(): lax.ppermute(v, ROW, wide)  8.4 us
    ppermute x3, waiting for transfers between devices, over_side(): return lax.ppermute(line, COL, steps + [(b, a) for a, b in steps])  4.29 us
    ppermute x1, starting transfers between devices, body(): lax.ppermute(following, ROW, odd)  3.74 us
    ppermute x1, starting transfers between devices, beside(): lax.ppermute(v, ROW, odd)  3.71 us
    ppermute x3, starting transfers between devices, over_side(): return lax.ppermute(line, COL, steps + [(b, a) for a, b in steps])  2.43 us
  transfers between devices with their start and end apart: 20, of which 10 were waited for; matrix products, arithmetic and copies ran while one was open for 0% of the time, Pallas kernels for 8%

profile of v4, /device:TPU:8, one launch (start us, length us, event | category | flops | bytes accessed | tf_op | source)
XLA Modules:
  0.0 61.0 jit_solution(12412173607560368321)
XLA Ops:
  1.3 1.4 %shard_map.113 = (f32[8,2176]{1,0:T(8,128)S(1)}, f32[1,128]{1,0:T(1,128)S(1)}, f32[48,1920]{1,0:T(8,128)S(1)}) custom-call(s32[1]{0:T(128)S(6)} %copy.20.count_ref, f32[48,1920]{1,0:T(8,128)} %refs_0_.1, s32[1,48]{1,0:T(1,128)} %bitcast.39, s32[2,512]{1,0:T(2,128)} %bitcast.46, s32[1,512]{1,0:T(1,128)} %bitcast.47, f32[1,512]{1,0:T(1,128)} %bitcast.48, ...), custom_call_target="tpu_custom_call" | custom-call | tf_op jit(solution)/shard_map/pallas_call | solution.py:312
  2.7 8.4 %collective-permute-start.3 = (f32[8,2176]{1,0:T(8,128)S(1)}, f32[8,2176]{1,0:T(8,128)S(1)}, u32[]{:S(2)}, u32[]{:S(2)}) collective-permute-start(f32[8,2176]{1,0:T(8,128)S(1)} %get-tuple-element.17), channel_id=1, source_target_pairs={{2,4},{3,5},{6,8},{7,9},{10,12},{11,13},{14,16},{15,17},{18,20},{1... | collective-permute-start | bytes 208904 | tf_op jit(solution)/shard_map/ppermute | solution.py:336
  11.1 0.0 collective-permute-start.2
  11.1 3.7 %collective-permute-start.1 = (f32[8,2176]{1,0:T(8,128)S(1)}, f32[8,2176]{1,0:T(8,128)S(1)}, u32[]{:S(2)}, u32[]{:S(2)}) collective-permute-start(f32[8,2176]{1,0:T(8,128)S(1)} %get-tuple-element.17), channel_id=1, source_target_pairs={{1,2},{5,6},{9,10},{13,14},{17,18},{21,22},{25,26},{29,30},{3,4},{... | collective-permute-start | bytes 208904 | tf_op jit(solution)/shard_map/ppermute | solution.py:336
  14.8 0.0 collective-permute-start
  14.8 0.0 copy-start
  14.8 0.0 copy-start.1
  14.8 3.0 %shard_map.114 = (bf16[15,384,256]{2,1,0:T(8,128)(2,1)S(1)}, bf16[15,256,256]{2,1,0:T(8,128)(2,1)S(1)}, bf16[15,384,256]{2,1,0:T(8,128)(2,1)S(1)}) custom-call(f32[3,15,128,128]{3,2,1,0:T(8,128)} %rotation_any.1, f32[15,128,128]{2,1,0:T(8,128)} %translation_any.1), custom_call_target="tpu_custom_call" | custom-call | flops 3000000000 | tf_op jit(solution)/shard_map/pallas_call | solution.py:312
  17.9 0.0 collective-permute-done.3
  17.9 0.0 collective-permute-done.2
  17.9 0.1 collective-permute-start.5
  18.0 1.1 %collective-permute-done = f32[8,2176]{1,0:T(8,128)S(1)} collective-permute-done((f32[8,2176]{1,0:T(8,128)S(1)}, f32[8,2176]{1,0:T(8,128)S(1)}, u32[]{:S(2)}, u32[]{:S(2)}) %collective-permute-start) | collective-permute-done | bytes 69664 | tf_op jit(solution)/shard_map/ppermute | solution.py:322
  19.1 0.0 collective-permute-done.1
  19.1 0.7 %collective-permute-start.4 = (f32[5,8,2176]{2,1,0:T(8,128)S(1)}, f32[5,8,2176]{2,1,0:T(8,128)S(1)}, u32[]{:S(2)}, u32[]{:S(2)}) collective-permute-start(f32[5,8,2176]{2,1,0:T(8,128)S(1)} %constant_dynamic-update-slice_fusion.own_ref), channel_id=1, source_target_pairs={{0,32},{32,0},{1,33},{33,1},{2,34},{34,2},{3,35},{35,3},{4,36},{36... | collective-permute-start | bytes 1044488 | tf_op jit(solution)/shard_map/ppermute | solution.py:322
  19.9 0.6 collective-permute-start.6
  20.4 4.3 %collective-permute-done.6.close_ref = f32[2,8,2176]{2,1,0:T(8,128)S(1)} collective-permute-done((f32[2,8,2176]{2,1,0:T(8,128)S(1)}, f32[2,8,2176]{2,1,0:T(8,128)S(1)}, u32[]{:S(2)}, u32[]{:S(2)}) %collective-permute-start.6) | collective-permute-done | bytes 139296 | tf_op jit(solution)/shard_map/ppermute | solution.py:342
  24.7 0.0 collective-permute-done.5.wide_ref
  24.7 0.0 collective-permute-done.4.core_ref
  24.7 0.0 copy-done
  24.7 0.0 copy-done.1
  24.7 1.9 %shard_map.115 = (f32[48,120]{1,0:T(8,128)S(1)}, f32[8,1920]{1,0:T(8,128)S(1)}, f32[8,1920]{1,0:T(8,128)S(1)}, f32[8,128]{1,0:T(8,128)S(1)}) custom-call(f32[5,8,2176]{2,1,0:T(8,128)S(1)} %constant_dynamic-update-slice_fusion.own_ref, f32[5,8,2176]{2,1,0:T(8,128)S(1)} %collective-permute-done.4.core_ref, f32[3,8,2176]{2,1,0:T(8,128)S(1)} %collective-permute-done.5.wide_ref, ...), custom_call_target="tpu_custom_call" | custom-call | tf_op jit(solution)/shard_map/pallas_call | solution.py:312
  26.7 1.1 %collective-permute-start.7 = (f32[8,128]{1,0:T(8,128)S(1)}, f32[8,128]{1,0:T(8,128)S(1)}, u32[]{:S(2)}, u32[]{:S(2)}) collective-permute-start(f32[8,128]{1,0:T(8,128)S(1)} %get-tuple-element.24), channel_id=1, source_target_pairs={{0,4},{4,0},{8,12},{12,8},{16,20},{20,16},{24,28},{28,24},{1,5},{5... | collective-permute-start | bytes 12296 | tf_op jit(solution)/shard_map/ppermute | solution.py:322
  27.8 2.2 %collective-permute-start.11 = (f32[8,1920]{1,0:T(8,128)S(1)}, f32[8,1920]{1,0:T(8,128)S(1)}, u32[]{:S(2)}, u32[]{:S(2)}) collective-permute-start(f32[8,1920]{1,0:T(8,128)S(1)} %get-tuple-element.23), channel_id=1, source_target_pairs={{2,4},{3,5},{6,8},{7,9},{10,12},{11,13},{14,16},{15,17},{18,20},{1... | collective-permute-start | bytes 184328 | tf_op jit(solution)/shard_map/ppermute | solution.py:400
  29.9 0.5 collective-permute-done.7
  30.4 1.4 %collective-permute-start.10 = (f32[8,2048]{1,0:T(8,128)S(1)}, f32[8,2048]{1,0:T(8,128)S(1)}, u32[]{:S(2)}, u32[]{:S(2)}) collective-permute-start(f32[8,2048]{1,0:T(8,128)S(1)} %pad_maximum_fusion.2), channel_id=1, source_target_pairs={{0,2},{1,3},{2,0},{3,1},{4,6},{5,7},{6,4},{7,5},{8,10},{9,11},{10,... | collective-permute-start | bytes 196616 | tf_op jit(solution)/shard_map/ppermute | solution.py:322
  31.8 3.7 %collective-permute-start.9 = (f32[8,2048]{1,0:T(8,128)S(1)}, f32[8,2048]{1,0:T(8,128)S(1)}, u32[]{:S(2)}, u32[]{:S(2)}) collective-permute-start(f32[8,2048]{1,0:T(8,128)S(1)} %pad_maximum_fusion.2), channel_id=1, source_target_pairs={{1,2},{5,6},{9,10},{13,14},{17,18},{21,22},{25,26},{29,30},{3,4},{... | collective-permute-start | bytes 196616 | tf_op jit(solution)/shard_map/ppermute | solution.py:402
  35.6 0.0 collective-permute-start.8
  35.6 1.5 %collective-permute-done.10 = f32[8,2048]{1,0:T(8,128)S(1)} collective-permute-done((f32[8,2048]{1,0:T(8,128)S(1)}, f32[8,2048]{1,0:T(8,128)S(1)}, u32[]{:S(2)}, u32[]{:S(2)}) %collective-permute-start.10) | collective-permute-done | bytes 65568 | tf_op jit(solution)/shard_map/ppermute | solution.py:322
  37.1 2.4 %collective-permute-done.9 = f32[8,2048]{1,0:T(8,128)S(1)} collective-permute-done((f32[8,2048]{1,0:T(8,128)S(1)}, f32[8,2048]{1,0:T(8,128)S(1)}, u32[]{:S(2)}, u32[]{:S(2)}) %collective-permute-start.9) | collective-permute-done | bytes 65568 | tf_op jit(solution)/shard_map/ppermute | solution.py:402
  39.4 0.4 collective-permute-done.8
  39.9 0.0 collective-permute-done.11
  39.9 0.1 collective-permute-start.12
  40.0 1.8 %collective-permute-start.13 = (f32[5,8,1920]{2,1,0:T(8,128)S(1)}, f32[5,8,1920]{2,1,0:T(8,128)S(1)}, u32[]{:S(2)}, u32[]{:S(2)}) collective-permute-start(f32[5,8,1920]{2,1,0:T(8,128)S(1)} %bitcast_dynamic-update-slice_fusion.own_ref), channel_id=1, source_target_pairs={{32,64},{96,128},{160,192},{224,0},{64,32},{128,96},{192,160},{0,2... | collective-permute-start | bytes 921608 | tf_op jit(solution)/shard_map/ppermute | solution.py:342
  41.8 0.0 collective-permute-done.12.core_ref
  41.8 2.5 %collective-permute-start.16 = (f32[8,128]{1,0:T(8,128)S(1)}, f32[8,128]{1,0:T(8,128)S(1)}, u32[]{:S(2)}, u32[]{:S(2)}) collective-permute-start(f32[8,128]{1,0:T(8,128)S(1)} %slice_add_fusion), channel_id=1, source_target_pairs={{0,16},{4,20},{8,24},{12,28},{16,0},{20,4},{24,8},{28,12},{1,17},{... | collective-permute-start | bytes 12296 | tf_op jit(solution)/shard_map/ppermute | solution.py:322
  44.3 2.6 %collective-permute-start.15 = (f32[8,128]{1,0:T(8,128)S(1)}, f32[8,128]{1,0:T(8,128)S(1)}, u32[]{:S(2)}, u32[]{:S(2)}) collective-permute-start(f32[8,128]{1,0:T(8,128)S(1)} %slice_add_fusion), channel_id=1, source_target_pairs={{0,24},{4,28},{8,16},{12,20},{16,8},{20,12},{24,0},{28,4},{1,25},{... | collective-permute-start | bytes 12296 | tf_op jit(solution)/shard_map/ppermute | solution.py:322
  46.9 1.5 %collective-permute-start.14 = (f32[8,128]{1,0:T(8,128)S(1)}, f32[8,128]{1,0:T(8,128)S(1)}, u32[]{:S(2)}, u32[]{:S(2)}) collective-permute-start(f32[8,128]{1,0:T(8,128)S(1)} %slice_add_fusion), channel_id=1, source_target_pairs={{0,8},{4,12},{8,0},{12,4},{16,24},{20,28},{24,16},{28,20},{1,9},{5... | collective-permute-start | bytes 12296 | tf_op jit(solution)/shard_map/ppermute | solution.py:322
  48.3 1.0 %collective-permute-done.16 = f32[8,128]{1,0:T(8,128)S(1)} collective-permute-done((f32[8,128]{1,0:T(8,128)S(1)}, f32[8,128]{1,0:T(8,128)S(1)}, u32[]{:S(2)}, u32[]{:S(2)}) %collective-permute-start.16) | collective-permute-done | bytes 4128 | tf_op jit(solution)/shard_map/ppermute | solution.py:322
  49.4 0.7 %collective-permute-done.15 = f32[8,128]{1,0:T(8,128)S(1)} collective-permute-done((f32[8,128]{1,0:T(8,128)S(1)}, f32[8,128]{1,0:T(8,128)S(1)}, u32[]{:S(2)}, u32[]{:S(2)}) %collective-permute-start.15) | collective-permute-done | bytes 4128 | tf_op jit(solution)/shard_map/ppermute | solution.py:322
  50.0 1.3 %collective-permute-done.14 = f32[8,128]{1,0:T(8,128)S(1)} collective-permute-done((f32[8,128]{1,0:T(8,128)S(1)}, f32[8,128]{1,0:T(8,128)S(1)}, u32[]{:S(2)}, u32[]{:S(2)}) %collective-permute-start.14) | collective-permute-done | bytes 4128 | tf_op jit(solution)/shard_map/ppermute | solution.py:322
  51.4 1.5 %collective-permute-start.19 = (f32[8,128]{1,0:T(8,128)S(1)}, f32[8,128]{1,0:T(8,128)S(1)}, u32[]{:S(2)}, u32[]{:S(2)}) collective-permute-start(f32[8,128]{1,0:T(8,128)S(1)} %add_add_fusion.1), channel_id=1, source_target_pairs={{0,192},{64,128},{128,64},{192,0},{1,193},{65,129},{129,65},{193,1... | collective-permute-start | bytes 12296 | tf_op jit(solution)/shard_map/ppermute | solution.py:322
  52.9 1.9 %collective-permute-start.18 = (f32[8,128]{1,0:T(8,128)S(1)}, f32[8,128]{1,0:T(8,128)S(1)}, u32[]{:S(2)}, u32[]{:S(2)}) collective-permute-start(f32[8,128]{1,0:T(8,128)S(1)} %add_add_fusion.1), channel_id=1, source_target_pairs={{0,64},{64,0},{128,192},{192,128},{1,65},{65,1},{129,193},{193,129... | collective-permute-start | bytes 12296 | tf_op jit(solution)/shard_map/ppermute | solution.py:322
  54.7 0.5 collective-permute-start.17
  55.2 0.0 collective-permute-done.13.side_ref
  55.3 1.9 %shard_map.116 = (f32[48,1920]{1,0:T(8,128)S(1)}, f32[48,1920]{1,0:T(8,128)S(1)}) custom-call(f32[5,8,1920]{2,1,0:T(8,128)S(1)} %bitcast_dynamic-update-slice_fusion.own_ref, f32[48,1920]{1,0:T(8,128)S(1)} %collective-permute-done.12.core_ref, f32[5,8,1920]{2,1,0:T(8,128)S(1)} %collective-permute-done.13.side_ref, ...), custom_call_target="tpu_custom_call" | custom-call | flops 5000000000 | tf_op jit(solution)/shard_map/pallas_call | solution.py:312
  57.1 0.0 collective-permute-done.19
  57.1 0.0 collective-permute-done.18
  57.1 2.7 %collective-permute-done.17 = f32[8,128]{1,0:T(8,128)S(1)} collective-permute-done((f32[8,128]{1,0:T(8,128)S(1)}, f32[8,128]{1,0:T(8,128)S(1)}, u32[]{:S(2)}, u32[]{:S(2)}) %collective-permute-start.17) | collective-permute-done | bytes 4128 | tf_op jit(solution)/shard_map/ppermute | solution.py:322
  59.9 1.1 %shard_map.117 = (f32[48,1920]{1,0:T(8,128)}, f32[48,1920]{1,0:T(8,128)}) custom-call(f32[48,1920]{1,0:T(8,128)S(1)} %get-tuple-element.16.rhs_ref, f32[48,1920]{1,0:T(8,128)S(1)} %get-tuple-element.28.first_ref, f32[48,1920]{1,0:T(8,128)S(1)} %get-tuple-element.29.second_ref, f32[8,128]{1,0:T(8,128)S(1)} %add_add_fusion.sums_ref), custom_call_target="tpu_custom_call" | custom-call | tf_op jit(solution)/shard_map/pallas_call | solution.py:312
  (19 shorter events, 0.2 us)
Async XLA Ops:
  2.7 15.2 %collective-permute-start.3 = (f32[8,2176]{1,0:T(8,128)S(1)}, f32[8,2176]{1,0:T(8,128)S(1)}, u32[]{:S(2)}, u32[]{:S(2)}) collective-permute-start(f32[8,2176]{1,0:T(8,128)S(1)} %get-tuple-element.17), channel_id=1, source_target_pairs={{2,4},{3,5},{6,8},{7,9},{10,12},{11,13},{14,16},{15,17},{18,20},{1... | collective-permute-start | bytes 208904 | tf_op jit(solution)/shard_map/ppermute | solution.py:336
  11.1 6.8 %collective-permute-start.2 = (f32[8,2176]{1,0:T(8,128)S(1)}, f32[8,2176]{1,0:T(8,128)S(1)}, u32[]{:S(2)}, u32[]{:S(2)}) collective-permute-start(f32[8,2176]{1,0:T(8,128)S(1)} %get-tuple-element.17), channel_id=1, source_target_pairs={{0,2},{1,3},{2,0},{3,1},{4,6},{5,7},{6,4},{7,5},{8,10},{9,11},{10,... | collective-permute-start | bytes 208904 | tf_op jit(solution)/shard_map/ppermute | solution.py:322
  11.1 8.0 %collective-permute-start.1 = (f32[8,2176]{1,0:T(8,128)S(1)}, f32[8,2176]{1,0:T(8,128)S(1)}, u32[]{:S(2)}, u32[]{:S(2)}) collective-permute-start(f32[8,2176]{1,0:T(8,128)S(1)} %get-tuple-element.17), channel_id=1, source_target_pairs={{1,2},{5,6},{9,10},{13,14},{17,18},{21,22},{25,26},{29,30},{3,4},{... | collective-permute-start | bytes 208904 | tf_op jit(solution)/shard_map/ppermute | solution.py:336
  14.8 4.3 %collective-permute-start = (f32[8,2176]{1,0:T(8,128)S(1)}, f32[8,2176]{1,0:T(8,128)S(1)}, u32[]{:S(2)}, u32[]{:S(2)}) collective-permute-start(f32[8,2176]{1,0:T(8,128)S(1)} %get-tuple-element.17), channel_id=1, source_target_pairs={{0,1},{1,0},{2,3},{3,2},{4,5},{5,4},{6,7},{7,6},{8,9},{9,8},{10,11... | collective-permute-start | bytes 208904 | tf_op jit(solution)/shard_map/ppermute | solution.py:322
  14.8 9.9 %copy-start = (f32[1920]{0:T(1024)S(1)}, f32[1920]{0:T(1024)}, u32[]{:S(2)}) copy-start(f32[1920]{0:T(1024)} %param.19) | copy-start | bytes 23044
  14.8 9.9 %copy-start.1 = (s32[48]{0:T(128)S(1)}, s32[48]{0:T(128)}, u32[]{:S(2)}) copy-start(s32[48]{0:T(128)} %param.11) | copy-start | bytes 580
  17.9 6.8 %collective-permute-start.5 = (f32[3,8,2176]{2,1,0:T(8,128)S(1)}, f32[3,8,2176]{2,1,0:T(8,128)S(1)}, u32[]{:S(2)}, u32[]{:S(2)}) collective-permute-start(f32[3,8,2176]{2,1,0:T(8,128)S(1)} %pad_maximum_fusion), channel_id=1, source_target_pairs={{32,64},{96,128},{160,192},{224,0},{64,32},{128,96},{192,160},{0,2... | collective-permute-start | bytes 626696 | tf_op jit(solution)/shard_map/ppermute | solution.py:342
  19.1 5.6 %collective-permute-start.4 = (f32[5,8,2176]{2,1,0:T(8,128)S(1)}, f32[5,8,2176]{2,1,0:T(8,128)S(1)}, u32[]{:S(2)}, u32[]{:S(2)}) collective-permute-start(f32[5,8,2176]{2,1,0:T(8,128)S(1)} %constant_dynamic-update-slice_fusion.own_ref), channel_id=1, source_target_pairs={{0,32},{32,0},{1,33},{33,1},{2,34},{34,2},{3,35},{35,3},{4,36},{36... | collective-permute-start | bytes 1044488 | tf_op jit(solution)/shard_map/ppermute | solution.py:322
  19.9 4.9 %collective-permute-start.6 = (f32[2,8,2176]{2,1,0:T(8,128)S(1)}, f32[2,8,2176]{2,1,0:T(8,128)S(1)}, u32[]{:S(2)}, u32[]{:S(2)}) collective-permute-start(f32[2,8,2176]{2,1,0:T(8,128)S(1)} %pad_maximum_fusion.1), channel_id=1, source_target_pairs={{32,64},{96,128},{160,192},{224,0},{64,32},{128,96},{192,160},{0,2... | collective-permute-start | bytes 417800 | tf_op jit(solution)/shard_map/ppermute | solution.py:342
  26.7 3.7 %collective-permute-start.7 = (f32[8,128]{1,0:T(8,128)S(1)}, f32[8,128]{1,0:T(8,128)S(1)}, u32[]{:S(2)}, u32[]{:S(2)}) collective-permute-start(f32[8,128]{1,0:T(8,128)S(1)} %get-tuple-element.24), channel_id=1, source_target_pairs={{0,4},{4,0},{8,12},{12,8},{16,20},{20,16},{24,28},{28,24},{1,5},{5... | collective-permute-start | bytes 12296 | tf_op jit(solution)/shard_map/ppermute | solution.py:322
  27.8 12.1 %collective-permute-start.11 = (f32[8,1920]{1,0:T(8,128)S(1)}, f32[8,1920]{1,0:T(8,128)S(1)}, u32[]{:S(2)}, u32[]{:S(2)}) collective-permute-start(f32[8,1920]{1,0:T(8,128)S(1)} %get-tuple-element.23), channel_id=1, source_target_pairs={{2,4},{3,5},{6,8},{7,9},{10,12},{11,13},{14,16},{15,17},{18,20},{1... | collective-permute-start | bytes 184328 | tf_op jit(solution)/shard_map/ppermute | solution.py:400
  30.4 6.7 %collective-permute-start.10 = (f32[8,2048]{1,0:T(8,128)S(1)}, f32[8,2048]{1,0:T(8,128)S(1)}, u32[]{:S(2)}, u32[]{:S(2)}) collective-permute-start(f32[8,2048]{1,0:T(8,128)S(1)} %pad_maximum_fusion.2), channel_id=1, source_target_pairs={{0,2},{1,3},{2,0},{3,1},{4,6},{5,7},{6,4},{7,5},{8,10},{9,11},{10,... | collective-permute-start | bytes 196616 | tf_op jit(solution)/shard_map/ppermute | solution.py:322
  31.8 7.6 %collective-permute-start.9 = (f32[8,2048]{1,0:T(8,128)S(1)}, f32[8,2048]{1,0:T(8,128)S(1)}, u32[]{:S(2)}, u32[]{:S(2)}) collective-permute-start(f32[8,2048]{1,0:T(8,128)S(1)} %pad_maximum_fusion.2), channel_id=1, source_target_pairs={{1,2},{5,6},{9,10},{13,14},{17,18},{21,22},{25,26},{29,30},{3,4},{... | collective-permute-start | bytes 196616 | tf_op jit(solution)/shard_map/ppermute | solution.py:402
  35.6 4.3 %collective-permute-start.8 = (f32[8,2048]{1,0:T(8,128)S(1)}, f32[8,2048]{1,0:T(8,128)S(1)}, u32[]{:S(2)}, u32[]{:S(2)}) collective-permute-start(f32[8,2048]{1,0:T(8,128)S(1)} %pad_maximum_fusion.2), channel_id=1, source_target_pairs={{0,1},{1,0},{2,3},{3,2},{4,5},{5,4},{6,7},{7,6},{8,9},{9,8},{10,11... | collective-permute-start | bytes 196616 | tf_op jit(solution)/shard_map/ppermute | solution.py:322
  39.9 1.9 %collective-permute-start.12 = (f32[48,1920]{1,0:T(8,128)S(1)}, f32[48,1920]{1,0:T(8,128)S(1)}, u32[]{:S(2)}, u32[]{:S(2)}) collective-permute-start(f32[48,1920]{1,0:T(8,128)S(1)} %select_maximum_fusion), channel_id=1, source_target_pairs={{0,32},{32,0},{1,33},{33,1},{2,34},{34,2},{3,35},{35,3},{4,36},{36... | collective-permute-start | bytes 1105928 | tf_op jit(solution)/shard_map/ppermute | solution.py:322
  40.0 15.2 %collective-permute-start.13 = (f32[5,8,1920]{2,1,0:T(8,128)S(1)}, f32[5,8,1920]{2,1,0:T(8,128)S(1)}, u32[]{:S(2)}, u32[]{:S(2)}) collective-permute-start(f32[5,8,1920]{2,1,0:T(8,128)S(1)} %bitcast_dynamic-update-slice_fusion.own_ref), channel_id=1, source_target_pairs={{32,64},{96,128},{160,192},{224,0},{64,32},{128,96},{192,160},{0,2... | collective-permute-start | bytes 921608 | tf_op jit(solution)/shard_map/ppermute | solution.py:342
  41.8 7.5 %collective-permute-start.16 = (f32[8,128]{1,0:T(8,128)S(1)}, f32[8,128]{1,0:T(8,128)S(1)}, u32[]{:S(2)}, u32[]{:S(2)}) collective-permute-start(f32[8,128]{1,0:T(8,128)S(1)} %slice_add_fusion), channel_id=1, source_target_pairs={{0,16},{4,20},{8,24},{12,28},{16,0},{20,4},{24,8},{28,12},{1,17},{... | collective-permute-start | bytes 12296 | tf_op jit(solution)/shard_map/ppermute | solution.py:322
  44.3 5.7 %collective-permute-start.15 = (f32[8,128]{1,0:T(8,128)S(1)}, f32[8,128]{1,0:T(8,128)S(1)}, u32[]{:S(2)}, u32[]{:S(2)}) collective-permute-start(f32[8,128]{1,0:T(8,128)S(1)} %slice_add_fusion), channel_id=1, source_target_pairs={{0,24},{4,28},{8,16},{12,20},{16,8},{20,12},{24,0},{28,4},{1,25},{... | collective-permute-start | bytes 12296 | tf_op jit(solution)/shard_map/ppermute | solution.py:322
  46.9 4.5 %collective-permute-start.14 = (f32[8,128]{1,0:T(8,128)S(1)}, f32[8,128]{1,0:T(8,128)S(1)}, u32[]{:S(2)}, u32[]{:S(2)}) collective-permute-start(f32[8,128]{1,0:T(8,128)S(1)} %slice_add_fusion), channel_id=1, source_target_pairs={{0,8},{4,12},{8,0},{12,4},{16,24},{20,28},{24,16},{28,20},{1,9},{5... | collective-permute-start | bytes 12296 | tf_op jit(solution)/shard_map/ppermute | solution.py:322
  51.4 5.8 %collective-permute-start.19 = (f32[8,128]{1,0:T(8,128)S(1)}, f32[8,128]{1,0:T(8,128)S(1)}, u32[]{:S(2)}, u32[]{:S(2)}) collective-permute-start(f32[8,128]{1,0:T(8,128)S(1)} %add_add_fusion.1), channel_id=1, source_target_pairs={{0,192},{64,128},{128,64},{192,0},{1,193},{65,129},{129,65},{193,1... | collective-permute-start | bytes 12296 | tf_op jit(solution)/shard_map/ppermute | solution.py:322
  52.9 4.3 %collective-permute-start.18 = (f32[8,128]{1,0:T(8,128)S(1)}, f32[8,128]{1,0:T(8,128)S(1)}, u32[]{:S(2)}, u32[]{:S(2)}) collective-permute-start(f32[8,128]{1,0:T(8,128)S(1)} %add_add_fusion.1), channel_id=1, source_target_pairs={{0,64},{64,0},{128,192},{192,128},{1,65},{65,1},{129,193},{193,129... | collective-permute-start | bytes 12296 | tf_op jit(solution)/shard_map/ppermute | solution.py:322
  54.7 5.1 %collective-permute-start.17 = (f32[8,128]{1,0:T(8,128)S(1)}, f32[8,128]{1,0:T(8,128)S(1)}, u32[]{:S(2)}, u32[]{:S(2)}) collective-permute-start(f32[8,128]{1,0:T(8,128)S(1)} %add_add_fusion.1), channel_id=1, source_target_pairs={{0,128},{64,192},{128,0},{192,64},{1,129},{65,193},{129,1},{193,65... | collective-permute-start | bytes 12296 | tf_op jit(solution)/shard_map/ppermute | solution.py:322

commit v5 on v3

--- a/solution.py
+++ b/solution.py
@@ -89,18 +89,10 @@
     copies = [pltpu.make_async_copy(a, b, sem.at[i]) for i, (a, b) in enumerate(zip(sources, targets))]
     for copy in copies:
         copy.start()
-    for copy in copies:
+    for copy in copies[1:]:
         copy.wait()
     spheres = rhs_ref.shape[0]
     pairs = dir_ref.shape[1]
-    rhs = rhs_ref[...]
-    member = (sublanes((K, spheres)) == member_ref[...]).astype(F32)
-    out_ref[:, :C] = hot_times(member, rhs)
-    squares = jnp.sum(rhs * rhs, axis=0, keepdims=True)
-    partial = squares[:, :W]
-    for g in range(1, NB):
-        partial = partial + squares[:, g * W : (g + 1) * W]
-    square_ref[...] = partial
     weight = jnp.where(lanes((1, pairs)) < count_ref[0], reach_ref[...], 0.0)
     own = ends_ref[0:1, :]
     near = ends_ref[1:2, :]
@@ -121,6 +113,15 @@
         names = names + pltpu.roll(row, 64 + K + NPEER * slot, 1)
     out_ref[:, C : C + W] = jnp.where(lane < 64, blocks[0], blocks[1])
     out_ref[:, C + W :] = jnp.where(lane < 64, blocks[2], names)
+    copies[0].wait()
+    rhs = rhs_ref[...]
+    member = (sublanes((K, spheres)) == member_ref[...]).astype(F32)
+    out_ref[:, :C] = hot_times(member, rhs)
+    squares = jnp.sum(rhs * rhs, axis=0, keepdims=True)
+    partial = squares[:, :W]
+    for g in range(1, NB):
+        partial = partial + squares[:, g * W : (g + 1) * W]
+    square_ref[...] = partial
 
 
 def pair_matrix(units):

time: 60.6 us -> 60.6 us (level)
  no operation moved by 1% of the time
where the time goes in v5:
time: 60.6 us; the launch traced here: 60.5 us
  starting transfers between devices  33.1 us (55%)
  waiting for transfers between devices  16.5 us (27%)
  Pallas kernels  9.26 us (15%)
  between operations  1.47 us (2%)
    ppermute x13, starting transfers between devices, swap(): lax.ppermute(v, axis, [(i, i ^ mask) for i in range(lax.axis_size(axis))])  14.8 us
    ppermute x13, waiting for transfers between devices, swap(): lax.ppermute(v, axis, [(i, i ^ mask) for i in range(lax.axis_size(axis))])  12.1 us
    pallas_call x5, Pallas kernels, placed(): return run(*operands[:smem + vmem], *held)  9.26 us
    ppermute x1, starting transfers between devices, beside(): lax.ppermute(v, ROW, wide)  8.4 us
    ppermute x1, starting transfers between devices, beside(): lax.ppermute(v, ROW, odd)  3.7 us
    ppermute x1, starting transfers between devices, body(): lax.ppermute(following, ROW, odd)  3.29 us
    ppermute x1, waiting for transfers between devices, body(): lax.ppermute(following, ROW, odd)  2.42 us
    ppermute x2, waiting for transfers between devices, over_side(): return lax.ppermute(line, COL, steps + [(b, a) for a, b in steps])  1.98 us
  transfers between devices with their start and end apart: 19, of which 8 were waited for; matrix products, arithmetic and copies ran while one was open for 0% of the time, Pallas kernels for 8%

profile of v5, /device:TPU:8, one launch (start us, length us, event | category | flops | bytes accessed | tf_op | source)
XLA Modules:
  0.0 60.5 jit_solution(2975044509117255274)
XLA Ops:
  1.3 1.4 %shard_map.113 = (f32[8,2176]{1,0:T(8,128)S(1)}, f32[1,128]{1,0:T(1,128)S(1)}, f32[48,1920]{1,0:T(8,128)S(1)}) custom-call(s32[1]{0:T(128)S(6)} %copy.20.count_ref, f32[48,1920]{1,0:T(8,128)} %refs_0_.1, s32[1,48]{1,0:T(1,128)} %bitcast.38, s32[2,512]{1,0:T(2,128)} %bitcast.41, s32[1,512]{1,0:T(1,128)} %bitcast.42, f32[1,512]{1,0:T(1,128)} %bitcast.43, ...), custom_call_target="tpu_custom_call" | custom-call | tf_op jit(solution)/shard_map/pallas_call | solution.py:312
  2.7 8.4 %collective-permute-start.3 = (f32[8,2176]{1,0:T(8,128)S(1)}, f32[8,2176]{1,0:T(8,128)S(1)}, u32[]{:S(2)}, u32[]{:S(2)}) collective-permute-start(f32[8,2176]{1,0:T(8,128)S(1)} %get-tuple-element.16), channel_id=1, source_target_pairs={{2,4},{3,5},{6,8},{7,9},{10,12},{11,13},{14,16},{15,17},{18,20},{1... | collective-permute-start | bytes 208904 | tf_op jit(solution)/shard_map/ppermute | solution.py:336
  11.1 0.0 collective-permute-start.2
  11.1 3.7 %collective-permute-start.1 = (f32[8,2176]{1,0:T(8,128)S(1)}, f32[8,2176]{1,0:T(8,128)S(1)}, u32[]{:S(2)}, u32[]{:S(2)}) collective-permute-start(f32[8,2176]{1,0:T(8,128)S(1)} %get-tuple-element.16), channel_id=1, source_target_pairs={{1,2},{5,6},{9,10},{13,14},{17,18},{21,22},{25,26},{29,30},{3,4},{... | collective-permute-start | bytes 208904 | tf_op jit(solution)/shard_map/ppermute | solution.py:336
  14.8 0.0 collective-permute-start
  14.8 4.3 %collective-permute-done = f32[8,2176]{1,0:T(8,128)S(1)} collective-permute-done((f32[8,2176]{1,0:T(8,128)S(1)}, f32[8,2176]{1,0:T(8,128)S(1)}, u32[]{:S(2)}, u32[]{:S(2)}) %collective-permute-start) | collective-permute-done | bytes 69664 | tf_op jit(solution)/shard_map/ppermute | solution.py:322
  19.1 0.0 collective-permute-done.1
  19.1 0.0 collective-permute-done.2
  19.1 0.0 collective-permute-done.3
  19.2 0.0 copy-start
  19.2 0.0 copy-start.1
  19.2 0.1 collective-permute-start.5
  19.3 1.7 %collective-permute-start.4 = (f32[5,8,2176]{2,1,0:T(8,128)S(1)}, f32[5,8,2176]{2,1,0:T(8,128)S(1)}, u32[]{:S(2)}, u32[]{:S(2)}) collective-permute-start(f32[5,8,2176]{2,1,0:T(8,128)S(1)} %bitcast_dynamic-update-slice_fusion.own_ref), channel_id=1, source_target_pairs={{0,32},{32,0},{1,33},{33,1},{2,34},{34,2},{3,35},{35,3},{4,36},{36... | collective-permute-start | bytes 1044488 | tf_op jit(solution)/shard_map/ppermute | solution.py:322
  21.0 3.0 %shard_map.114 = (bf16[15,384,256]{2,1,0:T(8,128)(2,1)S(1)}, bf16[15,256,256]{2,1,0:T(8,128)(2,1)S(1)}, bf16[15,384,256]{2,1,0:T(8,128)(2,1)S(1)}) custom-call(f32[3,15,128,128]{3,2,1,0:T(8,128)} %rotation_any.1, f32[15,128,128]{2,1,0:T(8,128)} %translation_any.1), custom_call_target="tpu_custom_call" | custom-call | flops 3000000000 | tf_op jit(solution)/shard_map/pallas_call | solution.py:312
  24.0 2.0 %collective-permute-done.5.side_ref = f32[5,8,2176]{2,1,0:T(8,128)S(1)} collective-permute-done((f32[5,8,2176]{2,1,0:T(8,128)S(1)}, f32[5,8,2176]{2,1,0:T(8,128)S(1)}, u32[]{:S(2)}, u32[]{:S(2)}) %collective-permute-start.5) | collective-permute-done | bytes 348192 | tf_op jit(solution)/shard_map/ppermute | solution.py:342
  26.0 0.0 collective-permute-done.4.core_ref
  26.0 0.0 copy-done
  26.0 0.0 copy-done.1
  26.0 1.9 %shard_map.115 = (f32[48,120]{1,0:T(8,128)S(1)}, f32[8,1920]{1,0:T(8,128)S(1)}, f32[8,1920]{1,0:T(8,128)S(1)}, f32[8,128]{1,0:T(8,128)S(1)}) custom-call(f32[5,8,2176]{2,1,0:T(8,128)S(1)} %bitcast_dynamic-update-slice_fusion.own_ref, f32[5,8,2176]{2,1,0:T(8,128)S(1)} %collective-permute-done.4.core_ref, f32[5,8,2176]{2,1,0:T(8,128)S(1)} %collective-permute-done.5.side_ref, ...), custom_call_target="tpu_custom_call" | custom-call | tf_op jit(solution)/shard_map/pallas_call | solution.py:312
  27.9 1.1 %collective-permute-start.6 = (f32[8,128]{1,0:T(8,128)S(1)}, f32[8,128]{1,0:T(8,128)S(1)}, u32[]{:S(2)}, u32[]{:S(2)}) collective-permute-start(f32[8,128]{1,0:T(8,128)S(1)} %get-tuple-element.22), channel_id=1, source_target_pairs={{0,4},{4,0},{8,12},{12,8},{16,20},{20,16},{24,28},{28,24},{1,5},{5... | collective-permute-start | bytes 12296 | tf_op jit(solution)/shard_map/ppermute | solution.py:322
  29.0 1.0 %collective-permute-start.10 = (f32[8,1920]{1,0:T(8,128)S(1)}, f32[8,1920]{1,0:T(8,128)S(1)}, u32[]{:S(2)}, u32[]{:S(2)}) collective-permute-start(f32[8,1920]{1,0:T(8,128)S(1)} %get-tuple-element.21), channel_id=1, source_target_pairs={{2,4},{3,5},{6,8},{7,9},{10,12},{11,13},{14,16},{15,17},{18,20},{1... | collective-permute-start | bytes 184328 | tf_op jit(solution)/shard_map/ppermute | solution.py:397
  30.0 1.6 %collective-permute-done.6 = f32[8,128]{1,0:T(8,128)S(1)} collective-permute-done((f32[8,128]{1,0:T(8,128)S(1)}, f32[8,128]{1,0:T(8,128)S(1)}, u32[]{:S(2)}, u32[]{:S(2)}) %collective-permute-start.6) | collective-permute-done | bytes 4128 | tf_op jit(solution)/shard_map/ppermute | solution.py:322
  31.6 1.5 %collective-permute-start.9 = (f32[8,2048]{1,0:T(8,128)S(1)}, f32[8,2048]{1,0:T(8,128)S(1)}, u32[]{:S(2)}, u32[]{:S(2)}) collective-permute-start(f32[8,2048]{1,0:T(8,128)S(1)} %pad_maximum_fusion), channel_id=1, source_target_pairs={{0,2},{1,3},{2,0},{3,1},{4,6},{5,7},{6,4},{7,5},{8,10},{9,11},{10,... | collective-permute-start | bytes 196616 | tf_op jit(solution)/shard_map/ppermute | solution.py:322
  33.1 3.3 %collective-permute-start.8 = (f32[8,2048]{1,0:T(8,128)S(1)}, f32[8,2048]{1,0:T(8,128)S(1)}, u32[]{:S(2)}, u32[]{:S(2)}) collective-permute-start(f32[8,2048]{1,0:T(8,128)S(1)} %pad_maximum_fusion), channel_id=1, source_target_pairs={{1,2},{5,6},{9,10},{13,14},{17,18},{21,22},{25,26},{29,30},{3,4},{... | collective-permute-start | bytes 196616 | tf_op jit(solution)/shard_map/ppermute | solution.py:399
  36.4 0.0 collective-permute-start.7
  36.4 1.9 %collective-permute-done.9 = f32[8,2048]{1,0:T(8,128)S(1)} collective-permute-done((f32[8,2048]{1,0:T(8,128)S(1)}, f32[8,2048]{1,0:T(8,128)S(1)}, u32[]{:S(2)}, u32[]{:S(2)}) %collective-permute-start.9) | collective-permute-done | bytes 65568 | tf_op jit(solution)/shard_map/ppermute | solution.py:322
  38.3 2.4 %collective-permute-done.8 = f32[8,2048]{1,0:T(8,128)S(1)} collective-permute-done((f32[8,2048]{1,0:T(8,128)S(1)}, f32[8,2048]{1,0:T(8,128)S(1)}, u32[]{:S(2)}, u32[]{:S(2)}) %collective-permute-start.8) | collective-permute-done | bytes 65568 | tf_op jit(solution)/shard_map/ppermute | solution.py:399
  40.7 0.0 collective-permute-done.7
  40.7 0.0 collective-permute-done.10
  40.8 0.1 collective-permute-start.11
  40.9 1.8 %collective-permute-start.12 = (f32[5,8,1920]{2,1,0:T(8,128)S(1)}, f32[5,8,1920]{2,1,0:T(8,128)S(1)}, u32[]{:S(2)}, u32[]{:S(2)}) collective-permute-start(f32[5,8,1920]{2,1,0:T(8,128)S(1)} %bitcast_dynamic-update-slice_fusion.5.own_ref), channel_id=1, source_target_pairs={{32,64},{96,128},{160,192},{224,0},{64,32},{128,96},{192,160},{0,2... | collective-permute-start | bytes 921608 | tf_op jit(solution)/shard_map/ppermute | solution.py:342
  42.6 0.0 collective-permute-done.11.core_ref
  42.7 2.4 %collective-permute-start.15 = (f32[8,128]{1,0:T(8,128)S(1)}, f32[8,128]{1,0:T(8,128)S(1)}, u32[]{:S(2)}, u32[]{:S(2)}) collective-permute-start(f32[8,128]{1,0:T(8,128)S(1)} %slice_add_fusion), channel_id=1, source_target_pairs={{0,16},{4,20},{8,24},{12,28},{16,0},{20,4},{24,8},{28,12},{1,17},{... | collective-permute-start | bytes 12296 | tf_op jit(solution)/shard_map/ppermute | solution.py:322
  45.1 1.0 %collective-permute-start.14 = (f32[8,128]{1,0:T(8,128)S(1)}, f32[8,128]{1,0:T(8,128)S(1)}, u32[]{:S(2)}, u32[]{:S(2)}) collective-permute-start(f32[8,128]{1,0:T(8,128)S(1)} %slice_add_fusion), channel_id=1, source_target_pairs={{0,24},{4,28},{8,16},{12,20},{16,8},{20,12},{24,0},{28,4},{1,25},{... | collective-permute-start | bytes 12296 | tf_op jit(solution)/shard_map/ppermute | solution.py:322
  46.1 3.1 %collective-permute-start.13 = (f32[8,128]{1,0:T(8,128)S(1)}, f32[8,128]{1,0:T(8,128)S(1)}, u32[]{:S(2)}, u32[]{:S(2)}) collective-permute-start(f32[8,128]{1,0:T(8,128)S(1)} %slice_add_fusion), channel_id=1, source_target_pairs={{0,8},{4,12},{8,0},{12,4},{16,24},{20,28},{24,16},{28,20},{1,9},{5... | collective-permute-start | bytes 12296 | tf_op jit(solution)/shard_map/ppermute | solution.py:322
  49.2 1.0 %collective-permute-done.15 = f32[8,128]{1,0:T(8,128)S(1)} collective-permute-done((f32[8,128]{1,0:T(8,128)S(1)}, f32[8,128]{1,0:T(8,128)S(1)}, u32[]{:S(2)}, u32[]{:S(2)}) %collective-permute-start.15) | collective-permute-done | bytes 4128 | tf_op jit(solution)/shard_map/ppermute | solution.py:322
  50.2 0.6 %collective-permute-done.14 = f32[8,128]{1,0:T(8,128)S(1)} collective-permute-done((f32[8,128]{1,0:T(8,128)S(1)}, f32[8,128]{1,0:T(8,128)S(1)}, u32[]{:S(2)}, u32[]{:S(2)}) %collective-permute-start.14) | collective-permute-done | bytes 4128 | tf_op jit(solution)/shard_map/ppermute | solution.py:322
  50.8 0.0 collective-permute-done.13
  50.8 1.6 %collective-permute-start.18 = (f32[8,128]{1,0:T(8,128)S(1)}, f32[8,128]{1,0:T(8,128)S(1)}, u32[]{:S(2)}, u32[]{:S(2)}) collective-permute-start(f32[8,128]{1,0:T(8,128)S(1)} %add_add_fusion.1), channel_id=1, source_target_pairs={{0,192},{64,128},{128,64},{192,0},{1,193},{65,129},{129,65},{193,1... | collective-permute-start | bytes 12296 | tf_op jit(solution)/shard_map/ppermute | solution.py:322
  52.4 1.9 %collective-permute-start.17 = (f32[8,128]{1,0:T(8,128)S(1)}, f32[8,128]{1,0:T(8,128)S(1)}, u32[]{:S(2)}, u32[]{:S(2)}) collective-permute-start(f32[8,128]{1,0:T(8,128)S(1)} %add_add_fusion.1), channel_id=1, source_target_pairs={{0,64},{64,0},{128,192},{192,128},{1,65},{65,1},{129,193},{193,129... | collective-permute-start | bytes 12296 | tf_op jit(solution)/shard_map/ppermute | solution.py:322
  54.3 0.5 collective-permute-start.16
  54.8 0.0 collective-permute-done.12.side_ref
  54.8 1.9 %shard_map.116 = (f32[48,1920]{1,0:T(8,128)S(1)}, f32[48,1920]{1,0:T(8,128)S(1)}) custom-call(f32[5,8,1920]{2,1,0:T(8,128)S(1)} %bitcast_dynamic-update-slice_fusion.5.own_ref, f32[48,1920]{1,0:T(8,128)S(1)} %collective-permute-done.11.core_ref, f32[5,8,1920]{2,1,0:T(8,128)S(1)} %collective-permute-done.12.side_ref, ...), custom_call_target="tpu_custom_call" | custom-call | flops 5000000000 | tf_op jit(solution)/shard_map/pallas_call | solution.py:312
  56.7 0.0 collective-permute-done.18
  56.7 0.0 collective-permute-done.17
  56.7 2.7 %collective-permute-done.16 = f32[8,128]{1,0:T(8,128)S(1)} collective-permute-done((f32[8,128]{1,0:T(8,128)S(1)}, f32[8,128]{1,0:T(8,128)S(1)}, u32[]{:S(2)}, u32[]{:S(2)}) %collective-permute-start.16) | collective-permute-done | bytes 4128 | tf_op jit(solution)/shard_map/ppermute | solution.py:322
  59.4 1.1 %shard_map.117 = (f32[48,1920]{1,0:T(8,128)}, f32[48,1920]{1,0:T(8,128)}) custom-call(f32[48,1920]{1,0:T(8,128)S(1)} %get-tuple-element.15.rhs_ref, f32[48,1920]{1,0:T(8,128)S(1)} %get-tuple-element.26.first_ref, f32[48,1920]{1,0:T(8,128)S(1)} %get-tuple-element.27.second_ref, f32[8,128]{1,0:T(8,128)S(1)} %add_add_fusion.sums_ref), custom_call_target="tpu_custom_call" | custom-call | tf_op jit(solution)/shard_map/pallas_call | solution.py:312
  (17 shorter events, 0.1 us)
Async XLA Ops:
  2.7 16.5 %collective-permute-start.3 = (f32[8,2176]{1,0:T(8,128)S(1)}, f32[8,2176]{1,0:T(8,128)S(1)}, u32[]{:S(2)}, u32[]{:S(2)}) collective-permute-start(f32[8,2176]{1,0:T(8,128)S(1)} %get-tuple-element.16), channel_id=1, source_target_pairs={{2,4},{3,5},{6,8},{7,9},{10,12},{11,13},{14,16},{15,17},{18,20},{1... | collective-permute-start | bytes 208904 | tf_op jit(solution)/shard_map/ppermute | solution.py:336
  11.1 8.0 %collective-permute-start.2 = (f32[8,2176]{1,0:T(8,128)S(1)}, f32[8,2176]{1,0:T(8,128)S(1)}, u32[]{:S(2)}, u32[]{:S(2)}) collective-permute-start(f32[8,2176]{1,0:T(8,128)S(1)} %get-tuple-element.16), channel_id=1, source_target_pairs={{0,2},{1,3},{2,0},{3,1},{4,6},{5,7},{6,4},{7,5},{8,10},{9,11},{10,... | collective-permute-start | bytes 208904 | tf_op jit(solution)/shard_map/ppermute | solution.py:322
  11.1 8.0 %collective-permute-start.1 = (f32[8,2176]{1,0:T(8,128)S(1)}, f32[8,2176]{1,0:T(8,128)S(1)}, u32[]{:S(2)}, u32[]{:S(2)}) collective-permute-start(f32[8,2176]{1,0:T(8,128)S(1)} %get-tuple-element.16), channel_id=1, source_target_pairs={{1,2},{5,6},{9,10},{13,14},{17,18},{21,22},{25,26},{29,30},{3,4},{... | collective-permute-start | bytes 208904 | tf_op jit(solution)/shard_map/ppermute | solution.py:336
  14.8 4.3 %collective-permute-start = (f32[8,2176]{1,0:T(8,128)S(1)}, f32[8,2176]{1,0:T(8,128)S(1)}, u32[]{:S(2)}, u32[]{:S(2)}) collective-permute-start(f32[8,2176]{1,0:T(8,128)S(1)} %get-tuple-element.16), channel_id=1, source_target_pairs={{0,1},{1,0},{2,3},{3,2},{4,5},{5,4},{6,7},{7,6},{8,9},{9,8},{10,11... | collective-permute-start | bytes 208904 | tf_op jit(solution)/shard_map/ppermute | solution.py:322
  19.2 6.8 %copy-start = (f32[1920]{0:T(1024)S(1)}, f32[1920]{0:T(1024)}, u32[]{:S(2)}) copy-start(f32[1920]{0:T(1024)} %param.19) | copy-start | bytes 23044
  19.2 6.8 %copy-start.1 = (s32[48]{0:T(128)S(1)}, s32[48]{0:T(128)}, u32[]{:S(2)}) copy-start(s32[48]{0:T(128)} %param.11) | copy-start | bytes 580
  19.2 6.8 %collective-permute-start.5 = (f32[5,8,2176]{2,1,0:T(8,128)S(1)}, f32[5,8,2176]{2,1,0:T(8,128)S(1)}, u32[]{:S(2)}, u32[]{:S(2)}) collective-permute-start(f32[5,8,2176]{2,1,0:T(8,128)S(1)} %bitcast_dynamic-update-slice_fusion.own_ref), channel_id=1, source_target_pairs={{32,64},{96,128},{160,192},{224,0},{64,32},{128,96},{192,160},{0,2... | collective-permute-start | bytes 1044488 | tf_op jit(solution)/shard_map/ppermute | solution.py:342
  19.3 6.7 %collective-permute-start.4 = (f32[5,8,2176]{2,1,0:T(8,128)S(1)}, f32[5,8,2176]{2,1,0:T(8,128)S(1)}, u32[]{:S(2)}, u32[]{:S(2)}) collective-permute-start(f32[5,8,2176]{2,1,0:T(8,128)S(1)} %bitcast_dynamic-update-slice_fusion.own_ref), channel_id=1, source_target_pairs={{0,32},{32,0},{1,33},{33,1},{2,34},{34,2},{3,35},{35,3},{4,36},{36... | collective-permute-start | bytes 1044488 | tf_op jit(solution)/shard_map/ppermute | solution.py:322
  27.9 3.7 %collective-permute-start.6 = (f32[8,128]{1,0:T(8,128)S(1)}, f32[8,128]{1,0:T(8,128)S(1)}, u32[]{:S(2)}, u32[]{:S(2)}) collective-permute-start(f32[8,128]{1,0:T(8,128)S(1)} %get-tuple-element.22), channel_id=1, source_target_pairs={{0,4},{4,0},{8,12},{12,8},{16,20},{20,16},{24,28},{28,24},{1,5},{5... | collective-permute-start | bytes 12296 | tf_op jit(solution)/shard_map/ppermute | solution.py:322
  29.0 11.7 %collective-permute-start.10 = (f32[8,1920]{1,0:T(8,128)S(1)}, f32[8,1920]{1,0:T(8,128)S(1)}, u32[]{:S(2)}, u32[]{:S(2)}) collective-permute-start(f32[8,1920]{1,0:T(8,128)S(1)} %get-tuple-element.21), channel_id=1, source_target_pairs={{2,4},{3,5},{6,8},{7,9},{10,12},{11,13},{14,16},{15,17},{18,20},{1... | collective-permute-start | bytes 184328 | tf_op jit(solution)/shard_map/ppermute | solution.py:397
  31.6 6.6 %collective-permute-start.9 = (f32[8,2048]{1,0:T(8,128)S(1)}, f32[8,2048]{1,0:T(8,128)S(1)}, u32[]{:S(2)}, u32[]{:S(2)}) collective-permute-start(f32[8,2048]{1,0:T(8,128)S(1)} %pad_maximum_fusion), channel_id=1, source_target_pairs={{0,2},{1,3},{2,0},{3,1},{4,6},{5,7},{6,4},{7,5},{8,10},{9,11},{10,... | collective-permute-start | bytes 196616 | tf_op jit(solution)/shard_map/ppermute | solution.py:322
  33.1 7.6 %collective-permute-start.8 = (f32[8,2048]{1,0:T(8,128)S(1)}, f32[8,2048]{1,0:T(8,128)S(1)}, u32[]{:S(2)}, u32[]{:S(2)}) collective-permute-start(f32[8,2048]{1,0:T(8,128)S(1)} %pad_maximum_fusion), channel_id=1, source_target_pairs={{1,2},{5,6},{9,10},{13,14},{17,18},{21,22},{25,26},{29,30},{3,4},{... | collective-permute-start | bytes 196616 | tf_op jit(solution)/shard_map/ppermute | solution.py:399
  36.4 4.3 %collective-permute-start.7 = (f32[8,2048]{1,0:T(8,128)S(1)}, f32[8,2048]{1,0:T(8,128)S(1)}, u32[]{:S(2)}, u32[]{:S(2)}) collective-permute-start(f32[8,2048]{1,0:T(8,128)S(1)} %pad_maximum_fusion), channel_id=1, source_target_pairs={{0,1},{1,0},{2,3},{3,2},{4,5},{5,4},{6,7},{7,6},{8,9},{9,8},{10,11... | collective-permute-start | bytes 196616 | tf_op jit(solution)/shard_map/ppermute | solution.py:322
  40.8 1.9 %collective-permute-start.11 = (f32[48,1920]{1,0:T(8,128)S(1)}, f32[48,1920]{1,0:T(8,128)S(1)}, u32[]{:S(2)}, u32[]{:S(2)}) collective-permute-start(f32[48,1920]{1,0:T(8,128)S(1)} %select_maximum_fusion), channel_id=1, source_target_pairs={{0,32},{32,0},{1,33},{33,1},{2,34},{34,2},{3,35},{35,3},{4,36},{36... | collective-permute-start | bytes 1105928 | tf_op jit(solution)/shard_map/ppermute | solution.py:322
  40.9 13.9 %collective-permute-start.12 = (f32[5,8,1920]{2,1,0:T(8,128)S(1)}, f32[5,8,1920]{2,1,0:T(8,128)S(1)}, u32[]{:S(2)}, u32[]{:S(2)}) collective-permute-start(f32[5,8,1920]{2,1,0:T(8,128)S(1)} %bitcast_dynamic-update-slice_fusion.5.own_ref), channel_id=1, source_target_pairs={{32,64},{96,128},{160,192},{224,0},{64,32},{128,96},{192,160},{0,2... | collective-permute-start | bytes 921608 | tf_op jit(solution)/shard_map/ppermute | solution.py:342
  42.7 7.5 %collective-permute-start.15 = (f32[8,128]{1,0:T(8,128)S(1)}, f32[8,128]{1,0:T(8,128)S(1)}, u32[]{:S(2)}, u32[]{:S(2)}) collective-permute-start(f32[8,128]{1,0:T(8,128)S(1)} %slice_add_fusion), channel_id=1, source_target_pairs={{0,16},{4,20},{8,24},{12,28},{16,0},{20,4},{24,8},{28,12},{1,17},{... | collective-permute-start | bytes 12296 | tf_op jit(solution)/shard_map/ppermute | solution.py:322
  45.1 5.7 %collective-permute-start.14 = (f32[8,128]{1,0:T(8,128)S(1)}, f32[8,128]{1,0:T(8,128)S(1)}, u32[]{:S(2)}, u32[]{:S(2)}) collective-permute-start(f32[8,128]{1,0:T(8,128)S(1)} %slice_add_fusion), channel_id=1, source_target_pairs={{0,24},{4,28},{8,16},{12,20},{16,8},{20,12},{24,0},{28,4},{1,25},{... | collective-permute-start | bytes 12296 | tf_op jit(solution)/shard_map/ppermute | solution.py:322
  46.1 4.7 %collective-permute-start.13 = (f32[8,128]{1,0:T(8,128)S(1)}, f32[8,128]{1,0:T(8,128)S(1)}, u32[]{:S(2)}, u32[]{:S(2)}) collective-permute-start(f32[8,128]{1,0:T(8,128)S(1)} %slice_add_fusion), channel_id=1, source_target_pairs={{0,8},{4,12},{8,0},{12,4},{16,24},{20,28},{24,16},{28,20},{1,9},{5... | collective-permute-start | bytes 12296 | tf_op jit(solution)/shard_map/ppermute | solution.py:322
  50.8 5.8 %collective-permute-start.18 = (f32[8,128]{1,0:T(8,128)S(1)}, f32[8,128]{1,0:T(8,128)S(1)}, u32[]{:S(2)}, u32[]{:S(2)}) collective-permute-start(f32[8,128]{1,0:T(8,128)S(1)} %add_add_fusion.1), channel_id=1, source_target_pairs={{0,192},{64,128},{128,64},{192,0},{1,193},{65,129},{129,65},{193,1... | collective-permute-start | bytes 12296 | tf_op jit(solution)/shard_map/ppermute | solution.py:322
  52.4 4.3 %collective-permute-start.17 = (f32[8,128]{1,0:T(8,128)S(1)}, f32[8,128]{1,0:T(8,128)S(1)}, u32[]{:S(2)}, u32[]{:S(2)}) collective-permute-start(f32[8,128]{1,0:T(8,128)S(1)} %add_add_fusion.1), channel_id=1, source_target_pairs={{0,64},{64,0},{128,192},{192,128},{1,65},{65,1},{129,193},{193,129... | collective-permute-start | bytes 12296 | tf_op jit(solution)/shard_map/ppermute | solution.py:322
  54.3 5.1 %collective-permute-start.16 = (f32[8,128]{1,0:T(8,128)S(1)}, f32[8,128]{1,0:T(8,128)S(1)}, u32[]{:S(2)}, u32[]{:S(2)}) collective-permute-start(f32[8,128]{1,0:T(8,128)S(1)} %add_add_fusion.1), channel_id=1, source_target_pairs={{0,128},{64,192},{128,0},{192,64},{1,129},{65,193},{129,1},{193,65... | collective-permute-start | bytes 12296 | tf_op jit(solution)/shard_map/ppermute | solution.py:322

commit v6 on v3

--- a/solution.py
+++ b/solution.py
@@ -406,7 +406,7 @@
         line, core, side, matrix, *weights, mie, member, first
     )
     sums = plus(sums, "z", (2, 6, 4))
-    sums = plus(sums, "y", (2, 1, 3))
+    sums = plus(sums, "y", (1, 3, 2))
     entries = float(lax.axis_size(ALL) * spheres * C)
     return tuple(
         call(functools.partial(last_kernel, entries), (like(spheres, C), like(spheres, C)), 4)(

time: 60.6 us -> 59.5 us (0.982)
  waiting for transfers between devices: 16.5 us -> 14.1 us
  starting transfers between devices: 33.1 us -> 33.9 us
    ppermute x13, waiting for transfers between devices: 12.1 us -> 9.68 us  [swap(): lax.ppermute(v, axis, [(i, i ^ mask) for i in range(lax.axis_size(axis))])]
    ppermute x13, starting transfers between devices: 14.8 us -> 15.6 us  [swap(): lax.ppermute(v, axis, [(i, i ^ mask) for i in range(lax.axis_size(axis))])]
where the time goes in v6:
time: 59.5 us; the launch traced here: 58.9 us
  starting transfers between devices  33.9 us (57%)
  waiting for transfers between devices  14.1 us (24%)
  Pallas kernels  9.26 us (16%)
  between operations  1.47 us (2%)
    ppermute x13, starting transfers between devices, swap(): lax.ppermute(v, axis, [(i, i ^ mask) for i in range(lax.axis_size(axis))])  15.6 us
    ppermute x13, waiting for transfers between devices, swap(): lax.ppermute(v, axis, [(i, i ^ mask) for i in range(lax.axis_size(axis))])  9.68 us
    pallas_call x5, Pallas kernels, placed(): return run(*operands[:smem + vmem], *held)  9.26 us
    ppermute x1, starting transfers between devices, beside(): lax.ppermute(v, ROW, wide)  8.4 us
    ppermute x1, starting transfers between devices, beside(): lax.ppermute(v, ROW, odd)  3.71 us
    ppermute x1, starting transfers between devices, body(): lax.ppermute(following, ROW, odd)  3.29 us
    ppermute x1, waiting for transfers between devices, body(): lax.ppermute(following, ROW, odd)  2.43 us
    ppermute x2, waiting for transfers between devices, over_side(): return lax.ppermute(line, COL, steps + [(b, a) for a, b in steps])  1.98 us
  transfers between devices with their start and end apart: 19, of which 8 were waited for; matrix products, arithmetic and copies ran while one was open for 0% of the time, Pallas kernels for 8%

profile of v6, /device:TPU:8, one launch (start us, length us, event | category | flops | bytes accessed | tf_op | source)
XLA Modules:
  0.0 58.9 jit_solution(2094796190493355121)
XLA Ops:
  1.3 1.4 %shard_map.113 = (f32[8,2176]{1,0:T(8,128)S(1)}, f32[1,128]{1,0:T(1,128)S(1)}, f32[48,1920]{1,0:T(8,128)S(1)}) custom-call(s32[1]{0:T(128)S(6)} %copy.20.count_ref, f32[48,1920]{1,0:T(8,128)} %refs_0_.1, s32[1,48]{1,0:T(1,128)} %bitcast.38, s32[2,512]{1,0:T(2,128)} %bitcast.41, s32[1,512]{1,0:T(1,128)} %bitcast.42, f32[1,512]{1,0:T(1,128)} %bitcast.43, ...), custom_call_target="tpu_custom_call" | custom-call | tf_op jit(solution)/shard_map/pallas_call | solution.py:311
  2.7 8.4 %collective-permute-start.3 = (f32[8,2176]{1,0:T(8,128)S(1)}, f32[8,2176]{1,0:T(8,128)S(1)}, u32[]{:S(2)}, u32[]{:S(2)}) collective-permute-start(f32[8,2176]{1,0:T(8,128)S(1)} %get-tuple-element.16), channel_id=1, source_target_pairs={{2,4},{3,5},{6,8},{7,9},{10,12},{11,13},{14,16},{15,17},{18,20},{1... | collective-permute-start | bytes 208904 | tf_op jit(solution)/shard_map/ppermute | solution.py:335
  11.1 0.0 collective-permute-start.2
  11.1 3.7 %collective-permute-start.1 = (f32[8,2176]{1,0:T(8,128)S(1)}, f32[8,2176]{1,0:T(8,128)S(1)}, u32[]{:S(2)}, u32[]{:S(2)}) collective-permute-start(f32[8,2176]{1,0:T(8,128)S(1)} %get-tuple-element.16), channel_id=1, source_target_pairs={{1,2},{5,6},{9,10},{13,14},{17,18},{21,22},{25,26},{29,30},{3,4},{... | collective-permute-start | bytes 208904 | tf_op jit(solution)/shard_map/ppermute | solution.py:335
  14.8 0.0 collective-permute-start
  14.8 4.3 %collective-permute-done = f32[8,2176]{1,0:T(8,128)S(1)} collective-permute-done((f32[8,2176]{1,0:T(8,128)S(1)}, f32[8,2176]{1,0:T(8,128)S(1)}, u32[]{:S(2)}, u32[]{:S(2)}) %collective-permute-start) | collective-permute-done | bytes 69664 | tf_op jit(solution)/shard_map/ppermute | solution.py:321
  19.1 0.0 collective-permute-done.1
  19.1 0.0 collective-permute-done.2
  19.1 0.0 collective-permute-done.3
  19.2 0.0 copy-start
  19.2 0.0 copy-start.1
  19.2 0.1 collective-permute-start.5
  19.3 1.7 %collective-permute-start.4 = (f32[5,8,2176]{2,1,0:T(8,128)S(1)}, f32[5,8,2176]{2,1,0:T(8,128)S(1)}, u32[]{:S(2)}, u32[]{:S(2)}) collective-permute-start(f32[5,8,2176]{2,1,0:T(8,128)S(1)} %bitcast_dynamic-update-slice_fusion.own_ref), channel_id=1, source_target_pairs={{0,32},{32,0},{1,33},{33,1},{2,34},{34,2},{3,35},{35,3},{4,36},{36... | collective-permute-start | bytes 1044488 | tf_op jit(solution)/shard_map/ppermute | solution.py:321
  21.0 3.0 %shard_map.114 = (bf16[15,384,256]{2,1,0:T(8,128)(2,1)S(1)}, bf16[15,256,256]{2,1,0:T(8,128)(2,1)S(1)}, bf16[15,384,256]{2,1,0:T(8,128)(2,1)S(1)}) custom-call(f32[3,15,128,128]{3,2,1,0:T(8,128)} %rotation_any.1, f32[15,128,128]{2,1,0:T(8,128)} %translation_any.1), custom_call_target="tpu_custom_call" | custom-call | flops 3000000000 | tf_op jit(solution)/shard_map/pallas_call | solution.py:311
  24.0 2.0 %collective-permute-done.5.side_ref = f32[5,8,2176]{2,1,0:T(8,128)S(1)} collective-permute-done((f32[5,8,2176]{2,1,0:T(8,128)S(1)}, f32[5,8,2176]{2,1,0:T(8,128)S(1)}, u32[]{:S(2)}, u32[]{:S(2)}) %collective-permute-start.5) | collective-permute-done | bytes 348192 | tf_op jit(solution)/shard_map/ppermute | solution.py:341
  26.0 0.0 collective-permute-done.4.core_ref
  26.0 0.0 copy-done
  26.0 0.0 copy-done.1
  26.0 1.9 %shard_map.115 = (f32[48,120]{1,0:T(8,128)S(1)}, f32[8,1920]{1,0:T(8,128)S(1)}, f32[8,1920]{1,0:T(8,128)S(1)}, f32[8,128]{1,0:T(8,128)S(1)}) custom-call(f32[5,8,2176]{2,1,0:T(8,128)S(1)} %bitcast_dynamic-update-slice_fusion.own_ref, f32[5,8,2176]{2,1,0:T(8,128)S(1)} %collective-permute-done.4.core_ref, f32[5,8,2176]{2,1,0:T(8,128)S(1)} %collective-permute-done.5.side_ref, ...), custom_call_target="tpu_custom_call" | custom-call | tf_op jit(solution)/shard_map/pallas_call | solution.py:311
  27.9 1.1 %collective-permute-start.6 = (f32[8,128]{1,0:T(8,128)S(1)}, f32[8,128]{1,0:T(8,128)S(1)}, u32[]{:S(2)}, u32[]{:S(2)}) collective-permute-start(f32[8,128]{1,0:T(8,128)S(1)} %get-tuple-element.22), channel_id=1, source_target_pairs={{0,4},{4,0},{8,12},{12,8},{16,20},{20,16},{24,28},{28,24},{1,5},{5... | collective-permute-start | bytes 12296 | tf_op jit(solution)/shard_map/ppermute | solution.py:321
  29.0 1.0 %collective-permute-start.10 = (f32[8,1920]{1,0:T(8,128)S(1)}, f32[8,1920]{1,0:T(8,128)S(1)}, u32[]{:S(2)}, u32[]{:S(2)}) collective-permute-start(f32[8,1920]{1,0:T(8,128)S(1)} %get-tuple-element.21), channel_id=1, source_target_pairs={{2,4},{3,5},{6,8},{7,9},{10,12},{11,13},{14,16},{15,17},{18,20},{1... | collective-permute-start | bytes 184328 | tf_op jit(solution)/shard_map/ppermute | solution.py:396
  30.1 1.6 %collective-permute-done.6 = f32[8,128]{1,0:T(8,128)S(1)} collective-permute-done((f32[8,128]{1,0:T(8,128)S(1)}, f32[8,128]{1,0:T(8,128)S(1)}, u32[]{:S(2)}, u32[]{:S(2)}) %collective-permute-start.6) | collective-permute-done | bytes 4128 | tf_op jit(solution)/shard_map/ppermute | solution.py:321
  31.6 1.5 %collective-permute-start.9 = (f32[8,2048]{1,0:T(8,128)S(1)}, f32[8,2048]{1,0:T(8,128)S(1)}, u32[]{:S(2)}, u32[]{:S(2)}) collective-permute-start(f32[8,2048]{1,0:T(8,128)S(1)} %pad_maximum_fusion), channel_id=1, source_target_pairs={{0,2},{1,3},{2,0},{3,1},{4,6},{5,7},{6,4},{7,5},{8,10},{9,11},{10,... | collective-permute-start | bytes 196616 | tf_op jit(solution)/shard_map/ppermute | solution.py:321
  33.1 3.3 %collective-permute-start.8 = (f32[8,2048]{1,0:T(8,128)S(1)}, f32[8,2048]{1,0:T(8,128)S(1)}, u32[]{:S(2)}, u32[]{:S(2)}) collective-permute-start(f32[8,2048]{1,0:T(8,128)S(1)} %pad_maximum_fusion), channel_id=1, source_target_pairs={{1,2},{5,6},{9,10},{13,14},{17,18},{21,22},{25,26},{29,30},{3,4},{... | collective-permute-start | bytes 196616 | tf_op jit(solution)/shard_map/ppermute | solution.py:398
  36.4 0.0 collective-permute-start.7
  36.4 1.9 %collective-permute-done.9 = f32[8,2048]{1,0:T(8,128)S(1)} collective-permute-done((f32[8,2048]{1,0:T(8,128)S(1)}, f32[8,2048]{1,0:T(8,128)S(1)}, u32[]{:S(2)}, u32[]{:S(2)}) %collective-permute-start.9) | collective-permute-done | bytes 65568 | tf_op jit(solution)/shard_map/ppermute | solution.py:321
  38.3 2.4 %collective-permute-done.8 = f32[8,2048]{1,0:T(8,128)S(1)} collective-permute-done((f32[8,2048]{1,0:T(8,128)S(1)}, f32[8,2048]{1,0:T(8,128)S(1)}, u32[]{:S(2)}, u32[]{:S(2)}) %collective-permute-start.8) | collective-permute-done | bytes 65568 | tf_op jit(solution)/shard_map/ppermute | solution.py:398
  40.7 0.0 collective-permute-done.7
  40.7 0.0 collective-permute-done.10
  40.8 0.1 collective-permute-start.11
  40.9 1.8 %collective-permute-start.12 = (f32[5,8,1920]{2,1,0:T(8,128)S(1)}, f32[5,8,1920]{2,1,0:T(8,128)S(1)}, u32[]{:S(2)}, u32[]{:S(2)}) collective-permute-start(f32[5,8,1920]{2,1,0:T(8,128)S(1)} %bitcast_dynamic-update-slice_fusion.5.own_ref), channel_id=1, source_target_pairs={{32,64},{96,128},{160,192},{224,0},{64,32},{128,96},{192,160},{0,2... | collective-permute-start | bytes 921608 | tf_op jit(solution)/shard_map/ppermute | solution.py:341
  42.7 0.0 collective-permute-done.11.core_ref
  42.7 2.4 %collective-permute-start.15 = (f32[8,128]{1,0:T(8,128)S(1)}, f32[8,128]{1,0:T(8,128)S(1)}, u32[]{:S(2)}, u32[]{:S(2)}) collective-permute-start(f32[8,128]{1,0:T(8,128)S(1)} %slice_add_fusion), channel_id=1, source_target_pairs={{0,16},{4,20},{8,24},{12,28},{16,0},{20,4},{24,8},{28,12},{1,17},{... | collective-permute-start | bytes 12296 | tf_op jit(solution)/shard_map/ppermute | solution.py:321
  45.1 1.0 %collective-permute-start.14 = (f32[8,128]{1,0:T(8,128)S(1)}, f32[8,128]{1,0:T(8,128)S(1)}, u32[]{:S(2)}, u32[]{:S(2)}) collective-permute-start(f32[8,128]{1,0:T(8,128)S(1)} %slice_add_fusion), channel_id=1, source_target_pairs={{0,24},{4,28},{8,16},{12,20},{16,8},{20,12},{24,0},{28,4},{1,25},{... | collective-permute-start | bytes 12296 | tf_op jit(solution)/shard_map/ppermute | solution.py:321
  46.1 3.1 %collective-permute-start.13 = (f32[8,128]{1,0:T(8,128)S(1)}, f32[8,128]{1,0:T(8,128)S(1)}, u32[]{:S(2)}, u32[]{:S(2)}) collective-permute-start(f32[8,128]{1,0:T(8,128)S(1)} %slice_add_fusion), channel_id=1, source_target_pairs={{0,8},{4,12},{8,0},{12,4},{16,24},{20,28},{24,16},{28,20},{1,9},{5... | collective-permute-start | bytes 12296 | tf_op jit(solution)/shard_map/ppermute | solution.py:321
  49.2 1.0 %collective-permute-done.15 = f32[8,128]{1,0:T(8,128)S(1)} collective-permute-done((f32[8,128]{1,0:T(8,128)S(1)}, f32[8,128]{1,0:T(8,128)S(1)}, u32[]{:S(2)}, u32[]{:S(2)}) %collective-permute-start.15) | collective-permute-done | bytes 4128 | tf_op jit(solution)/shard_map/ppermute | solution.py:321
  50.2 0.6 %collective-permute-done.14 = f32[8,128]{1,0:T(8,128)S(1)} collective-permute-done((f32[8,128]{1,0:T(8,128)S(1)}, f32[8,128]{1,0:T(8,128)S(1)}, u32[]{:S(2)}, u32[]{:S(2)}) %collective-permute-start.14) | collective-permute-done | bytes 4128 | tf_op jit(solution)/shard_map/ppermute | solution.py:321
  50.8 0.0 collective-permute-done.13
  50.8 2.3 %collective-permute-start.18 = (f32[8,128]{1,0:T(8,128)S(1)}, f32[8,128]{1,0:T(8,128)S(1)}, u32[]{:S(2)}, u32[]{:S(2)}) collective-permute-start(f32[8,128]{1,0:T(8,128)S(1)} %add_add_fusion.1), channel_id=1, source_target_pairs={{0,128},{64,192},{128,0},{192,64},{1,129},{65,193},{129,1},{193,65... | collective-permute-start | bytes 12296 | tf_op jit(solution)/shard_map/ppermute | solution.py:321
  53.1 1.1 %collective-permute-start.17 = (f32[8,128]{1,0:T(8,128)S(1)}, f32[8,128]{1,0:T(8,128)S(1)}, u32[]{:S(2)}, u32[]{:S(2)}) collective-permute-start(f32[8,128]{1,0:T(8,128)S(1)} %add_add_fusion.1), channel_id=1, source_target_pairs={{0,192},{64,128},{128,64},{192,0},{1,193},{65,129},{129,65},{193,1... | collective-permute-start | bytes 12296 | tf_op jit(solution)/shard_map/ppermute | solution.py:321
  54.2 1.4 %collective-permute-start.16 = (f32[8,128]{1,0:T(8,128)S(1)}, f32[8,128]{1,0:T(8,128)S(1)}, u32[]{:S(2)}, u32[]{:S(2)}) collective-permute-start(f32[8,128]{1,0:T(8,128)S(1)} %add_add_fusion.1), channel_id=1, source_target_pairs={{0,64},{64,0},{128,192},{192,128},{1,65},{65,1},{129,193},{193,129... | collective-permute-start | bytes 12296 | tf_op jit(solution)/shard_map/ppermute | solution.py:321
  55.6 0.0 collective-permute-done.12.side_ref
  55.6 1.9 %shard_map.116 = (f32[48,1920]{1,0:T(8,128)S(1)}, f32[48,1920]{1,0:T(8,128)S(1)}) custom-call(f32[5,8,1920]{2,1,0:T(8,128)S(1)} %bitcast_dynamic-update-slice_fusion.5.own_ref, f32[48,1920]{1,0:T(8,128)S(1)} %collective-permute-done.11.core_ref, f32[5,8,1920]{2,1,0:T(8,128)S(1)} %collective-permute-done.12.side_ref, ...), custom_call_target="tpu_custom_call" | custom-call | flops 5000000000 | tf_op jit(solution)/shard_map/pallas_call | solution.py:311
  57.5 0.0 collective-permute-done.18
  57.5 0.0 collective-permute-done.17
  57.5 0.3 collective-permute-done.16
  57.8 1.1 %shard_map.117 = (f32[48,1920]{1,0:T(8,128)}, f32[48,1920]{1,0:T(8,128)}) custom-call(f32[48,1920]{1,0:T(8,128)S(1)} %get-tuple-element.15.rhs_ref, f32[48,1920]{1,0:T(8,128)S(1)} %get-tuple-element.26.first_ref, f32[48,1920]{1,0:T(8,128)S(1)} %get-tuple-element.27.second_ref, f32[8,128]{1,0:T(8,128)S(1)} %add_add_fusion.sums_ref), custom_call_target="tpu_custom_call" | custom-call | tf_op jit(solution)/shard_map/pallas_call | solution.py:311
  (17 shorter events, 0.1 us)
Async XLA Ops:
  2.7 16.5 %collective-permute-start.3 = (f32[8,2176]{1,0:T(8,128)S(1)}, f32[8,2176]{1,0:T(8,128)S(1)}, u32[]{:S(2)}, u32[]{:S(2)}) collective-permute-start(f32[8,2176]{1,0:T(8,128)S(1)} %get-tuple-element.16), channel_id=1, source_target_pairs={{2,4},{3,5},{6,8},{7,9},{10,12},{11,13},{14,16},{15,17},{18,20},{1... | collective-permute-start | bytes 208904 | tf_op jit(solution)/shard_map/ppermute | solution.py:335
  11.1 8.1 %collective-permute-start.2 = (f32[8,2176]{1,0:T(8,128)S(1)}, f32[8,2176]{1,0:T(8,128)S(1)}, u32[]{:S(2)}, u32[]{:S(2)}) collective-permute-start(f32[8,2176]{1,0:T(8,128)S(1)} %get-tuple-element.16), channel_id=1, source_target_pairs={{0,2},{1,3},{2,0},{3,1},{4,6},{5,7},{6,4},{7,5},{8,10},{9,11},{10,... | collective-permute-start | bytes 208904 | tf_op jit(solution)/shard_map/ppermute | solution.py:321
  11.1 8.0 %collective-permute-start.1 = (f32[8,2176]{1,0:T(8,128)S(1)}, f32[8,2176]{1,0:T(8,128)S(1)}, u32[]{:S(2)}, u32[]{:S(2)}) collective-permute-start(f32[8,2176]{1,0:T(8,128)S(1)} %get-tuple-element.16), channel_id=1, source_target_pairs={{1,2},{5,6},{9,10},{13,14},{17,18},{21,22},{25,26},{29,30},{3,4},{... | collective-permute-start | bytes 208904 | tf_op jit(solution)/shard_map/ppermute | solution.py:335
  14.8 4.3 %collective-permute-start = (f32[8,2176]{1,0:T(8,128)S(1)}, f32[8,2176]{1,0:T(8,128)S(1)}, u32[]{:S(2)}, u32[]{:S(2)}) collective-permute-start(f32[8,2176]{1,0:T(8,128)S(1)} %get-tuple-element.16), channel_id=1, source_target_pairs={{0,1},{1,0},{2,3},{3,2},{4,5},{5,4},{6,7},{7,6},{8,9},{9,8},{10,11... | collective-permute-start | bytes 208904 | tf_op jit(solution)/shard_map/ppermute | solution.py:321
  19.2 6.8 %copy-start = (f32[1920]{0:T(1024)S(1)}, f32[1920]{0:T(1024)}, u32[]{:S(2)}) copy-start(f32[1920]{0:T(1024)} %param.19) | copy-start | bytes 23044
  19.2 6.8 %copy-start.1 = (s32[48]{0:T(128)S(1)}, s32[48]{0:T(128)}, u32[]{:S(2)}) copy-start(s32[48]{0:T(128)} %param.11) | copy-start | bytes 580
  19.2 6.8 %collective-permute-start.5 = (f32[5,8,2176]{2,1,0:T(8,128)S(1)}, f32[5,8,2176]{2,1,0:T(8,128)S(1)}, u32[]{:S(2)}, u32[]{:S(2)}) collective-permute-start(f32[5,8,2176]{2,1,0:T(8,128)S(1)} %bitcast_dynamic-update-slice_fusion.own_ref), channel_id=1, source_target_pairs={{32,64},{96,128},{160,192},{224,0},{64,32},{128,96},{192,160},{0,2... | collective-permute-start | bytes 1044488 | tf_op jit(solution)/shard_map/ppermute | solution.py:341
  19.3 6.7 %collective-permute-start.4 = (f32[5,8,2176]{2,1,0:T(8,128)S(1)}, f32[5,8,2176]{2,1,0:T(8,128)S(1)}, u32[]{:S(2)}, u32[]{:S(2)}) collective-permute-start(f32[5,8,2176]{2,1,0:T(8,128)S(1)} %bitcast_dynamic-update-slice_fusion.own_ref), channel_id=1, source_target_pairs={{0,32},{32,0},{1,33},{33,1},{2,34},{34,2},{3,35},{35,3},{4,36},{36... | collective-permute-start | bytes 1044488 | tf_op jit(solution)/shard_map/ppermute | solution.py:321
  27.9 3.7 %collective-permute-start.6 = (f32[8,128]{1,0:T(8,128)S(1)}, f32[8,128]{1,0:T(8,128)S(1)}, u32[]{:S(2)}, u32[]{:S(2)}) collective-permute-start(f32[8,128]{1,0:T(8,128)S(1)} %get-tuple-element.22), channel_id=1, source_target_pairs={{0,4},{4,0},{8,12},{12,8},{16,20},{20,16},{24,28},{28,24},{1,5},{5... | collective-permute-start | bytes 12296 | tf_op jit(solution)/shard_map/ppermute | solution.py:321
  29.0 11.7 %collective-permute-start.10 = (f32[8,1920]{1,0:T(8,128)S(1)}, f32[8,1920]{1,0:T(8,128)S(1)}, u32[]{:S(2)}, u32[]{:S(2)}) collective-permute-start(f32[8,1920]{1,0:T(8,128)S(1)} %get-tuple-element.21), channel_id=1, source_target_pairs={{2,4},{3,5},{6,8},{7,9},{10,12},{11,13},{14,16},{15,17},{18,20},{1... | collective-permute-start | bytes 184328 | tf_op jit(solution)/shard_map/ppermute | solution.py:396
  31.6 6.6 %collective-permute-start.9 = (f32[8,2048]{1,0:T(8,128)S(1)}, f32[8,2048]{1,0:T(8,128)S(1)}, u32[]{:S(2)}, u32[]{:S(2)}) collective-permute-start(f32[8,2048]{1,0:T(8,128)S(1)} %pad_maximum_fusion), channel_id=1, source_target_pairs={{0,2},{1,3},{2,0},{3,1},{4,6},{5,7},{6,4},{7,5},{8,10},{9,11},{10,... | collective-permute-start | bytes 196616 | tf_op jit(solution)/shard_map/ppermute | solution.py:321
  33.1 7.6 %collective-permute-start.8 = (f32[8,2048]{1,0:T(8,128)S(1)}, f32[8,2048]{1,0:T(8,128)S(1)}, u32[]{:S(2)}, u32[]{:S(2)}) collective-permute-start(f32[8,2048]{1,0:T(8,128)S(1)} %pad_maximum_fusion), channel_id=1, source_target_pairs={{1,2},{5,6},{9,10},{13,14},{17,18},{21,22},{25,26},{29,30},{3,4},{... | collective-permute-start | bytes 196616 | tf_op jit(solution)/shard_map/ppermute | solution.py:398
  36.4 4.3 %collective-permute-start.7 = (f32[8,2048]{1,0:T(8,128)S(1)}, f32[8,2048]{1,0:T(8,128)S(1)}, u32[]{:S(2)}, u32[]{:S(2)}) collective-permute-start(f32[8,2048]{1,0:T(8,128)S(1)} %pad_maximum_fusion), channel_id=1, source_target_pairs={{0,1},{1,0},{2,3},{3,2},{4,5},{5,4},{6,7},{7,6},{8,9},{9,8},{10,11... | collective-permute-start | bytes 196616 | tf_op jit(solution)/shard_map/ppermute | solution.py:321
  40.8 1.9 %collective-permute-start.11 = (f32[48,1920]{1,0:T(8,128)S(1)}, f32[48,1920]{1,0:T(8,128)S(1)}, u32[]{:S(2)}, u32[]{:S(2)}) collective-permute-start(f32[48,1920]{1,0:T(8,128)S(1)} %select_maximum_fusion), channel_id=1, source_target_pairs={{0,32},{32,0},{1,33},{33,1},{2,34},{34,2},{3,35},{35,3},{4,36},{36... | collective-permute-start | bytes 1105928 | tf_op jit(solution)/shard_map/ppermute | solution.py:321
  40.9 14.7 %collective-permute-start.12 = (f32[5,8,1920]{2,1,0:T(8,128)S(1)}, f32[5,8,1920]{2,1,0:T(8,128)S(1)}, u32[]{:S(2)}, u32[]{:S(2)}) collective-permute-start(f32[5,8,1920]{2,1,0:T(8,128)S(1)} %bitcast_dynamic-update-slice_fusion.5.own_ref), channel_id=1, source_target_pairs={{32,64},{96,128},{160,192},{224,0},{64,32},{128,96},{192,160},{0,2... | collective-permute-start | bytes 921608 | tf_op jit(solution)/shard_map/ppermute | solution.py:341
  42.7 7.5 %collective-permute-start.15 = (f32[8,128]{1,0:T(8,128)S(1)}, f32[8,128]{1,0:T(8,128)S(1)}, u32[]{:S(2)}, u32[]{:S(2)}) collective-permute-start(f32[8,128]{1,0:T(8,128)S(1)} %slice_add_fusion), channel_id=1, source_target_pairs={{0,16},{4,20},{8,24},{12,28},{16,0},{20,4},{24,8},{28,12},{1,17},{... | collective-permute-start | bytes 12296 | tf_op jit(solution)/shard_map/ppermute | solution.py:321
  45.1 5.7 %collective-permute-start.14 = (f32[8,128]{1,0:T(8,128)S(1)}, f32[8,128]{1,0:T(8,128)S(1)}, u32[]{:S(2)}, u32[]{:S(2)}) collective-permute-start(f32[8,128]{1,0:T(8,128)S(1)} %slice_add_fusion), channel_id=1, source_target_pairs={{0,24},{4,28},{8,16},{12,20},{16,8},{20,12},{24,0},{28,4},{1,25},{... | collective-permute-start | bytes 12296 | tf_op jit(solution)/shard_map/ppermute | solution.py:321
  46.1 4.7 %collective-permute-start.13 = (f32[8,128]{1,0:T(8,128)S(1)}, f32[8,128]{1,0:T(8,128)S(1)}, u32[]{:S(2)}, u32[]{:S(2)}) collective-permute-start(f32[8,128]{1,0:T(8,128)S(1)} %slice_add_fusion), channel_id=1, source_target_pairs={{0,8},{4,12},{8,0},{12,4},{16,24},{20,28},{24,16},{28,20},{1,9},{5... | collective-permute-start | bytes 12296 | tf_op jit(solution)/shard_map/ppermute | solution.py:321
  50.8 6.7 %collective-permute-start.18 = (f32[8,128]{1,0:T(8,128)S(1)}, f32[8,128]{1,0:T(8,128)S(1)}, u32[]{:S(2)}, u32[]{:S(2)}) collective-permute-start(f32[8,128]{1,0:T(8,128)S(1)} %add_add_fusion.1), channel_id=1, source_target_pairs={{0,128},{64,192},{128,0},{192,64},{1,129},{65,193},{129,1},{193,65... | collective-permute-start | bytes 12296 | tf_op jit(solution)/shard_map/ppermute | solution.py:321
  53.1 4.4 %collective-permute-start.17 = (f32[8,128]{1,0:T(8,128)S(1)}, f32[8,128]{1,0:T(8,128)S(1)}, u32[]{:S(2)}, u32[]{:S(2)}) collective-permute-start(f32[8,128]{1,0:T(8,128)S(1)} %add_add_fusion.1), channel_id=1, source_target_pairs={{0,192},{64,128},{128,64},{192,0},{1,193},{65,129},{129,65},{193,1... | collective-permute-start | bytes 12296 | tf_op jit(solution)/shard_map/ppermute | solution.py:321
  54.2 3.6 %collective-permute-start.16 = (f32[8,128]{1,0:T(8,128)S(1)}, f32[8,128]{1,0:T(8,128)S(1)}, u32[]{:S(2)}, u32[]{:S(2)}) collective-permute-start(f32[8,128]{1,0:T(8,128)S(1)} %add_add_fusion.1), channel_id=1, source_target_pairs={{0,64},{64,0},{128,192},{192,128},{1,65},{65,1},{129,193},{193,129... | collective-permute-start | bytes 12296 | tf_op jit(solution)/shard_map/ppermute | solution.py:321
